TPU v7x, 32 devices: a whole 2x2x4 slice. The times are simulated.
32 devices in a mesh: band: 8 (over y, x, core), row: 4 (over z).
Axes of the slice: x: 2, y: 2, z: 4, core: 2. Of those that a mesh axis runs over, the one named last changes fastest.
Arguments:
- grid_input: float32 [7680, 227], P('band'), may hold values from -6 to 6
- grid_target: float32 [7680, 227], P('band'), may hold values from -6 to 6
- edge_input: float32 [10240, 4], P('band'), may hold values from -6 to 6
- senders: int32 [10240], P('band'), may hold values from 0 to 831
- receivers: int32 [10240], P('band'), may hold values from 0 to 319
- border_nodes: int32 [512], P('band'), may hold values from 0 to 319
- grid_to_mesh: int32 [7680], P('band'), may hold values from 0 to 319, as said below
- mesh_to_grid: int32 [23040], P('band'), may hold values from 0 to 831
- loss_mask: int32 [7680], P('band'), may hold values from 0 to 1
- encoder_weights: float32 [231, 512], replicated, may hold values from -0.375 to 0.375
- encoder_first: float32 [231, 512], replicated, may hold values from -0.0546875 to 0.0546875
- encoder_second: float32 [231, 512], replicated, may hold values from 5.859375e-05 to 0.000234375
- processor_weights: float32 [3, 7, 512, 512], P(None, None, 'row'), may hold values from -0.25 to 0.25
- processor_momentum: float32 [3, 7, 512, 512], P(None, None, 'row'), may hold values from -0.4107919 to 0.4107919
- processor_average: float32 [3, 7, 512, 512], P(None, None, 'row'), may hold values from -0.25 to 0.25
- norm_params: float32 [3, 8, 512], replicated, may hold values from -4 to 4
- norm_first: float32 [3, 8, 512], replicated, may hold values from -0.0546875 to 0.0546875
- norm_second: float32 [3, 8, 512], replicated, may hold values from 5.859375e-05 to 0.000234375
- decoder_weights: float32 [512, 227], replicated, may hold values from -0.25 to 0.25
- decoder_first: float32 [512, 227], replicated, may hold values from -0.0546875 to 0.0546875
- decoder_second: float32 [512, 227], replicated, may hold values from 5.859375e-05 to 0.000234375
Outputs:
- loss_total: float32 [], replicated
- mask_count: float32 [], replicated
- next_weights: float32 [3, 7, 512, 512], P(None, None, 'row')
- next_momentum: float32 [3, 7, 512, 512], P(None, None, 'row')
- next_average: float32 [3, 7, 512, 512], P(None, None, 'row')
- param_moment: float32 [3, 8, 512], replicated
- param_square: float32 [3, 8, 512], replicated
- param_values: float32 [3, 8, 512], replicated
- encoder_moment: float32 [231, 512], replicated
- encoder_square: float32 [231, 512], replicated
- encoder_values: float32 [231, 512], replicated
- decoder_moment: float32 [512, 227], replicated
- decoder_square: float32 [512, 227], replicated
- decoder_values: float32 [512, 227], replicated
Inputs may be any that keep to these rules, and one draw needn't show every extreme that they name: `grid_to_mesh`: every mesh node of a band is named by some grid point of that band.
All inputs are finite; a program needn't handle non-finite values.
Results may differ from a plain program's by a relative error of at most 0.0003.
Values sent between devices are 32-bit elements; how exact they have to be, the bound alone decides.
A program may use at most 256 MiB of HBM per device.

v0:
```python
import jax
import jax.numpy as jnp
from jax import lax
from jax.sharding import PartitionSpec as P

LAYERS = 3
NS_ITERS = 2
STEP = 10
NODE_DEV = 320


highest = lax.Precision.HIGHEST
coef_a = 3.4445
coef_b = -4.775
coef_c = 2.0315
momentum_decay = 0.95
muon_rate = 0.3
adam_rate = 0.02
param_rate = 0.1
beta_one = 0.9
beta_two = 0.95
adam_eps = 1e-08
weight_decay = 0.01
average_decay = 0.9
block_group = (0, 0, 0, 1, 2, 2, 3)
block_scale = (3.0**0.5, 3.0**0.5, 3.0**0.5, 1.0, 2.0**0.5, 2.0**0.5, 1.0)


def matmul(left, right):
    return jnp.dot(left, right, precision=highest)


def silu(value):
    return value * jax.nn.sigmoid(value)


def layer_norm(value):
    centered = value - jnp.mean(value, axis=-1, keepdims=True)
    return centered * lax.rsqrt(jnp.mean(centered * centered, axis=-1, keepdims=True) + 1e-05)


def encode(grid_input, edge_input, mesh_index, encoder_weights, node_count):
    channels = grid_input.shape[1]
    embedded = silu(matmul(grid_input, encoder_weights[:channels]))
    node_lat = layer_norm(jax.ops.segment_sum(embedded, mesh_index, num_segments=node_count))
    edge_lat = silu(matmul(edge_input, encoder_weights[channels:]))
    return (node_lat, edge_lat)


def processor(node_lat, edge_lat, send_lat, recv_index, weights, params):
    recv_lat = node_lat[recv_index]
    before = (
        matmul(edge_lat, weights[0])
        + matmul(send_lat, weights[1])
        + matmul(recv_lat, weights[2])
        + params[0]
    )
    message = matmul(silu(before), weights[3]) + params[1]
    edge_lat = edge_lat + layer_norm(message) * (1.0 + params[2]) + params[3]
    summed = jax.ops.segment_sum(edge_lat, recv_index, num_segments=node_lat.shape[0])
    before = matmul(node_lat, weights[4]) + matmul(summed, weights[5]) + params[4]
    update = matmul(silu(before), weights[6]) + params[5]
    node_lat = node_lat + layer_norm(update) * (1.0 + params[6]) + params[7]
    return (node_lat, edge_lat)


def decode(read_lat, grid_input, grid_target, loss_mask, decoder_weights):
    gathered = jnp.sum(read_lat.reshape(-1, 3, read_lat.shape[1]), axis=1)
    predicted = grid_input + matmul(silu(gathered), decoder_weights)
    missed = predicted - grid_target
    return jnp.sum(loss_mask.astype(jnp.float32)[:, None] * missed * missed)


def group_sum(values):
    return jnp.stack(
        [
            values[:, 0] + values[:, 1] + values[:, 2],
            values[:, 3],
            values[:, 4] + values[:, 5],
            values[:, 6],
        ],
        axis=1,
    )


def spread(values):
    return jnp.take(values, jnp.array(block_group, dtype=jnp.int32), axis=1)


def orthogonalize(momentum, total_norm, total_gram):
    squares = total_norm(group_sum(jnp.sum(momentum * momentum, axis=(2, 3))))
    iterate = momentum / (jnp.sqrt(spread(squares)) + 1e-07)[:, :, None, None]
    for sweep in range(NS_ITERS):
        gram = total_gram(
            group_sum(jnp.einsum("lbrd,lbre->lbde", iterate, iterate, precision=highest))
        )
        polynom = coef_b * gram + coef_c * jnp.einsum(
            "lgde,lgef->lgdf", gram, gram, precision=highest
        )
        iterate = coef_a * iterate + jnp.einsum(
            "lbrd,lbde->lbre", iterate, spread(polynom), precision=highest
        )
    return iterate


def muon_finish(weights, ortho):
    scales = jnp.array(block_scale, dtype=weights.dtype)[None, :, None, None]
    return weights * (1.0 - muon_rate * weight_decay) - muon_rate * scales * ortho


def adam_update(values, first, second, gradient, rate):
    first = beta_one * first + (1.0 - beta_one) * gradient
    second = beta_two * second + (1.0 - beta_two) * gradient * gradient
    corrected = (
        first / (1.0 - beta_one**STEP) / (jnp.sqrt(second / (1.0 - beta_two**STEP)) + adam_eps)
    )
    return (first, second, values * (1.0 - rate * weight_decay) - rate * corrected)


def body(
    grid_input,
    grid_target,
    edge_input,
    senders,
    receivers,
    border_nodes,
    grid_to_mesh,
    mesh_to_grid,
    loss_mask,
    encoder_weights,
    encoder_first,
    encoder_second,
    processor_weights,
    processor_momentum,
    processor_average,
    norm_params,
    norm_first,
    norm_second,
    decoder_weights,
    decoder_first,
    decoder_second,
):
    full_weights = lax.all_gather(processor_weights, "row", axis=2, tiled=True)

    def share_border(node_lat):
        return lax.all_gather(node_lat[border_nodes], "band", axis=0, tiled=True)

    def return_border(table_grad, node_grad):
        owned = lax.psum_scatter(table_grad, "band", scatter_dimension=0, tiled=True)
        return node_grad + jax.ops.segment_sum(owned, border_nodes, num_segments=NODE_DEV)

    def encode_local(encoder_now):
        return encode(grid_input, edge_input, grid_to_mesh, encoder_now, NODE_DEV)

    def layer_local(node_lat, edge_lat, table, weights, params):
        combined = jnp.concatenate([node_lat, table], axis=0)
        return processor(node_lat, edge_lat, combined[senders], receivers, weights, params)

    def decode_local(node_lat, table, decoder_now):
        combined = jnp.concatenate([node_lat, table], axis=0)
        return decode(combined[mesh_to_grid], grid_input, grid_target, loss_mask, decoder_now)

    node_lat, edge_lat = encode_local(encoder_weights)
    kept = []
    for depth in range(LAYERS):
        table = share_border(node_lat)
        kept.append((node_lat, edge_lat, table))
        node_lat, edge_lat = layer_local(
            node_lat, edge_lat, table, full_weights[depth], norm_params[depth]
        )
    table = share_border(node_lat)
    local_loss, decode_back = jax.vjp(decode_local, node_lat, table, decoder_weights)
    loss_total, mask_count = lax.psum((local_loss, jnp.sum(loss_mask.astype(jnp.float32))), "band")
    node_grad, table_grad, decoder_grad = decode_back(1.0 / mask_count)
    node_grad = return_border(table_grad, node_grad)
    edge_grad = jnp.zeros_like(edge_lat)
    weight_list = [None] * LAYERS
    param_list = [None] * LAYERS
    for depth in reversed(range(LAYERS)):
        saved_nodes, saved_edges, saved_table = kept[depth]
        outputs, layer_back = jax.vjp(
            layer_local,
            saved_nodes,
            saved_edges,
            saved_table,
            full_weights[depth],
            norm_params[depth],
        )
        node_grad, edge_grad, table_grad, weight_list[depth], param_list[depth] = layer_back(
            (node_grad, edge_grad)
        )
        node_grad = return_border(table_grad, node_grad)
    outputs, encode_back = jax.vjp(encode_local, encoder_weights)
    (encoder_grad,) = encode_back((node_grad, edge_grad))
    rows_dev = processor_weights.shape[2]
    row_start = lax.axis_index("row") * rows_dev
    row_grad = lax.dynamic_slice_in_dim(jnp.stack(weight_list), row_start, rows_dev, 2)
    row_grad, param_grad, encoder_grad, decoder_grad = lax.psum(
        (row_grad, jnp.stack(param_list), encoder_grad, decoder_grad), "band"
    )
    next_momentum = momentum_decay * processor_momentum + row_grad

    def norm_total(value):
        return lax.psum(value, "row")

    def gram_total(value):
        return lax.psum(value, "row")

    ortho = orthogonalize(next_momentum, norm_total, gram_total)
    next_weights = muon_finish(processor_weights, ortho)
    next_average = average_decay * processor_average + (1.0 - average_decay) * next_weights
    param_moment, param_square, param_values = adam_update(
        norm_params, norm_first, norm_second, param_grad, param_rate
    )
    encoder_moment, encoder_square, encoder_values = adam_update(
        encoder_weights, encoder_first, encoder_second, encoder_grad, adam_rate
    )
    decoder_moment, decoder_square, decoder_values = adam_update(
        decoder_weights, decoder_first, decoder_second, decoder_grad, adam_rate
    )
    return (
        loss_total,
        mask_count,
        next_weights,
        next_momentum,
        next_average,
        param_moment,
        param_square,
        param_values,
        encoder_moment,
        encoder_square,
        encoder_values,
        decoder_moment,
        decoder_square,
        decoder_values,
    )


def solution(mesh):
    return jax.shard_map(
        body,
        mesh=mesh,
        in_specs=(
            P("band", None),
            P("band", None),
            P("band", None),
            P("band"),
            P("band"),
            P("band"),
            P("band"),
            P("band"),
            P("band"),
            P(),
            P(),
            P(),
            P(None, None, "row", None),
            P(None, None, "row", None),
            P(None, None, "row", None),
            P(),
            P(),
            P(),
            P(),
            P(),
            P(),
        ),
        out_specs=(
            P(),
            P(),
            P(None, None, "row", None),
            P(None, None, "row", None),
            P(None, None, "row", None),
            P(),
            P(),
            P(),
            P(),
            P(),
            P(),
            P(),
            P(),
            P(),
        ),
        check_vma=False,
    )
```

profile of v0, /device:TPU:0, one launch (start us, length us, event | category | flops | bytes accessed | tf_op | source)
XLA Modules:
  0.0 2321.5 jit_solution(2988629578712785335)
XLA Ops:
  11.2 7.3 scatter_custom_fusion
  31.0 16.0 all-gather.12.cloned.1.call-done
  53.1 369.5 %all-gather.10.cloned.1.call-done = f32[3,7,512,512]{3,2,1,0:T(8,128)} async-done(((f32[3,7,128,512]{3,2,1,0:T(8,128)}), f32[3,7,512,512]{3,2,1,0:T(8,128)}) %all-gather.10.cloned.1.call-update) | async-done | bytes 22020112 | tf_op jit(solution)/shard_map/all_gather | solution.py:143
  441.1 7.5 fusion.232
  452.6 10.6 scatter_custom_fusion.1
  488.6 7.3 all-gather.14.cloned.1.call-done
  501.8 7.6 convolution_add_fusion.8
  525.6 10.5 scatter_custom_fusion.2
  552.1 7.8 fusion.114
  559.9 8.0 all-gather.16.cloned.1.call-done
  573.8 7.6 convolution_add_fusion.5
  596.6 12.0 scatter_custom_fusion.3
  617.3 13.8 psum.64
  631.9 8.5 all-gather.18.cloned.1.call-done
  641.8 8.7 gather_fusion.10
  650.6 10.0 reshape.492
  660.5 7.9 reduce_sum.513
  684.6 9.8 reshape.698
  694.4 19.8 scatter_custom_fusion.4
  722.7 28.9 %reduce-scatter.5.cloned.1.call-done = f32[64,512]{1,0:T(8,128)} async-done(((f32[512,512]{1,0:T(8,128)}), f32[64,512]{1,0:T(8,128)}) %reduce-scatter.5.cloned.1.call-update) | async-done | bytes 131088 | tf_op jit(solution)/shard_map/reduce_scatter | solution.py:149
  777.0 8.2 fusion.238
  803.3 11.5 scatter_custom_fusion.6
  829.3 10.9 scatter_fusion.1
  875.1 9.8 multiply_reduce_fusion.2
  887.8 7.3 fusion.240
  913.7 11.5 scatter_custom_fusion.9
  940.6 10.7 scatter_fusion.2
  991.3 9.7 multiply_reduce_fusion.3
  1010.1 7.3 fusion.242
  1034.3 7.5 fusion.103
  1041.8 11.5 scatter_custom_fusion.12
  1071.3 10.7 scatter_fusion.3
  1109.6 106.5 %all-reduce.57.cloned.1.call-done = (f32[3,7,128,512]{3,2,1,0:T(8,128)}, f32[231,512]{1,0:T(8,128)}, f32[512,227]{0,1:T(8,128)}) async-done(((f32[3,7,128,512]{3,2,1,0:T(8,128)}, f32[231,512]{1,0:T(8,128)}, f32[512,227]{0,1:T(8,128)}), (f32[3,7,128,512]{3,2,1,0:T(8,128)}, f32[231,512]{1,0:T(8,128)}, f32[512,227]{0,1:T(8,128)})) %all-reduce.57.cloned.1.call-update) | async-done | bytes 6443024 | tf_op jit(solution)/shard_map/psum | solution.py:198
  1216.1 7.5 multiply_reduce_fusion
  1224.3 11.7 psum.66
  1236.7 21.6 fusion.52
  1264.2 10.3 pad_maximum_fusion
  1274.8 423.3 %all-reduce.53.cloned.1.call-done = f32[3,4,512,512]{3,2,1,0:T(8,128)} async-done(((f32[3,4,512,512]{3,2,1,0:T(8,128)}), f32[3,4,512,512]{3,2,1,0:T(8,128)}) %all-reduce.53.cloned.1.call-update) | async-done | bytes 12582928 | tf_op jit(solution)/shard_map/psum | solution.py:207
  1698.1 37.8 %multiply_add_fusion.1 = f32[3,4,512,512]{3,2,1,0:T(8,128)} fusion(f32[3,4,512,512]{3,2,1,0:T(8,128)} %all-reduce.53.cloned.1.call-done), kind=kOutput, calls=%fused_computation.43 | convolution fusion | flops 19336790016 | bytes 25165824 | tf_op jit(solution)/shard_map/lgde,lgef->lgdf/dot_general | solution.py:97
  1735.9 14.9 gather_fusion.16
  1750.8 22.1 multiply_add_fusion.3
  1772.9 20.8 fusion.244
  1799.7 10.7 pad_maximum_fusion.1
  1815.2 26.8 %all-reduce.47 = (f32[]{:T(128)}, f32[3,8,512]{2,1,0:T(8,128)}) all-reduce(f32[]{:T(128)} %get-tuple-element.116, f32[3,8,512]{2,1,0:T(8,128)S(1)} %pad_maximum_fusion.6), channel_id=1, replica_groups=mesh['band'=8,'row'=4] {'band'}, use_global_device_ids=true, to_apply=%region_20.0 | all-reduce | flops 12289 | bytes 98312 | tf_op jit(solution)/shard_map/psum | solution.py:173
  1847.2 388.5 %all-reduce.55.cloned.1.call-done = f32[3,4,512,512]{3,2,1,0:T(8,128)} async-done(((f32[3,4,512,512]{3,2,1,0:T(8,128)}), f32[3,4,512,512]{3,2,1,0:T(8,128)}) %all-reduce.55.cloned.1.call-update) | async-done | bytes 12582928 | tf_op jit(solution)/shard_map/psum | solution.py:207
  2235.7 37.8 %multiply_add_fusion = f32[3,4,512,512]{3,2,1,0:T(8,128)} fusion(f32[3,4,512,512]{3,2,1,0:T(8,128)} %all-reduce.55.cloned.1.call-done), kind=kOutput, calls=%fused_computation.42 | convolution fusion | flops 19336790016 | bytes 25165824 | tf_op jit(solution)/shard_map/lgde,lgef->lgdf/dot_general | solution.py:97
  2273.5 15.0 gather_fusion.17
  2288.5 26.0 %multiply_add_fusion.2 = (f32[3,7,128,512]{3,2,1,0:T(8,128)}, f32[3,7,128,512]{3,2,1,0:T(8,128)}) fusion(f32[3,7,128,512]{3,2,1,0:T(8,128)} %param.41, f32[3,7,128,512]{3,2,1,0:T(8,128)} %multiply_add_fusion.3, f32[7]{0:T(128)S(1)} %copy-done.167, f32[3,7,128,512]{3,2,1,0:T(8,128)} %param.39, f32[7,3,512,512]{3,2,1,0:T(8,128)} %gather_fusion.17), kind=kOutput, calls=%fused_computation.49 | convolution fusion | flops 8466726912 | bytes 49545244 | tf_op jit(solution)/shard_map/lbrd,lbde->lbre/dot_general | solution.py:100
  (576 shorter events, 426.9 us)
Async XLA Ops:
  7.2 19.3 copy-start
  7.2 39.8 %all-gather.12.cloned.1.call-start = ((), (), s32[]{:S(2)}) async-start(), calls=%async_computation.11 | async-start | bytes 1179648 | tf_op jit(solution)/shard_map/all_gather | solution.py:146
  18.7 452.8 %copy-start.119 = (f32[320]{0:T(512)}, f32[320]{0:T(512)S(1)}, u32[]{:S(2)}) copy-start(f32[320]{0:T(512)S(1)} %broadcast_multiply_fusion.6) | copy-start | bytes 3844
  19.0 452.6 %copy-start.136 = (f32[320]{0:T(512)}, f32[320]{0:T(512)S(1)}, u32[]{:S(2)}) copy-start(f32[320]{0:T(512)S(1)} %fusion.197) | copy-start | bytes 3844
  19.2 444.1 %copy-start.1 = (f32[320,512]{1,0:T(8,128)}, f32[320,512]{1,0:T(8,128)S(1)}, u32[]{:S(2)}) copy-start(f32[320,512]{1,0:T(8,128)S(1)} %subtract_multiply_fusion.9) | copy-start | bytes 1966084
  20.5 402.0 %all-gather.10.cloned.1.call-start = ((), (), s32[]{:S(2)}) async-start(), calls=%async_computation.4 | async-start | bytes 27525120 | tf_op jit(solution)/shard_map/all_gather | solution.py:143
  21.3 474.5 %all-gather.14.cloned.1.call-start = ((), (), s32[]{:S(2)}) async-start(), calls=%async_computation.12 | async-start | bytes 1179648 | tf_op jit(solution)/shard_map/all_gather | solution.py:146
  26.4 22.0 copy-start.133
  26.4 422.9 %copy-start.125 = (f32[1,1,512]{2,1,0:T(1,128)}, f32[1,1,512]{2,1,0:T(1,128)S(1)}, u32[]{:S(2)}) copy-start(f32[1,1,512]{2,1,0:T(1,128)S(1)} %get-tuple-element.94) | copy-start | bytes 6148
  26.5 445.1 %copy-start.134 = (f32[1,1,512]{2,1,0:T(1,128)}, f32[1,1,512]{2,1,0:T(1,128)S(1)}, u32[]{:S(2)}) copy-start(f32[1,1,512]{2,1,0:T(1,128)S(1)} %get-tuple-element.89) | copy-start | bytes 6148
  53.1 376.4 %copy-start.27 = (f32[1280,512]{1,0:T(8,128)S(1)}, f32[1280,512]{1,0:T(8,128)}, u32[]{:S(2)}) copy-start(f32[1280,512]{1,0:T(8,128)} %gather_fusion.1) | copy-start | bytes 7864324
  452.6 29.0 %copy-start.7 = (f32[1280,512]{1,0:T(8,128)}, f32[1280,512]{1,0:T(8,128)S(1)}, u32[]{:S(2)}) copy-start(f32[1280,512]{1,0:T(8,128)S(1)} %add_add_fusion.4) | copy-start | bytes 7864324
  473.7 94.1 %all-gather.16.cloned.1.call-start = ((), (), s32[]{:S(2)}) async-start(), calls=%async_computation.13 | async-start | bytes 1179648 | tf_op jit(solution)/shard_map/all_gather | solution.py:146
  525.6 16.3 copy-start.14
  544.2 96.1 %all-gather.18.cloned.1.call-start = ((), (), s32[]{:S(2)}) async-start(), calls=%async_computation.14 | async-start | bytes 1179648 | tf_op jit(solution)/shard_map/all_gather | solution.py:146
  596.6 12.0 copy-start.84
  614.3 17.5 copy-start.147
  615.3 16.5 copy-start.56
  616.7 134.9 %reduce-scatter.5.cloned.1.call-start = ((), (), s32[]{:S(2)}) async-start(), calls=%async_computation.5 | async-start | bytes 1179648 | tf_op jit(solution)/shard_map/reduce_scatter | solution.py:149
  715.4 140.6 %reduce-scatter.7.cloned.1.call-start = ((), (), s32[]{:S(2)}) async-start(), calls=%async_computation.6 | async-start | bytes 1179648 | tf_op jit(solution)/shard_map/reduce_scatter | solution.py:149
  717.8 33.8 %copy-start.175 = (s32[64]{0:T(128)S(1)}, s32[64]{0:T(128)}, u32[]{:S(2)}) copy-start(s32[64]{0:T(128)} %param.32) | copy-start | bytes 772
  722.7 30.7 %copy-start.55 = (f32[320,512]{1,0:T(8,128)S(1)}, f32[320,512]{1,0:T(8,128)}, u32[]{:S(2)}) copy-start(f32[320,512]{1,0:T(8,128)} %copy-done.54) | copy-start | bytes 1966084
  722.7 32.0 %copy-start.100 = (f32[320,512]{1,0:T(8,128)S(1)}, f32[320,512]{1,0:T(8,128)}, u32[]{:S(2)}) copy-start(f32[320,512]{1,0:T(8,128)} %copy-done.99) | copy-start | bytes 1966084
  776.9 8.2 copy-start.39
  776.9 70.4 %copy-start.127 = (f32[1280]{0:T(1024)}, f32[1280]{0:T(1024)S(1)}, u32[]{:S(2)}) copy-start(f32[1280]{0:T(1024)S(1)} %negate_multiply_fusion.2) | copy-start | bytes 15364
  785.1 32.3 %copy-start.3 = (f32[1280,512]{1,0:T(8,128)}, f32[1280,512]{1,0:T(8,128)S(1)}, u32[]{:S(2)}) copy-start(f32[1280,512]{1,0:T(8,128)S(1)} %get-tuple-element.119) | copy-start | bytes 7864324
  817.2 149.2 %reduce-scatter.9.cloned.1.call-start = ((), (), s32[]{:S(2)}) async-start(), calls=%async_computation.7 | async-start | bytes 1179648 | tf_op jit(solution)/shard_map/reduce_scatter | solution.py:149
  875.1 9.8 copy-start.11
  886.6 8.5 copy-start.45
  886.6 71.0 %copy-start.129 = (f32[1280]{0:T(1024)}, f32[1280]{0:T(1024)S(1)}, u32[]{:S(2)}) copy-start(f32[1280]{0:T(1024)S(1)} %negate_multiply_fusion.1) | copy-start | bytes 15364
  927.5 169.2 %reduce-scatter.11.cloned.1.call-start = ((), (), s32[]{:S(2)}) async-start(), calls=%async_computation.10 | async-start | bytes 1179648 | tf_op jit(solution)/shard_map/reduce_scatter | solution.py:149
  991.2 9.8 copy-start.117
  991.2 9.8 copy-start.6
  1055.6 160.5 %all-reduce.57.cloned.1.call-start = ((), (), s32[]{:S(2)}) async-start(), calls=%async_computation.15 | async-start | bytes 12910592 | tf_op jit(solution)/shard_map/psum | solution.py:198
  1109.1 588.9 %all-reduce.53.cloned.1.call-start = ((), (), s32[]{:S(2)}) async-start(), calls=%async_computation.8 | async-start | bytes 25165824 | tf_op jit(solution)/shard_map/psum | solution.py:207
  1216.1 8.2 copy-start.176
  1274.6 961.1 %all-reduce.55.cloned.1.call-start = ((), (), s32[]{:S(2)}) async-start(), calls=%async_computation.9 | async-start | bytes 25165824 | tf_op jit(solution)/shard_map/psum | solution.py:207
  1813.7 28.3 %copy-start.113 = (f32[3,8,512]{2,1,0:T(8,128)S(1)}, f32[3,8,512]{2,1,0:T(8,128)}, u32[]{:S(2)}) copy-start(f32[3,8,512]{2,1,0:T(8,128)} %param.42) | copy-start | bytes 147460
  1813.7 28.3 %copy-start.123 = (f32[3,8,512]{2,1,0:T(8,128)S(1)}, f32[3,8,512]{2,1,0:T(8,128)}, u32[]{:S(2)}) copy-start(f32[3,8,512]{2,1,0:T(8,128)} %param.44) | copy-start | bytes 147460
  1813.7 28.3 %copy-start.124 = (f32[3,8,512]{2,1,0:T(8,128)S(1)}, f32[3,8,512]{2,1,0:T(8,128)}, u32[]{:S(2)}) copy-start(f32[3,8,512]{2,1,0:T(8,128)} %param.43) | copy-start | bytes 147460
  1814.0 29.5 %copy-start.91 = (f32[231,512]{1,0:T(8,128)S(1)}, f32[231,512]{1,0:T(8,128)}, u32[]{:S(2)}) copy-start(f32[231,512]{1,0:T(8,128)} %param.36) | copy-start | bytes 1419268
  1814.0 29.5 %copy-start.101 = (f32[231,512]{1,0:T(8,128)S(1)}, f32[231,512]{1,0:T(8,128)}, u32[]{:S(2)}) copy-start(f32[231,512]{1,0:T(8,128)} %param.38) | copy-start | bytes 1419268
  1814.0 29.4 %copy-start.102 = (f32[231,512]{1,0:T(8,128)S(1)}, f32[231,512]{1,0:T(8,128)}, u32[]{:S(2)}) copy-start(f32[231,512]{1,0:T(8,128)} %param.37) | copy-start | bytes 1419268
  1814.8 31.1 %copy-start.104 = (f32[512,227]{0,1:T(8,128)S(1)}, f32[512,227]{0,1:T(8,128)}, u32[]{:S(2)}) copy-start(f32[512,227]{0,1:T(8,128)} %param.45) | copy-start | bytes 1394692
  1814.8 31.1 %copy-start.105 = (f32[512,227]{0,1:T(8,128)S(1)}, f32[512,227]{0,1:T(8,128)}, u32[]{:S(2)}) copy-start(f32[512,227]{0,1:T(8,128)} %param.47) | copy-start | bytes 1394692
  1814.8 31.1 %copy-start.106 = (f32[512,227]{0,1:T(8,128)S(1)}, f32[512,227]{0,1:T(8,128)}, u32[]{:S(2)}) copy-start(f32[512,227]{0,1:T(8,128)} %param.46) | copy-start | bytes 1394692
  1814.8 31.1 %copy-start.107 = (f32[512,227]{0,1:T(8,128)S(1)}, f32[512,227]{0,1:T(8,128)}, u32[]{:S(2)}) copy-start(f32[512,227]{0,1:T(8,128)} %get-tuple-element.37) | copy-start | bytes 1394692
  2273.5 15.0 copy-start.167
  (142 other events, 560.5 us)
Sparse Core Ops, SparseCore 0:
  20.6 26.2 all-gather.11
  48.6 373.9 all-gather.9
  473.9 21.9 all-gather.13
  544.4 23.4 all-gather.15
  616.8 23.4 all-gather.17
  715.5 35.9 reduce-scatter.4
  817.3 36.0 reduce-scatter.6
  927.6 36.0 reduce-scatter.8
  1055.7 36.0 reduce-scatter.10
  1109.2 106.7 all-reduce.56
  1274.7 423.3 all-reduce.52
  1810.6 425.0 all-reduce.54
where the time goes:
time: 2330 us; the launch traced here: 2320 us
  waiting for transfers between devices  1360 us (58%)
  matrix products  514 us (22%)
  other arithmetic  238 us (10%)
  local copies, waits for them, and re-layouts  140 us (6%)
  blocking collectives  52.3 us (2%)
    psum x2, waiting for transfers between devices, gram_total(): return lax.psum(value, 'row')  812 us
    all_gather x1, waiting for transfers between devices, body(): full_weights = lax.all_gather(processor_weights, 'row', axis=2, tiled=True)  369 us
    dot_general x70, matrix products, matmul(): return jnp.dot(left, right, precision=highest)  348 us
    psum x1, waiting for transfers between devices, body(): lax.psum((row_grad, jnp.stack(param_list), encoder_grad, decoder_grad), '...  106 us
    dot_general x2, matrix products, orthogonalize(): jnp.einsum('lgde,lgef->lgdf', gram, gram, precision=highest)  75.6 us
    dot_general x2, matrix products, orthogonalize(): jnp.einsum('lbrd,lbde->lbre', iterate, spread(polynom), precision=highest)  48.1 us
  transfers between devices with their start and end apart: 12, of which 9 were waited for; matrix products, arithmetic and copies ran while one was open for 8% of the time, Pallas kernels for 0%

commit v1 on v0

--- a/solution.py
+++ b/solution.py
@@ -1,10 +1,13 @@
+import functools
+
 import jax
 import jax.numpy as jnp
 from jax import lax
+from jax.experimental import pallas as pl
+from jax.experimental.pallas import tpu as pltpu
 from jax.sharding import PartitionSpec as P
 
 LAYERS = 3
-NS_ITERS = 2
 STEP = 10
 NODE_DEV = 320
 
@@ -22,7 +25,6 @@
 adam_eps = 1e-08
 weight_decay = 0.01
 average_decay = 0.9
-block_group = (0, 0, 0, 1, 2, 2, 3)
 block_scale = (3.0**0.5, 3.0**0.5, 3.0**0.5, 1.0, 2.0**0.5, 2.0**0.5, 1.0)
 
 
@@ -71,36 +73,477 @@
     return jnp.sum(loss_mask.astype(jnp.float32)[:, None] * missed * missed)
 
 
-def group_sum(values):
-    return jnp.stack(
-        [
-            values[:, 0] + values[:, 1] + values[:, 2],
-            values[:, 3],
-            values[:, 4] + values[:, 5],
-            values[:, 6],
+MESH = pl.DeviceIdType.MESH
+NN = (((1,), (0,)), ((), ()))
+NT = (((1,), (1,)), ((), ()))
+TN = (((0,), (0,)), ((), ()))
+OWNER_CHIPS = 4
+SLOTS = 3
+ANY = pl.BlockSpec(memory_space=pl.ANY)
+VMEM = pl.BlockSpec(memory_space=pltpu.VMEM)
+
+
+def pieces(value):
+    high = value.astype(jnp.bfloat16)
+    return high, (value - high.astype(jnp.float32)).astype(jnp.bfloat16)
+
+
+def dot(left, right, dims=NN):
+    return lax.dot_general(left, right, dims, preferred_element_type=jnp.float32)
+
+
+def product(left, right, dims=NN):
+    left_high, left_low = pieces(left)
+    right_high, right_low = pieces(right)
+    return (
+        dot(left_high, right_high, dims)
+        + dot(left_low, right_high, dims)
+        + dot(left_high, right_low, dims)
+    )
+
+
+def slot_block(owner, slot):
+    third = owner // 3
+    last = third // 2
+    return (1 - last) * (7 * (owner % 3) + 4 * third + slot) + last * (
+        3 + 14 * (owner - 6) + 7 * slot
+    )
+
+
+def slot_used(owner, slot):
+    return owner < (8, 7, 6)[slot]
+
+
+def spread_slots(blocks, rows_dev, width):
+    empty = jnp.zeros((rows_dev, width), jnp.float32)
+    order = []
+    for core in range(2):
+        for chip in range(OWNER_CHIPS):
+            owner = 2 * chip + core
+            for slot in range(SLOTS):
+                order.append(blocks[slot_block(owner, slot)] if slot_used(owner, slot) else empty)
+    return jnp.stack(order).reshape(2, OWNER_CHIPS, SLOTS, rows_dev, width)
+
+
+def remote(src, dst, send_sem, recv_sem, device):
+    return pltpu.make_async_remote_copy(
+        src_ref=src,
+        dst_ref=dst,
+        send_sem=send_sem,
+        recv_sem=recv_sem,
+        device_id=device,
+        device_id_type=MESH,
+    )
+
+
+def newton(mom_ref, out_ref, first, count, gram, poly, temp, later):
+    def add_square(i, total):
+        block = mom_ref[first + i]
+        return total + jnp.sum(jnp.sum(block * block, axis=0, keepdims=True), axis=1, keepdims=True)
+
+    total = lax.fori_loop(0, count, add_square, jnp.zeros((1, 1), jnp.float32))
+    scale = 1.0 / (jnp.sqrt(total) + 1e-07)
+    gram[...] = jnp.zeros_like(gram)
+
+    def add_gram(i, carry):
+        block = mom_ref[first + i] * scale
+        mom_ref[first + i] = block
+        gram[...] += product(block, block, TN)
+        return carry
+
+    lax.fori_loop(0, count, add_gram, 0)
+    poly[...] = coef_b * gram[...] + coef_c * product(gram[...], gram[...])
+    temp[...] = coef_a * gram[...] + product(gram[...], poly[...])
+    gram[...] = coef_a * temp[...] + product(temp[...], poly[...])
+    later[...] = coef_b * gram[...] + coef_c * product(gram[...], gram[...])
+    temp[...] = coef_a * (poly[...] + later[...]) + product(poly[...], later[...])
+
+    def finish(i, carry):
+        block = mom_ref[first + i]
+        out_ref[first + i] = (coef_a * coef_a) * block + product(block, temp[...])
+        return carry
+
+    lax.fori_loop(0, count, finish, 0)
+
+
+def tail_kernel(
+    bands,
+    rows,
+    grad_ref,
+    small_ref,
+    mom_ref,
+    total_ref,
+    ortho_ref,
+    shared_ref,
+    sib_grad,
+    sib_small,
+    part,
+    part_small,
+    land,
+    land_small,
+    mine,
+    mine_small,
+    held,
+    matrix,
+    result,
+    back,
+    gram,
+    poly,
+    temp,
+    later,
+    load_sem,
+    sib_send,
+    sib_recv,
+    red_send,
+    red_recv,
+    all_send,
+    all_recv,
+    pass_send,
+    pass_recv,
+    up_send,
+    up_recv,
+    down_send,
+    down_recv,
+    keep_sem,
+):
+    chips = bands // 2
+    band = lax.axis_index("band")
+    row = lax.axis_index("row")
+    chip, core = band // 2, band % 2
+    sibling = (chip * 2 + 1 - core, row)
+    rows_dev = held.shape[1]
+    everyone = chips == OWNER_CHIPS
+
+    def guard(cond, body):
+        if cond is True:
+            body()
+        else:
+            pl.when(cond)(body)
+
+    def owns(at_chip):
+        return True if everyone else at_chip < OWNER_CHIPS
+
+    def both(one, two):
+        if one is True:
+            return two
+        if two is True:
+            return one
+        return jnp.logical_and(one, two)
+
+    def used(at_chip, slot):
+        owner = at_chip * 2 + core
+        return both(owns(at_chip), True if slot in (0, 3) else slot_used(owner, slot))
+
+    barrier = pltpu.get_barrier_semaphore()
+    partners = [((chip + j) % chips * 2 + core, row) for j in range(1, chips)] + [sibling]
+    partners += [(band, (row + j) % rows) for j in range(1, rows)]
+    for partner in partners:
+        pl.semaphore_signal(barrier, inc=1, device_id=partner, device_id_type=MESH)
+    pl.semaphore_wait(barrier, len(partners))
+
+    first = remote(grad_ref.at[1 - core], sib_grad, sib_send.at[0], sib_recv.at[0], sibling)
+    second = remote(small_ref.at[1 - core], sib_small, sib_send.at[1], sib_recv.at[1], sibling)
+    first.start()
+    second.start()
+    owner = band
+
+    def load(slot):
+        return pltpu.make_async_copy(
+            mom_ref.at[slot_block(owner, slot)], held.at[slot], load_sem.at[slot]
+        )
+
+    for slot in range(SLOTS):
+        guard(used(chip, slot), lambda slot=slot: load(slot).start())
+    first.wait()
+    second.wait()
+    for at in range(OWNER_CHIPS):
+        part[at] = grad_ref[core, at] + sib_grad[at]
+    part_small[...] = small_ref[core] + sib_small[...]
+
+    def to_owner(j):
+        to = (chip + j) % chips
+        return (
+            remote(part.at[to], land.at[j - 1], red_send.at[j - 1, 0], red_recv.at[j - 1, 0], (to * 2 + core, row)),
+            remote(part_small.at[to], land_small.at[j - 1], red_send.at[j - 1, 1], red_recv.at[j - 1, 1], (to * 2 + core, row)),
+        )
+
+    for j in range(1, chips):
+        def send(j=j):
+            for copy in to_owner(j):
+                copy.start()
+
+        guard(owns((chip + j) % chips), send)
+
+    def reduce():
+        mine[...] = part[chip]
+        mine_small[...] = part_small[chip]
+        for j in range(1, chips):
+            for copy in to_owner(j):
+                copy.wait_recv()
+            mine[...] += land[j - 1]
+            mine_small[...] += land_small[j - 1]
+
+    guard(owns(chip), reduce)
+
+    def source(kind, slot):
+        if slot == 3:
+            return mine_small
+        return (mine, back)[kind].at[slot]
+
+    def target(kind, slot, at_chip, at_core):
+        at_owner = at_chip * 2 + at_core
+        if slot == 3:
+            return shared_ref.at[at_owner]
+        return (total_ref, ortho_ref)[kind].at[slot_block(at_owner, slot)]
+
+    def keep(kind, slot):
+        return pltpu.make_async_copy(
+            source(kind, slot), target(kind, slot, chip, core), keep_sem.at[kind, slot]
+        )
+
+    def out(kind, slot, j):
+        return remote(
+            source(kind, slot),
+            target(kind, slot, chip, core),
+            all_send.at[kind, j - 1, slot],
+            all_recv.at[kind, j - 1, slot],
+            ((chip + j) % chips * 2 + core, row),
+        )
+
+    def across(kind, slot, at_chip, j):
+        src = source(kind, slot) if j == 0 else target(kind, slot, at_chip, core)
+        return remote(
+            src,
+            target(kind, slot, at_chip, core),
+            pass_send.at[kind, j, slot],
+            pass_recv.at[kind, j, slot],
+            sibling,
+        )
+
+    def crossed(kind, slot, at_chip, j):
+        return remote(
+            source(kind, slot),
+            target(kind, slot, at_chip, 1 - core),
+            pass_send.at[kind, j, slot],
+            pass_recv.at[kind, j, slot],
+            sibling,
+        )
+
+    def used_other(at_chip, slot):
+        at_owner = at_chip * 2 + 1 - core
+        return both(owns(at_chip), True if slot in (0, 3) else slot_used(at_owner, slot))
+
+    def publish(kind, slots):
+        for slot in slots:
+            def start(slot=slot):
+                for j in range(1, chips):
+                    out(kind, slot, j).start()
+                keep(kind, slot).start()
+                across(kind, slot, chip, 0).start()
+
+            guard(used(chip, slot), start)
+
+    def relay(kind, slots):
+        for j in range(1, chips):
+            origin = (chip - j + chips) % chips
+            for slot in slots:
+                def start(slot=slot, j=j, origin=origin):
+                    remote(
+                        source(kind, slot),
+                        target(kind, slot, origin, core),
+                        all_send.at[kind, j - 1, slot],
+                        all_recv.at[kind, j - 1, slot],
+                        (origin * 2 + core, row),
+                    ).wait_recv()
+                    across(kind, slot, origin, j).start()
+
+                guard(used(origin, slot), start)
+
+    def settle(kind, slots):
+        for j in range(chips):
+            origin = (chip - j + chips) % chips
+            for slot in slots:
+                def finish(slot=slot, j=j, origin=origin):
+                    across(kind, slot, origin, j).wait_send()
+
+                def arrive(slot=slot, j=j, origin=origin):
+                    crossed(kind, slot, origin, j).wait_recv()
+
+                guard(used(origin, slot), finish)
+                guard(used_other(origin, slot), arrive)
+        for slot in slots:
+            def sent(slot=slot):
+                for j in range(1, chips):
+                    out(kind, slot, j).wait_send()
+                keep(kind, slot).wait()
+
+            guard(used(chip, slot), sent)
+
+    third = owner // 3
+    row_a = rows // 2 - 1 + core
+    row_b = rows // 2 - core
+    split_at = 3 - third
+
+    def home(slot):
+        if slot == 0:
+            return row_a
+        late = (slot + third) // 3
+        return row_a + late * (row_b - row_a)
+
+    def up(slot, from_row):
+        at = pl.ds(pl.multiple_of(from_row * rows_dev, rows_dev), rows_dev)
+        step = (from_row - home(slot) + rows) % rows
+        return remote(
+            held.at[slot],
+            matrix.at[slot, at],
+            up_send.at[slot],
+            up_recv.at[slot, step],
+            (band, home(slot)),
+        )
+
+    for slot in range(SLOTS):
+        def momentum(slot=slot):
+            load(slot).wait()
+            held[slot] = momentum_decay * held[slot] + mine[slot]
+
+            @pl.when(row == home(slot))
+            def _():
+                at = pl.ds(pl.multiple_of(row * rows_dev, rows_dev), rows_dev)
+                matrix[slot, at] = held[slot]
+
+            @pl.when(row != home(slot))
+            def _():
+                up(slot, row).start()
+
+        guard(used(chip, slot), momentum)
+    publish(0, (0, 1, 2, 3))
+
+    def down(slot, to_row):
+        at = pl.ds(pl.multiple_of(to_row * rows_dev, rows_dev), rows_dev)
+        step = (to_row - home(slot) + rows) % rows
+        return remote(
+            result.at[slot, at],
+            back.at[slot],
+            down_send.at[slot, step],
+            down_recv.at[slot],
+            (band, to_row),
+        )
+
+    for slot in range(SLOTS):
+        def arrived(slot=slot):
+            @pl.when(row == home(slot))
+            def _():
+                for step in range(1, rows):
+                    up(slot, (row + step) % rows).wait_recv()
+
+        guard(used(chip, slot), arrived)
+
+    def at_a():
+        newton(matrix, result, 0, split_at, gram, poly, temp, later)
+
+    def at_b():
+        newton(matrix, result, split_at, 1, gram, poly, temp, later)
+
+    guard(both(owns(chip), row == row_a), at_a)
+    guard(
+        both(owns(chip), jnp.logical_and(row == row_b, jnp.logical_and(owner > 2, owner < 7))), at_b
+    )
+
+    for slot in range(SLOTS):
+        def give(slot=slot):
+            @pl.when(row == home(slot))
+            def _():
+                for step in range(1, rows):
+                    down(slot, (row + step) % rows).start()
+                at = pl.ds(pl.multiple_of(row * rows_dev, rows_dev), rows_dev)
+                back[slot] = result[slot, at]
+
+        guard(used(chip, slot), give)
+    relay(0, (0, 1, 2, 3))
+    for slot in range(SLOTS):
+        def take(slot=slot):
+            @pl.when(row != home(slot))
+            def _():
+                down(slot, row).wait_recv()
+
+        guard(used(chip, slot), take)
+    publish(1, (0, 1, 2))
+    relay(1, (0, 1, 2))
+    settle(0, (0, 1, 2, 3))
+    settle(1, (0, 1, 2))
+    for j in range(1, chips):
+        def reduced(j=j):
+            for copy in to_owner(j):
+                copy.wait_send()
+
+        guard(owns((chip + j) % chips), reduced)
+    for slot in range(SLOTS):
+        def closed(slot=slot):
+            @pl.when(row != home(slot))
+            def _():
+                up(slot, row).wait_send()
+
+            @pl.when(row == home(slot))
+            def _():
+                for step in range(1, rows):
+                    down(slot, (row + step) % rows).wait_send()
+
+        guard(used(chip, slot), closed)
+
+
+def tail(bands, rows, grads, small, momentum):
+    blocks, rows_dev, width = momentum.shape
+    chips = bands // 2
+    chunk = small.shape[2]
+    f32 = jnp.float32
+    dma = pltpu.SemaphoreType.DMA
+    square = pltpu.VMEM((width, width), f32)
+    return pl.pallas_call(
+        functools.partial(tail_kernel, bands, rows),
+        out_shape=(
+            jax.ShapeDtypeStruct((blocks, rows_dev, width), f32),
+            jax.ShapeDtypeStruct((blocks, rows_dev, width), f32),
+            jax.ShapeDtypeStruct((2 * OWNER_CHIPS, chunk, width), f32),
+        ),
+        in_specs=[VMEM, VMEM, ANY],
+        out_specs=[ANY, ANY, ANY],
+        scratch_shapes=[
+            pltpu.VMEM((OWNER_CHIPS, SLOTS, rows_dev, width), f32),
+            pltpu.VMEM((OWNER_CHIPS, chunk, width), f32),
+            pltpu.VMEM((OWNER_CHIPS, SLOTS, rows_dev, width), f32),
+            pltpu.VMEM((OWNER_CHIPS, chunk, width), f32),
+            pltpu.VMEM((chips - 1, SLOTS, rows_dev, width), f32),
+            pltpu.VMEM((chips - 1, chunk, width), f32),
+            pltpu.VMEM((SLOTS, rows_dev, width), f32),
+            pltpu.VMEM((chunk, width), f32),
+            pltpu.VMEM((SLOTS, rows_dev, width), f32),
+            pltpu.VMEM((SLOTS, width, width), f32),
+            pltpu.VMEM((SLOTS, width, width), f32),
+            pltpu.VMEM((SLOTS, rows_dev, width), f32),
+            square,
+            square,
+            square,
+            square,
+            dma((SLOTS,)),
+            dma((2,)),
+            dma((2,)),
+            dma((chips - 1, 2)),
+            dma((chips - 1, 2)),
+            dma((2, chips - 1, SLOTS + 1)),
+            dma((2, chips - 1, SLOTS + 1)),
+            dma((2, chips, SLOTS + 1)),
+            dma((2, chips, SLOTS + 1)),
+            dma((SLOTS,)),
+            dma((SLOTS, rows)),
+            dma((SLOTS, rows)),
+            dma((SLOTS,)),
+            dma((2, SLOTS + 1)),
         ],
-        axis=1,
-    )
-
-
-def spread(values):
-    return jnp.take(values, jnp.array(block_group, dtype=jnp.int32), axis=1)
-
-
-def orthogonalize(momentum, total_norm, total_gram):
-    squares = total_norm(group_sum(jnp.sum(momentum * momentum, axis=(2, 3))))
-    iterate = momentum / (jnp.sqrt(spread(squares)) + 1e-07)[:, :, None, None]
-    for sweep in range(NS_ITERS):
-        gram = total_gram(
-            group_sum(jnp.einsum("lbrd,lbre->lbde", iterate, iterate, precision=highest))
-        )
-        polynom = coef_b * gram + coef_c * jnp.einsum(
-            "lgde,lgef->lgdf", gram, gram, precision=highest
-        )
-        iterate = coef_a * iterate + jnp.einsum(
-            "lbrd,lbde->lbre", iterate, spread(polynom), precision=highest
-        )
-    return iterate
+        compiler_params=pltpu.CompilerParams(
+            collective_id=0, has_side_effects=True, vmem_limit_bytes=56 * 2**20
+        ),
+        name="tail",
+    )(grads, small, momentum)
 
 
 def muon_finish(weights, ortho):
@@ -192,22 +635,37 @@
         node_grad = return_border(table_grad, node_grad)
     outputs, encode_back = jax.vjp(encode_local, encoder_weights)
     (encoder_grad,) = encode_back((node_grad, edge_grad))
-    rows_dev = processor_weights.shape[2]
+    layers, blocks, rows_dev, width = processor_weights.shape
     row_start = lax.axis_index("row") * rows_dev
-    row_grad = lax.dynamic_slice_in_dim(jnp.stack(weight_list), row_start, rows_dev, 2)
-    row_grad, param_grad, encoder_grad, decoder_grad = lax.psum(
-        (row_grad, jnp.stack(param_list), encoder_grad, decoder_grad), "band"
-    )
-    next_momentum = momentum_decay * processor_momentum + row_grad
-
-    def norm_total(value):
-        return lax.psum(value, "row")
-
-    def gram_total(value):
-        return lax.psum(value, "row")
-
-    ortho = orthogonalize(next_momentum, norm_total, gram_total)
-    next_weights = muon_finish(processor_weights, ortho)
+    row_grads = [
+        lax.dynamic_slice_in_dim(weight_list[depth][block], row_start, rows_dev, 0)
+        for depth in range(layers)
+        for block in range(blocks)
+    ]
+    small_shapes = (encoder_weights.shape, decoder_weights.shape, norm_params.shape)
+    small = jnp.concatenate(
+        [encoder_grad.reshape(-1), decoder_grad.reshape(-1), jnp.stack(param_list).reshape(-1)]
+    )
+    chunk = -(-small.shape[0] // (2 * OWNER_CHIPS * width * 8)) * 8
+    padded = jnp.pad(small, (0, 2 * OWNER_CHIPS * chunk * width - small.shape[0]))
+    padded = padded.reshape(OWNER_CHIPS, 2, chunk, width).swapaxes(0, 1)
+    total, ortho, small = tail(
+        lax.axis_size("band"),
+        lax.axis_size("row"),
+        spread_slots(row_grads, rows_dev, width),
+        padded,
+        processor_momentum.reshape(layers * blocks, rows_dev, width),
+    )
+    small = small.reshape(-1)
+    parts = []
+    start = 0
+    for shape in small_shapes:
+        size = shape[0] * shape[1] * (shape[2] if len(shape) > 2 else 1)
+        parts.append(small[start : start + size].reshape(shape))
+        start += size
+    encoder_grad, decoder_grad, param_grad = parts
+    next_momentum = momentum_decay * processor_momentum + total.reshape(processor_weights.shape)
+    next_weights = muon_finish(processor_weights, ortho.reshape(processor_weights.shape))
     next_average = average_decay * processor_average + (1.0 - average_decay) * next_weights
     param_moment, param_square, param_values = adam_update(
         norm_params, norm_first, norm_second, param_grad, param_rate

time: 2330 us -> 1340 us (0.58)
  waiting for transfers between devices: 1360 us -> 452 us
  matrix products: 514 us -> 346 us
  Pallas kernels: 0 us -> 137 us
  blocking collectives: 52.3 us -> 13.9 us
  other arithmetic: 238 us -> 201 us
    psum x3 -> x0, waiting for transfers between devices: 918 us -> none  [the longest x2 812 us: gram_total(): return lax.psum(value, 'row')]
    dot_general x6 -> x0, matrix products: 166 us -> none  [the longest x2 75.6 us: orthogonalize(): jnp.einsum('lgde,lgef->lgdf', gram, gram, precision=highest)]
    pallas_call x0 -> x1, Pallas kernels: none -> 137 us  [tail(): pl.pallas_call(functools.partial(tail_kernel, bands, rows), out_shape=(ja...]
    another operation x10 -> x3, other arithmetic: 39.8 us -> 0.08 us  [body(): jnp.stack(param_list).reshape(-1)]
    unnamed x363 -> x358, local copies, waits for them, and re-layouts: 15.9 us -> 50.5 us
    gather x3 -> x0, local copies, waits for them, and re-layouts: 30.5 us -> none  [spread(): return jnp.take(values, jnp.array(block_group, dtype=jnp.int32), axis=1)]
    psum x2 -> x1, blocking collectives: 40.6 us -> 13.9 us  [body(): lax.psum((local_loss, jnp.sum(loss_mask.astype(jnp.float32))), 'band')]
  transfers between devices with their start and end apart: 12 -> 9, of which waited for: 9 -> 8; matrix products, arithmetic and copies ran while one was open for 8% -> 14% of each run, Pallas kernels for 0% -> 0%
where the time goes in v1:
time: 1340 us; the launch traced here: 1330 us
  waiting for transfers between devices  452 us (34%)
  matrix products  346 us (26%)
  other arithmetic  201 us (15%)
  local copies, waits for them, and re-layouts  157 us (12%)
  Pallas kernels  137 us (10%)
  between operations  17.7 us (1%)
  blocking collectives  13.9 us (1%)
    all_gather x1, waiting for transfers between devices, body(): full_weights = lax.all_gather(processor_weights, 'row', axis=2, tiled=True)  370 us
    dot_general x70, matrix products, matmul(): return jnp.dot(left, right, precision=highest)  346 us
    pallas_call x1, Pallas kernels, tail(): pl.pallas_call(functools.partial(tail_kernel, bands, rows), out_shape=(ja...  137 us
    all_gather x4, waiting for transfers between devices, share_border(): return lax.all_gather(node_lat[border_nodes], 'band', axis=0, tiled=True)  54.2 us
    unnamed x358, local copies, waits for them, and re-layouts  50.5 us
    scatter-add x3, other arithmetic, layer_local(): combined[senders]  35.7 us
    scatter-add x3, other arithmetic, processor(): jax.ops.segment_sum(edge_lat, recv_index, num_segments=node_lat.shape[0])  33.1 us
    scatter-add x3, other arithmetic, processor(): recv_lat = node_lat[recv_index]  32.2 us
  transfers between devices with their start and end apart: 9, of which 8 were waited for; matrix products, arithmetic and copies ran while one was open for 14% of the time, Pallas kernels for 0%

profile of v1, /device:TPU:0, one launch (start us, length us, event | category | flops | bytes accessed | tf_op | source)
XLA Modules:
  0.0 1325.6 jit_solution(7140885671957436979)
XLA Ops:
  11.2 7.4 scatter_custom_fusion
  31.1 16.0 %all-gather.12.cloned.1.call-done = f32[512,512]{1,0:T(8,128)} async-done(((f32[64,512]{1,0:T(8,128)}), f32[512,512]{1,0:T(8,128)}) %all-gather.12.cloned.1.call-update) | async-done | bytes 1048592 | tf_op jit(solution)/shard_map/all_gather | solution.py:589
  53.1 369.6 %all-gather.10.cloned.1.call-done = f32[3,7,512,512]{3,2,1,0:T(8,128)} async-done(((f32[3,7,128,512]{3,2,1,0:T(8,128)}), f32[3,7,512,512]{3,2,1,0:T(8,128)}) %all-gather.10.cloned.1.call-update) | async-done | bytes 22020112 | tf_op jit(solution)/shard_map/all_gather | solution.py:586
  422.7 6.9 fusion.91
  441.3 7.4 fusion.223
  452.7 10.6 scatter_custom_fusion.1
  481.6 7.0 fusion.97
  488.6 7.2 all-gather.14.cloned.1.call-done
  501.9 7.6 convolution_add_fusion.8
  515.4 7.0 fusion.225
  525.7 10.5 scatter_custom_fusion.2
  552.1 7.8 fusion.103
  559.9 8.1 all-gather.16.cloned.1.call-done
  574.0 7.6 convolution_add_fusion.5
  587.4 7.0 fusion.227
  596.6 12.0 scatter_custom_fusion.3
  617.5 22.9 %all-gather.18.cloned.1.call-done = f32[512,512]{1,0:T(8,128)} async-done(((f32[64,512]{1,0:T(8,128)}), f32[512,512]{1,0:T(8,128)}) %all-gather.18.cloned.1.call-update) | async-done | bytes 1048592 | tf_op jit(solution)/shard_map/all_gather | solution.py:589
  641.9 9.1 gather_fusion.10
  651.0 9.6 reshape.545
  660.6 7.9 reduce_sum.505
  668.5 6.2 fusion.112
  674.7 13.9 %all-reduce.48 = (f32[]{:T(128)}, f32[]{:T(128)}) all-reduce(f32[]{:T(128)} %get-tuple-element.138, f32[]{:T(128)} %convert_reduce_fusion), channel_id=1, replica_groups=mesh['band'=8,'row'=4] {'band'}, use_global_device_ids=true, to_apply=%region_20.0 | all-reduce | flops 2 | bytes 16 | tf_op jit(solution)/shard_map/psum | solution.py:616
  700.5 9.8 reshape.738
  710.3 19.7 %scatter_custom_fusion.4 = f32[832,512]{1,0:T(8,128)S(1)} fusion(s32[2880]{0:T(1024)} %copy-done.121, f32[2880,512]{1,0:T(8,128)} %reshape.738, f32[]{:T(128)} %constant.58.clone.1), kind=kCustom, calls=%fused_computation.246 | custom fusion | flops 1474560 | bytes 1704448 | tf_op jit(solution)/shard_map/transpose(jvp())/scatter-add | solution.py:604
  747.2 20.1 %reduce-scatter.5.cloned.1.call-done = f32[64,512]{1,0:T(8,128)} async-done(((f32[512,512]{1,0:T(8,128)}), f32[64,512]{1,0:T(8,128)}) %reduce-scatter.5.cloned.1.call-update) | async-done | bytes 131088 | tf_op jit(solution)/shard_map/reduce_scatter | solution.py:592
  797.2 6.8 fusion.229
  820.7 7.0 fusion.104
  827.7 12.0 scatter_custom_fusion.6
  842.0 7.1 fusion.105
  851.9 10.7 scatter_fusion.1
  862.8 7.8 fusion.57
  899.4 9.2 multiply_reduce_fusion.1
  913.2 6.8 fusion.231
  936.6 7.1 fusion.98
  943.7 11.9 scatter_custom_fusion.9
  958.0 7.2 fusion.99
  967.9 10.7 scatter_fusion.2
  978.8 7.8 fusion.60
  1017.6 9.1 multiply_reduce_fusion.2
  1035.5 6.8 fusion.233
  1060.2 7.0 fusion.92
  1067.2 11.9 scatter_custom_fusion.12
  1101.9 7.1 fusion.93
  1111.8 10.7 scatter_fusion.3
  1128.4 6.8 convolution_add_fusion
  1151.0 137.4 %tail.1 = (f32[21,128,512]{2,1,0:T(8,128)}, f32[21,128,512]{2,1,0:T(8,128)}, f32[8,64,512]{2,1,0:T(8,128)}) custom-call(f32[2,4,3,128,512]{4,3,2,1,0:T(8,128)} %bitcast.298, f32[2,4,64,512]{3,2,1,0:T(8,128)} %bitcast.301, f32[21,128,512]{2,1,0:T(8,128)} %bitcast.295), custom_call_target="tpu_custom_call" | custom-call | tf_op jit(solution)/shard_map/tail/pallas_call | solution.py:501
  1290.0 6.6 multiply_add_fusion.1
  1305.6 13.1 multiply_add_fusion
  (556 shorter events, 360.3 us)
Async XLA Ops:
  7.2 19.4 %copy-start = (f32[1280,4]{0,1:T(4,128)S(1)}, f32[1280,4]{0,1:T(4,128)}, u32[]{:S(2)}) copy-start(f32[1280,4]{0,1:T(4,128)} %param.24) | copy-start | bytes 61444
  7.2 39.9 %all-gather.12.cloned.1.call-start = ((), (), s32[]{:S(2)}) async-start(), calls=%async_computation.9 | async-start | bytes 1179648 | tf_op jit(solution)/shard_map/all_gather | solution.py:589
  18.8 452.8 %copy-start.115 = (f32[320]{0:T(512)}, f32[320]{0:T(512)S(1)}, u32[]{:S(2)}) copy-start(f32[320]{0:T(512)S(1)} %broadcast_multiply_fusion.6) | copy-start | bytes 3844
  19.1 452.5 %copy-start.137 = (f32[320]{0:T(512)}, f32[320]{0:T(512)S(1)}, u32[]{:S(2)}) copy-start(f32[320]{0:T(512)S(1)} %fusion.186) | copy-start | bytes 3844
  19.3 444.0 %copy-start.1 = (f32[320,512]{1,0:T(8,128)}, f32[320,512]{1,0:T(8,128)S(1)}, u32[]{:S(2)}) copy-start(f32[320,512]{1,0:T(8,128)S(1)} %subtract_multiply_fusion.9) | copy-start | bytes 1966084
  20.6 402.1 %all-gather.10.cloned.1.call-start = ((), (), s32[]{:S(2)}) async-start(), calls=%async_computation.4 | async-start | bytes 27525120 | tf_op jit(solution)/shard_map/all_gather | solution.py:586
  21.4 474.5 %all-gather.14.cloned.1.call-start = ((), (), s32[]{:S(2)}) async-start(), calls=%async_computation.10 | async-start | bytes 1179648 | tf_op jit(solution)/shard_map/all_gather | solution.py:589
  26.5 422.8 %copy-start.126 = (f32[1,1,512]{2,1,0:T(1,128)}, f32[1,1,512]{2,1,0:T(1,128)S(1)}, u32[]{:S(2)}) copy-start(f32[1,1,512]{2,1,0:T(1,128)S(1)} %get-tuple-element.123) | copy-start | bytes 6148
  26.6 445.1 %copy-start.131 = (f32[1,1,512]{2,1,0:T(1,128)}, f32[1,1,512]{2,1,0:T(1,128)S(1)}, u32[]{:S(2)}) copy-start(f32[1,1,512]{2,1,0:T(1,128)S(1)} %get-tuple-element.118) | copy-start | bytes 6148
  26.6 496.9 %copy-start.128 = (f32[1,1,512]{2,1,0:T(1,128)}, f32[1,1,512]{2,1,0:T(1,128)S(1)}, u32[]{:S(2)}) copy-start(f32[1,1,512]{2,1,0:T(1,128)S(1)} %get-tuple-element.114) | copy-start | bytes 6148
  26.6 515.7 %copy-start.133 = (f32[1,1,512]{2,1,0:T(1,128)}, f32[1,1,512]{2,1,0:T(1,128)S(1)}, u32[]{:S(2)}) copy-start(f32[1,1,512]{2,1,0:T(1,128)S(1)} %get-tuple-element.110) | copy-start | bytes 6148
  26.6 570.0 %copy-start.124 = (f32[1,1,512]{2,1,0:T(1,128)}, f32[1,1,512]{2,1,0:T(1,128)S(1)}, u32[]{:S(2)}) copy-start(f32[1,1,512]{2,1,0:T(1,128)S(1)} %get-tuple-element.106) | copy-start | bytes 6148
  26.6 588.0 %copy-start.135 = (f32[1,1,512]{2,1,0:T(1,128)}, f32[1,1,512]{2,1,0:T(1,128)S(1)}, u32[]{:S(2)}) copy-start(f32[1,1,512]{2,1,0:T(1,128)S(1)} %get-tuple-element.102) | copy-start | bytes 6148
  53.1 376.4 %copy-start.28 = (f32[1280,512]{1,0:T(8,128)S(1)}, f32[1280,512]{1,0:T(8,128)}, u32[]{:S(2)}) copy-start(f32[1280,512]{1,0:T(8,128)} %gather_fusion.1) | copy-start | bytes 7864324
  452.7 29.0 %copy-start.7 = (f32[1280,512]{1,0:T(8,128)}, f32[1280,512]{1,0:T(8,128)S(1)}, u32[]{:S(2)}) copy-start(f32[1280,512]{1,0:T(8,128)S(1)} %add_add_fusion.4) | copy-start | bytes 7864324
  473.8 94.2 %all-gather.16.cloned.1.call-start = ((), (), s32[]{:S(2)}) async-start(), calls=%async_computation.11 | async-start | bytes 1179648 | tf_op jit(solution)/shard_map/all_gather | solution.py:589
  525.7 16.3 %copy-start.14 = (f32[1280,512]{1,0:T(8,128)}, f32[1280,512]{1,0:T(8,128)S(1)}, u32[]{:S(2)}) copy-start(f32[1280,512]{1,0:T(8,128)S(1)} %add_add_fusion.3) | copy-start | bytes 7864324
  544.3 96.0 %all-gather.18.cloned.1.call-start = ((), (), s32[]{:S(2)}) async-start(), calls=%async_computation.12 | async-start | bytes 1179648 | tf_op jit(solution)/shard_map/all_gather | solution.py:589
  596.6 12.0 copy-start.83
  614.6 27.3 %copy-start.151 = (f32[320]{0:T(512)}, f32[320]{0:T(512)S(1)}, u32[]{:S(2)}) copy-start(f32[320]{0:T(512)S(1)} %multiply_reduce_fusion.16) | copy-start | bytes 3844
  614.6 27.3 %copy-start.143 = (f32[320]{0:T(512)}, f32[320]{0:T(512)S(1)}, u32[]{:S(2)}) copy-start(f32[320]{0:T(512)S(1)} %fusion.189) | copy-start | bytes 3844
  616.7 150.6 %reduce-scatter.5.cloned.1.call-start = ((), (), s32[]{:S(2)}) async-start(), calls=%async_computation.5 | async-start | bytes 1179648 | tf_op jit(solution)/shard_map/reduce_scatter | solution.py:592
  616.8 72.5 %copy-start.157 = (f32[960]{0:T(1024)}, f32[960]{0:T(1024)S(1)}, u32[]{:S(2)}) copy-start(f32[960]{0:T(1024)S(1)} %convert_element_type.6) | copy-start | bytes 11524
  617.4 33.6 %copy-start.121 = (s32[2880]{0:T(1024)}, s32[2880]{0:T(1024)S(1)}, u32[]{:S(2)}) copy-start(s32[2880]{0:T(1024)S(1)} %compare_select_fusion) | copy-start | bytes 34564
  668.5 20.8 %copy-start.88 = (f32[960,512]{1,0:T(8,128)}, f32[960,512]{1,0:T(8,128)S(1)}, u32[]{:S(2)}) copy-start(f32[960,512]{1,0:T(8,128)S(1)} %reduce_sum.505) | copy-start | bytes 5898244
  710.3 20.9 %copy-start.101 = (f32[512,227]{0,1:T(8,128)S(1)}, f32[512,227]{0,1:T(8,128)}, u32[]{:S(2)}) copy-start(f32[512,227]{0,1:T(8,128)} %param.40) | copy-start | bytes 1394692
  730.0 10.2 copy-start.32
  731.1 147.0 %reduce-scatter.7.cloned.1.call-start = ((), (), s32[]{:S(2)}) async-start(), calls=%async_computation.6 | async-start | bytes 1179648 | tf_op jit(solution)/shard_map/reduce_scatter | solution.py:592
  740.2 27.1 %slice-start.2 = ((f32[832,512]{1,0:T(8,128)}), f32[320,512]{1,0:T(8,128)S(1)}, s32[]{:S(2)}) async-start(f32[832,512]{1,0:T(8,128)} %copy-done.32), calls=%async_computation.15 | async-start | bytes 1310720 | tf_op jit(solution)/shard_map/transpose(jvp())/split | solution.py:603
  740.2 27.1 %copy-start.161 = (s32[64]{0:T(128)S(1)}, s32[64]{0:T(128)}, u32[]{:S(2)}) copy-start(s32[64]{0:T(128)} %param.27) | copy-start | bytes 772
  745.9 23.5 %copy-start.51 = (f32[320,512]{1,0:T(8,128)S(1)}, f32[320,512]{1,0:T(8,128)}, u32[]{:S(2)}) copy-start(f32[320,512]{1,0:T(8,128)} %copy-done.50) | copy-start | bytes 1966084
  745.9 23.5 %copy-start.120 = (f32[320]{0:T(512)S(1)}, f32[320]{0:T(512)}, u32[]{:S(2)}) copy-start(f32[320]{0:T(512)} %copy-done.119) | copy-start | bytes 3844
  745.9 23.5 %copy-start.136 = (f32[1,1,512]{2,1,0:T(1,128)S(1)}, f32[1,1,512]{2,1,0:T(1,128)}, u32[]{:S(2)}) copy-start(f32[1,1,512]{2,1,0:T(1,128)} %copy-done.135) | copy-start | bytes 6148
  745.9 23.5 %copy-start.144 = (f32[320]{0:T(512)S(1)}, f32[320]{0:T(512)}, u32[]{:S(2)}) copy-start(f32[320]{0:T(512)} %copy-done.143) | copy-start | bytes 3844
  745.9 23.8 %copy-start.152 = (f32[320]{0:T(512)S(1)}, f32[320]{0:T(512)}, u32[]{:S(2)}) copy-start(f32[320]{0:T(512)} %copy-done.151) | copy-start | bytes 3844
  747.2 23.0 %copy-start.98 = (f32[320,512]{1,0:T(8,128)S(1)}, f32[320,512]{1,0:T(8,128)}, u32[]{:S(2)}) copy-start(f32[320,512]{1,0:T(8,128)} %copy-done.97) | copy-start | bytes 1966084
  794.5 9.5 copy-start.41
  804.0 38.0 %copy-start.3 = (f32[1280,512]{1,0:T(8,128)}, f32[1280,512]{1,0:T(8,128)S(1)}, u32[]{:S(2)}) copy-start(f32[1280,512]{1,0:T(8,128)S(1)} %get-tuple-element.143) | copy-start | bytes 7864324
  842.0 152.1 %reduce-scatter.9.cloned.1.call-start = ((), (), s32[]{:S(2)}) async-start(), calls=%async_computation.7 | async-start | bytes 1179648 | tf_op jit(solution)/shard_map/reduce_scatter | solution.py:592
  899.3 9.3 copy-start.113
  899.4 9.3 copy-start.11
  910.5 9.5 copy-start.45
  957.9 179.8 %reduce-scatter.11.cloned.1.call-start = ((), (), s32[]{:S(2)}) async-start(), calls=%async_computation.8 | async-start | bytes 1179648 | tf_op jit(solution)/shard_map/reduce_scatter | solution.py:592
  987.4 8.9 copy-start.118
  1017.5 9.2 copy-start.111
  1017.6 9.2 copy-start.6
  1150.9 139.0 %slice-start = ((s8[5505024]{0:T(1024)(128)(4,1)}), s8[4194304]{0:T(1024)(128)(4,1)S(1)}, s32[]{:S(2)}) async-start(s8[5505024]{0:T(1024)(128)(4,1)} %bitcast.296), calls=%async_computation.13 | async-start | bytes 8388608
  1151.0 139.0 %slice-start.1 = ((s8[5505024]{0:T(1024)(128)(4,1)}), s8[1310720]{0:T(1024)(128)(4,1)S(1)}, s32[]{:S(2)}) async-start(s8[5505024]{0:T(1024)(128)(4,1)} %bitcast.296), calls=%async_computation.14 | async-start | bytes 2621440
  (126 other events, 606.2 us)
Sparse Core Ops, SparseCore 0:
  20.7 26.3 all-gather.11
  48.7 373.9 all-gather.9
  473.9 21.9 all-gather.13
  544.4 23.4 all-gather.15
  616.8 23.4 all-gather.17
  731.2 36.0 reduce-scatter.4
  842.1 35.9 reduce-scatter.6
  958.0 36.0 reduce-scatter.8
  1081.6 36.0 reduce-scatter.10

commit v2 on v1

--- a/solution.py
+++ b/solution.py
@@ -7,12 +7,10 @@
 from jax.experimental.pallas import tpu as pltpu
 from jax.sharding import PartitionSpec as P
 
-LAYERS = 3
 STEP = 10
 NODE_DEV = 320
 
 
-highest = lax.Precision.HIGHEST
 coef_a = 3.4445
 coef_b = -4.775
 coef_c = 2.0315
@@ -28,57 +26,13 @@
 block_scale = (3.0**0.5, 3.0**0.5, 3.0**0.5, 1.0, 2.0**0.5, 2.0**0.5, 1.0)
 
 
-def matmul(left, right):
-    return jnp.dot(left, right, precision=highest)
-
-
-def silu(value):
-    return value * jax.nn.sigmoid(value)
-
-
-def layer_norm(value):
-    centered = value - jnp.mean(value, axis=-1, keepdims=True)
-    return centered * lax.rsqrt(jnp.mean(centered * centered, axis=-1, keepdims=True) + 1e-05)
-
-
-def encode(grid_input, edge_input, mesh_index, encoder_weights, node_count):
-    channels = grid_input.shape[1]
-    embedded = silu(matmul(grid_input, encoder_weights[:channels]))
-    node_lat = layer_norm(jax.ops.segment_sum(embedded, mesh_index, num_segments=node_count))
-    edge_lat = silu(matmul(edge_input, encoder_weights[channels:]))
-    return (node_lat, edge_lat)
-
-
-def processor(node_lat, edge_lat, send_lat, recv_index, weights, params):
-    recv_lat = node_lat[recv_index]
-    before = (
-        matmul(edge_lat, weights[0])
-        + matmul(send_lat, weights[1])
-        + matmul(recv_lat, weights[2])
-        + params[0]
-    )
-    message = matmul(silu(before), weights[3]) + params[1]
-    edge_lat = edge_lat + layer_norm(message) * (1.0 + params[2]) + params[3]
-    summed = jax.ops.segment_sum(edge_lat, recv_index, num_segments=node_lat.shape[0])
-    before = matmul(node_lat, weights[4]) + matmul(summed, weights[5]) + params[4]
-    update = matmul(silu(before), weights[6]) + params[5]
-    node_lat = node_lat + layer_norm(update) * (1.0 + params[6]) + params[7]
-    return (node_lat, edge_lat)
-
-
-def decode(read_lat, grid_input, grid_target, loss_mask, decoder_weights):
-    gathered = jnp.sum(read_lat.reshape(-1, 3, read_lat.shape[1]), axis=1)
-    predicted = grid_input + matmul(silu(gathered), decoder_weights)
-    missed = predicted - grid_target
-    return jnp.sum(loss_mask.astype(jnp.float32)[:, None] * missed * missed)
-
-
 MESH = pl.DeviceIdType.MESH
 NN = (((1,), (0,)), ((), ()))
 NT = (((1,), (1,)), ((), ()))
 TN = (((0,), (0,)), ((), ()))
 OWNER_CHIPS = 4
 SLOTS = 3
+VMEM_BYTES = 62 * 2**20
 ANY = pl.BlockSpec(memory_space=pl.ANY)
 VMEM = pl.BlockSpec(memory_space=pltpu.VMEM)
 
@@ -112,17 +66,6 @@
 
 def slot_used(owner, slot):
     return owner < (8, 7, 6)[slot]
-
-
-def spread_slots(blocks, rows_dev, width):
-    empty = jnp.zeros((rows_dev, width), jnp.float32)
-    order = []
-    for core in range(2):
-        for chip in range(OWNER_CHIPS):
-            owner = 2 * chip + core
-            for slot in range(SLOTS):
-                order.append(blocks[slot_block(owner, slot)] if slot_used(owner, slot) else empty)
-    return jnp.stack(order).reshape(2, OWNER_CHIPS, SLOTS, rows_dev, width)
 
 
 def remote(src, dst, send_sem, recv_sem, device):
@@ -134,6 +77,853 @@
         device_id=device,
         device_id_type=MESH,
     )
+
+
+def silu(value):
+    return value / (1.0 + jnp.exp(-value))
+
+
+def silu_back(value):
+    gate = 1.0 / (1.0 + jnp.exp(-value))
+    return gate * (1.0 + value * (1.0 - gate))
+
+
+def normed(value):
+    centered = value - jnp.mean(value, axis=-1, keepdims=True)
+    scale = lax.rsqrt(jnp.mean(centered * centered, axis=-1, keepdims=True) + 1e-05)
+    return centered * scale, scale
+
+
+def normed_back(grad, norm, scale):
+    inner = jnp.mean(grad * norm, axis=-1, keepdims=True)
+    return (grad - jnp.mean(grad, axis=-1, keepdims=True) - norm * inner) * scale
+
+
+def column(value):
+    return jnp.sum(value, axis=0, keepdims=True)
+
+
+def hot(mask):
+    return jnp.where(mask, 1.0, 0.0).astype(jnp.bfloat16)
+
+
+def chosen(choice, high, low, dims=NN):
+    return dot(choice, high, dims) + dot(choice, low, dims)
+
+
+def picked(choice, value):
+    high, low = pieces(value)
+    return chosen(choice, high, low)
+
+
+def fill_rows(out_ref, make, tile=128):
+    def step(t, carry):
+        at = pl.multiple_of(t * tile, tile)
+        out_ref[pl.ds(at, tile)] = make(at, tile)
+        return carry
+
+    lax.fori_loop(0, out_ref.shape[0] // tile, step, 0)
+
+
+def iota(shape, axis):
+    return lax.broadcasted_iota(jnp.int32, shape, axis)
+
+
+class Weights:
+    def __init__(self, full_ref, stage, high, low, sem):
+        self.full, self.stage, self.high, self.low, self.sem = full_ref, stage, high, low, sem
+
+    def copy(self, block, slot):
+        return pltpu.make_async_copy(self.full.at[block], self.stage.at[slot], self.sem.at[slot])
+
+    def load(self, first, blocks):
+        for n, block in enumerate(blocks[:2]):
+            self.copy(first + block, n % 2).start()
+        for n, block in enumerate(blocks):
+            self.copy(first + block, n % 2).wait()
+            high, low = pieces(self.stage[n % 2])
+            self.high[block] = high
+            self.low[block] = low
+            if n + 2 < len(blocks):
+                self.copy(first + blocks[n + 2], n % 2).start()
+
+    def times(self, high, low, block, dims=NN):
+        weight = self.high[block]
+        return dot(high, weight, dims) + dot(low, weight, dims) + dot(high, self.low[block], dims)
+
+    def apply(self, value, block, dims=NN):
+        high, low = pieces(value)
+        return self.times(high, low, block, dims)
+
+
+def place(bands, rows):
+    band = lax.axis_index("band")
+    row = lax.axis_index("row")
+    return band, row, band // 2, band % 2
+
+
+def meet(partners):
+    barrier = pltpu.get_barrier_semaphore()
+    for partner in partners:
+        pl.semaphore_signal(barrier, inc=1, device_id=partner, device_id_type=MESH)
+    pl.semaphore_wait(barrier, len(partners))
+
+
+def forward_kernel(
+    bands,
+    rows,
+    chunks,
+    tile,
+    grid_ref,
+    edge_ref,
+    send_ref,
+    recv_ref,
+    recv_row_ref,
+    border_ref,
+    feed_ref,
+    mask_ref,
+    w_ref,
+    enc_ref,
+    enc_edge_ref,
+    param_ref,
+    full_ref,
+    before_ref,
+    message_ref,
+    edges_ref,
+    embed_ref,
+    nodes_ref,
+    fed_ref,
+    agg_ref,
+    inner_ref,
+    update_ref,
+    table_ref,
+    count_ref,
+    edge_buf,
+    before_buf,
+    message_buf,
+    pick,
+    gather_t,
+    src_high,
+    src_low,
+    high,
+    low,
+    stage,
+    table,
+    border_buf,
+    count_buf,
+    stage_sem,
+    save_sem,
+    own_sem,
+    z_send,
+    z_recv,
+    a_send,
+    a_recv,
+    b_send,
+    b_recv,
+    s_send,
+    s_recv,
+    x_send,
+    x_recv,
+    p_send,
+    p_recv,
+):
+    band, row, chip, core = place(bands, rows)
+    chips = bands // 2
+    layers, blocks = agg_ref.shape[0], w_ref.shape[0] // agg_ref.shape[0]
+    rows_dev = w_ref.shape[1]
+    nodes, width = fed_ref.shape
+    edges = edge_buf.shape[1]
+    border = border_ref.shape[0]
+    weights = Weights(full_ref, stage, high, low, stage_sem)
+    quad, pos = chip // 4, chip % 4
+    pos_x, pos_y = pos + 1 - 2 * (pos % 2), pos + 2 - 4 * (pos // 2)
+    sibling = (chip * 2 + 1 - core, row)
+    near = (((quad * 4 + pos_x) * 2 + core, row), ((quad * 4 + pos_y) * 2 + core, row))
+    near_pos = (pos_x, pos_y)
+    partners = [((chip + j) % chips * 2 + core, row) for j in range(1, chips)] + [sibling]
+    partners += [(band, (row + j) % rows) for j in range(1, rows)]
+    meet(partners)
+
+    piece = rows_dev // 8
+
+    def part(g, from_row, of_core, of_pos, first=0, size=None):
+        start, count = chunks[g]
+        size = piece if size is None else size
+        at = from_row * rows_dev + (of_core * 4 + of_pos) * piece + first
+        return full_ref.at[pl.ds(start, count), pl.ds(pl.multiple_of(at, 8), size)]
+
+    def z_copy(g, j, from_row):
+        start, count = chunks[g]
+        at = pl.multiple_of((core * 4 + pos) * piece, 8)
+        return remote(
+            w_ref.at[pl.ds(start, count), pl.ds(at, piece)],
+            part(g, from_row, core, pos),
+            z_send.at[g, j - 1],
+            z_recv.at[g, j - 1],
+            (band, (from_row + j) % rows),
+        )
+
+    def a_copy(g, side, j, of_pos):
+        region = part(g, (row - j + rows) % rows, core, of_pos)
+        return remote(region, region, a_send.at[g, side, j - 1], a_recv.at[g, side, j - 1], near[side])
+
+    def b_copy(g, side, j, of_pos):
+        half = piece // 2
+        region = part(g, (row - j + rows) % rows, core, of_pos, side * half, half)
+        return remote(region, region, b_send.at[g, side, j - 1], b_recv.at[g, side, j - 1], near[side])
+
+    def s_copy(g, j, of_core):
+        region = part(g, (row - j + rows) % rows, of_core, 0, 0, 4 * piece)
+        return remote(region, region, s_send.at[g, j - 1], s_recv.at[g, j - 1], sibling)
+
+    others = range(1, rows)
+    far = 3 - pos
+
+    def start_z(g):
+        for j in others:
+            z_copy(g, j, row).start()
+
+    def start_a(g):
+        for j in others:
+            z_copy(g, j, (row - j + rows) % rows).wait_recv()
+            for side in range(2):
+                a_copy(g, side, j, pos).start()
+
+    def start_b(g):
+        for j in others:
+            for side in range(2):
+                a_copy(g, side, j, near_pos[side]).wait_recv()
+                b_copy(g, 1 - side, j, near_pos[side]).start()
+
+    def start_s(g):
+        for j in others:
+            for side in range(2):
+                b_copy(g, side, j, far).wait_recv()
+            s_copy(g, j, core).start()
+
+    def ready(g):
+        for j in others:
+            s_copy(g, j, 1 - core).wait_recv()
+
+    def tick(t):
+        for g, stage_of in ((t - 4, ready), (t - 3, start_s), (t - 2, start_b), (t - 1, start_a), (t + 1, start_z)):
+            if 0 <= g < len(chunks):
+                stage_of(g)
+
+    own = pltpu.make_async_copy(
+        w_ref,
+        full_ref.at[:, pl.ds(pl.multiple_of(row * rows_dev, rows_dev), rows_dev)],
+        own_sem,
+    )
+    start_z(0)
+    start_z(1)
+    own.start()
+
+    def table_of(e):
+        return table_ref if (layers - e) % 2 == 0 else table
+
+    def items(e):
+        par = e % 2
+        found = [(0, border_buf.at[par], lambda k, c: table_of(e).at[k, c])]
+        if e == 0:
+            found.append((1, count_buf, lambda k, c: count_ref.at[k, c]))
+        return found
+
+    def out(e, item, src, dst, j):
+        return remote(
+            src,
+            dst(core, chip),
+            x_send.at[e + item * 4, j - 1],
+            x_recv.at[e + item * 4, j - 1],
+            ((chip + j) % chips * 2 + core, row),
+        )
+
+    def across(e, item, src, dst, j, of_core):
+        origin = (chip - j + chips) % chips
+        return remote(
+            src if j == 0 else dst(of_core, origin),
+            dst(of_core, origin),
+            p_send.at[e + item * 4, j],
+            p_recv.at[e + item * 4, j],
+            sibling,
+        )
+
+    def share(e, value):
+        par = e % 2
+        choice = hot(iota((border, nodes), 1) == border_ref[...])
+        rows_out = picked(choice, value)
+        border_buf[par] = rows_out
+        table_of(e)[core, chip] = rows_out
+        for item, src, dst in items(e):
+            for j in range(1, chips):
+                out(e, item, src, dst, j).start()
+            across(e, item, src, dst, 0, core).start()
+
+    def relay(e):
+        for item, src, dst in items(e):
+            for j in range(1, chips):
+                out(e, item, src, dst, j).wait_recv()
+                across(e, item, src, dst, j, core).start()
+
+    def gathered(e):
+        for item, src, dst in items(e):
+            for j in range(chips):
+                across(e, item, src, dst, j, 1 - core).wait_recv()
+            for j in range(chips):
+                across(e, item, src, dst, j, core).wait_send()
+            for j in range(1, chips):
+                out(e, item, src, dst, j).wait_send()
+
+    def put_src(at, value):
+        value_high, value_low = pieces(value)
+        size = value.shape[0]
+        src_high[pl.ds(at, size)] = value_high
+        src_low[pl.ds(at, size)] = value_low
+
+    def save(kind, layer, src):
+        dst = (before_ref, message_ref, edges_ref, embed_ref)[kind]
+        return pltpu.make_async_copy(src, dst if layer is None else dst.at[layer], save_sem.at[kind])
+
+    embed_buf = before_buf.at[pl.ds(0, grid_ref.shape[0])]
+    embed_buf[...] = product(grid_ref[...], enc_ref[...])
+    save(3, None, embed_buf).start()
+    feed = hot(iota((nodes, grid_ref.shape[0]), 0) == feed_ref[...])
+    fed = picked(feed, silu(embed_buf[...]))
+    fed_ref[...] = fed
+    nodes_ref[0] = normed(fed)[0]
+    count = jnp.sum(mask_ref[...].astype(jnp.float32), axis=1, keepdims=True)
+    counts = jnp.broadcast_to(count, count_buf.shape)
+    count_buf[...] = counts
+    count_ref[core, chip] = counts
+    fill_rows(
+        edge_buf.at[0], lambda at, size: silu(product(edge_ref[pl.ds(at, size)], enc_edge_ref[...])), 256
+    )
+    tick(1)
+    table_rows = 2 * chips * border
+    inputs = src_high.shape[0]
+
+    def choose(at, size):
+        columns = iota((size, inputs), 1)
+        sent = columns == send_ref[pl.ds(at, size)]
+        received = columns == recv_ref[pl.ds(at, size)] + (nodes + table_rows)
+        return hot(jnp.logical_or(sent, received))
+
+    fill_rows(pick, choose)
+
+    def choose_receiver(at, size):
+        return hot(iota((size, edges), 0) + at == recv_row_ref[...])
+
+    fill_rows(gather_t, choose_receiver, 64)
+    tick(2)
+    tick(3)
+    own.wait()
+    for layer in range(layers):
+        first = layer * blocks
+        now, later = layer % 2, (layer + 1) % 2
+        tick(4 + 2 * layer)
+        weights.load(first, (1, 2, 0))
+        node = nodes_ref[layer]
+        node_high, node_low = pieces(node)
+        sender = weights.times(node_high, node_low, 1)
+        share(layer, sender)
+        put_src(0, sender)
+        put_src(nodes + table_rows, weights.times(node_high, node_low, 2))
+        if layer > 0:
+            save(0, layer - 1, before_buf).wait()
+            save(1, layer - 1, message_buf).wait()
+            save(2, layer - 1, edge_buf.at[later]).wait()
+        else:
+            save(3, None, embed_buf).wait()
+        save(2, layer, edge_buf.at[now]).start()
+        tick(5 + 2 * layer)
+        relay(layer)
+        weights.load(first, (3, 4, 5, 6))
+        inner = weights.times(node_high, node_low, 4) + param_ref[layer, pl.ds(4, 1)]
+        gathered(layer)
+        table_now = table_of(layer)
+        for side in range(2):
+            for at in range(chips):
+                put_src(nodes + (side * chips + at) * border, table_now[side, at])
+        agg_ref[layer] = jnp.zeros((nodes, width), jnp.float32)
+
+        def edge_tile(t, carry):
+            at = pl.ds(pl.multiple_of(t * tile, tile), tile)
+            edge = edge_buf[now, at]
+            before = (
+                weights.apply(edge, 0)
+                + chosen(pick[at], src_high[...], src_low[...])
+                + param_ref[layer, pl.ds(0, 1)]
+            )
+            before_buf[at] = before
+            message = weights.apply(silu(before), 3) + param_ref[layer, pl.ds(1, 1)]
+            message_buf[at] = message
+            edge = (
+                edge
+                + normed(message)[0] * (1.0 + param_ref[layer, pl.ds(2, 1)])
+                + param_ref[layer, pl.ds(3, 1)]
+            )
+            if layer < layers - 1:
+                edge_buf[later, at] = edge
+            agg_ref[layer] += picked(gather_t[:, at], edge)
+            return carry
+
+        lax.fori_loop(0, edges // tile, edge_tile, 0)
+        save(0, layer, before_buf).start()
+        save(1, layer, message_buf).start()
+        inner = inner + weights.apply(agg_ref[layer], 5)
+        inner_ref[layer] = inner
+        update = weights.apply(silu(inner), 6) + param_ref[layer, pl.ds(5, 1)]
+        update_ref[layer] = update
+        nodes_ref[layer + 1] = (
+            node
+            + normed(update)[0] * (1.0 + param_ref[layer, pl.ds(6, 1)])
+            + param_ref[layer, pl.ds(7, 1)]
+        )
+    share(layers, nodes_ref[layers])
+    relay(layers)
+    gathered(layers)
+    save(0, layers - 1, before_buf).wait()
+    save(1, layers - 1, message_buf).wait()
+    save(2, layers - 1, edge_buf.at[(layers - 1) % 2]).wait()
+    for g in range(len(chunks)):
+        for j in others:
+            z_copy(g, j, row).wait_send()
+            for side in range(2):
+                a_copy(g, side, j, pos).wait_send()
+                b_copy(g, 1 - side, j, near_pos[side]).wait_send()
+            s_copy(g, j, core).wait_send()
+
+
+def forward(bands, rows, layers, grid, edge, send, recv, border, feed, mask, blocks, enc, enc_edge, params):
+    f32, bf16 = jnp.float32, jnp.bfloat16
+    dma = pltpu.SemaphoreType.DMA
+    width = blocks.shape[2]
+    edges, grids, rim = edge.shape[0], grid.shape[0], border.shape[0]
+    nodes = NODE_DEV
+    chips = bands // 2
+    inputs = 2 * nodes + bands * rim
+    each = blocks.shape[0] // layers
+    chunks = []
+    for layer in range(layers):
+        chunks += [(layer * each, 3), (layer * each + 3, each - 3)]
+    groups = len(chunks)
+    tile = edges // 2
+
+    def array(*shape):
+        return jax.ShapeDtypeStruct(shape, f32)
+
+    return pl.pallas_call(
+        functools.partial(forward_kernel, bands, rows, tuple(chunks), tile),
+        out_shape=(
+            array(blocks.shape[0], width, width),
+            array(layers, edges, width),
+            array(layers, edges, width),
+            array(layers, edges, width),
+            array(grids, width),
+            array(layers + 1, nodes, width),
+            array(nodes, width),
+            array(layers, nodes, width),
+            array(layers, nodes, width),
+            array(layers, nodes, width),
+            array(2, chips, rim, width),
+            array(2, chips, 8, 128),
+        ),
+        in_specs=[VMEM] * 12,
+        out_specs=[ANY] * 5 + [VMEM] * 7,
+        scratch_shapes=[
+            pltpu.VMEM((2, edges, width), f32),
+            pltpu.VMEM((edges, width), f32),
+            pltpu.VMEM((edges, width), f32),
+            pltpu.VMEM((edges, inputs), bf16),
+            pltpu.VMEM((nodes, edges), bf16),
+            pltpu.VMEM((inputs, width), bf16),
+            pltpu.VMEM((inputs, width), bf16),
+            pltpu.VMEM((each, width, width), bf16),
+            pltpu.VMEM((each, width, width), bf16),
+            pltpu.VMEM((2, width, width), f32),
+            pltpu.VMEM((2, chips, rim, width), f32),
+            pltpu.VMEM((2, rim, width), f32),
+            pltpu.VMEM((8, 128), f32),
+            dma((2,)),
+            dma((4,)),
+            dma,
+            dma((groups, rows - 1)),
+            dma((groups, rows - 1)),
+            dma((groups, 2, rows - 1)),
+            dma((groups, 2, rows - 1)),
+            dma((groups, 2, rows - 1)),
+            dma((groups, 2, rows - 1)),
+            dma((groups, rows - 1)),
+            dma((groups, rows - 1)),
+            dma((5, chips - 1)),
+            dma((5, chips - 1)),
+            dma((5, chips)),
+            dma((5, chips)),
+        ],
+        compiler_params=pltpu.CompilerParams(
+            collective_id=1, has_side_effects=True, vmem_limit_bytes=VMEM_BYTES
+        ),
+        name="forward",
+    )(
+        grid,
+        edge,
+        send[:, None],
+        recv[:, None],
+        recv[None, :],
+        border[:, None],
+        feed[None, :],
+        mask[None, :],
+        blocks,
+        enc,
+        enc_edge,
+        params,
+    )
+
+
+def slot_of(block):
+    for owner in range(2 * OWNER_CHIPS):
+        for slot in range(SLOTS):
+            if slot_used(owner, slot) and slot_block(owner, slot) == block:
+                return owner % 2, owner // 2, slot
+
+
+def backward_kernel(
+    bands,
+    rows,
+    each,
+    tile,
+    grid_ref,
+    target_ref,
+    mask_ref,
+    edge_ref,
+    read_ref,
+    send_row_ref,
+    recv_row_ref,
+    recv_ref,
+    border_row_ref,
+    enc_edge_ref,
+    dec_ref,
+    param_ref,
+    full_ref,
+    before_ref,
+    message_ref,
+    edges_ref,
+    embed_ref,
+    nodes_ref,
+    fed_ref,
+    agg_ref,
+    inner_ref,
+    update_ref,
+    table_ref,
+    count_ref,
+    grads_ref,
+    small_ref,
+    edge_buf,
+    before_buf,
+    message_buf,
+    node_buf,
+    agg_buf,
+    inner_buf,
+    update_buf,
+    edge_grad,
+    node_grad,
+    part_high,
+    part_low,
+    pick_t,
+    gather,
+    high,
+    low,
+    stage,
+    table,
+    sib,
+    land,
+    stage_sem,
+    load_sem,
+    d_send,
+    d_recv,
+    r_send,
+    r_recv,
+):
+    band, row, chip, core = place(bands, rows)
+    chips = bands // 2
+    layers = param_ref.shape[0]
+    nodes, width = node_buf.shape
+    edges = edge_buf.shape[0]
+    grids = grid_ref.shape[0]
+    border = border_row_ref.shape[1]
+    table_rows = bands * border
+    rows_dev = grads_ref.shape[3]
+    weights = Weights(full_ref, stage, high, low, stage_sem)
+    sibling = (chip * 2 + 1 - core, row)
+    partners = [((chip + j) % chips * 2 + core, row) for j in range(1, chips)] + [sibling]
+    own_rows = pl.ds(pl.multiple_of(row * rows_dev, rows_dev), rows_dev)
+
+    def load(kind, layer):
+        src = (before_ref, message_ref, edges_ref, agg_ref, inner_ref, update_ref, nodes_ref)[kind]
+        dst = (before_buf, message_buf, edge_buf, agg_buf, inner_buf, update_buf, node_buf)[kind]
+        return pltpu.make_async_copy(src.at[layer], dst, load_sem.at[kind])
+
+    table_load = pltpu.make_async_copy(table_ref, table, load_sem.at[7])
+    embed_buf = before_buf.at[pl.ds(0, grids)]
+    fed_buf = agg_buf
+    embed_load = pltpu.make_async_copy(embed_ref, embed_buf, load_sem.at[8])
+    fed_load = pltpu.make_async_copy(fed_ref, fed_buf, load_sem.at[9])
+    load(6, layers).start()
+    table_load.start()
+    for kind in range(6):
+        load(kind, layers - 1).start()
+    meet(partners)
+
+    def to_sibling(e):
+        return remote(table.at[1 - core], sib.at[e % 2], d_send.at[e], d_recv.at[e], sibling)
+
+    def to_band(e, j):
+        to = (chip + j) % chips
+        return remote(
+            table.at[core, to], land.at[e % 2, j - 1], r_send.at[e, j - 1], r_recv.at[e, j - 1], (to * 2 + core, row)
+        )
+
+    def give(e):
+        to_sibling(e).wait()
+        table[core] += sib[e % 2]
+        for j in range(1, chips):
+            to_band(e, j).start()
+
+    def returned(e):
+        total = table[core, chip]
+        for j in range(1, chips):
+            to_band(e, j).wait_recv()
+            total = total + land[e % 2, j - 1]
+        for j in range(1, chips):
+            to_band(e, j).wait_send()
+        return picked(hot(iota((nodes, border), 0) == border_row_ref[...]), total)
+
+    def put_table(value_high, value_low, count):
+        side_rows = chips * border
+        for side in range(2):
+            choice = pick_t[pl.ds(nodes + side * side_rows, side_rows), pl.ds(0, count)]
+            table[side] = chosen(choice, value_high, value_low).reshape(chips, border, width)
+
+    def put_grad(layer, block, value):
+        grads_ref[slot_of(layer * each + block)] = value
+
+    def add_grad(layer, block, value):
+        grads_ref[slot_of(layer * each + block)] += value
+
+    def choose_reads(at, size):
+        line = iota((size, grids), 0) + at
+        counts = jnp.zeros((size, grids), jnp.float32)
+        for way in range(read_ref.shape[0]):
+            counts = counts + jnp.where(line == read_ref[pl.ds(way, 1)], 1.0, 0.0)
+        return counts.astype(jnp.bfloat16)
+
+    def fill_reads(t, carry):
+        at = pl.multiple_of(t * 64, 64)
+        pick_t[pl.ds(at, 64), pl.ds(0, grids)] = choose_reads(at, 64)
+        return carry
+
+    lax.fori_loop(0, (nodes + table_rows) // 64, fill_reads, 0)
+
+    def choose_gather(at, size):
+        return hot(iota((size, nodes), 1) == recv_ref[pl.ds(at, size)])
+
+    fill_rows(gather, choose_gather)
+    load(6, layers).wait()
+    table_load.wait()
+    reads = edge_grad.at[pl.ds(0, grids)]
+    own_high, own_low = pieces(node_buf[...])
+    reads[...] = chosen(pick_t[pl.ds(0, nodes), pl.ds(0, grids)], own_high, own_low, TN)
+    side_rows = chips * border
+    for side in range(2):
+        side_high, side_low = pieces(table[side].reshape(side_rows, width))
+        choice = pick_t[pl.ds(nodes + side * side_rows, side_rows), pl.ds(0, grids)]
+        reads[...] += chosen(choice, side_high, side_low, TN)
+    load(6, layers - 1).start()
+    weights.load((layers - 1) * each, (6, 4, 5, 3, 0, 1, 2))
+    active = silu(reads[...])
+    mask = mask_ref[:, 0:1].astype(jnp.float32)
+    missed = grid_ref[...] + product(active, dec_ref[...]) - target_ref[...]
+    total = jnp.sum(jnp.sum(count_ref[:, :, 0:1, 0:1], axis=0), axis=0)
+    masked = mask * missed
+    loss = jnp.sum(column(masked * missed), axis=1, keepdims=True)
+    grad = (2.0 / total) * masked
+    encs = grid_ref.shape[1]
+    decs = dec_ref.shape[1]
+    decoder_at = encs + 8 + layers * 8
+    small_ref[pl.ds(decoder_at, decs)] = product(grad, active, TN)
+    tail_rows = small_ref.shape[0] - decoder_at - decs
+    small_ref[pl.ds(decoder_at + decs, tail_rows)] = jnp.broadcast_to(loss, (tail_rows, width))
+    read_high, read_low = pieces(product(grad, dec_ref[...], NT) * silu_back(reads[...]))
+    put_table(read_high, read_low, grids)
+    to_sibling(0).start()
+    node_grad[...] = chosen(pick_t[pl.ds(0, nodes), pl.ds(0, grids)], read_high, read_low)
+
+    def choose(at, size):
+        line = iota((size, edges), 0) + at
+        sent = line == send_row_ref[...]
+        received = line == recv_row_ref[...] + (nodes + table_rows)
+        return hot(jnp.logical_or(sent, received))
+
+    fill_rows(pick_t, choose, 64)
+    give(0)
+    edge_grad[...] = jnp.zeros_like(edge_grad)
+    node_grad[...] += returned(0)
+
+    for depth in range(layers):
+        layer = layers - 1 - depth
+        e = depth + 1
+        base = encs + 8 + layer * 8
+
+        def put_param(index, value, base=base):
+            small_ref[pl.ds(base + index, 1)] = value
+
+        def add_param(index, value, base=base):
+            small_ref[pl.ds(base + index, 1)] += value
+
+        for kind in (3, 4, 5, 6):
+            load(kind, layer).wait()
+        grad = node_grad[...]
+        norm, scale = normed(update_buf[...])
+        put_param(7, column(grad))
+        put_param(6, column(grad * norm))
+        grad = normed_back(grad * (1.0 + param_ref[layer, pl.ds(6, 1)]), norm, scale)
+        put_param(5, column(grad))
+        grad_high, grad_low = pieces(grad)
+        put_grad(layer, 6, product(silu(inner_buf[:, own_rows]), grad, TN))
+        grad = weights.times(grad_high, grad_low, 6, NT) * silu_back(inner_buf[...])
+        put_param(4, column(grad))
+        grad_high, grad_low = pieces(grad)
+        put_grad(layer, 4, product(node_buf[:, own_rows], grad, TN))
+        put_grad(layer, 5, product(agg_buf[:, own_rows], grad, TN))
+        node_grad[...] += weights.times(grad_high, grad_low, 4, NT)
+        agg_high, agg_low = pieces(weights.times(grad_high, grad_low, 5, NT))
+        for kind in (0, 1, 2):
+            load(kind, layer).wait()
+        for index in range(4):
+            put_param(index, jnp.zeros((1, width), jnp.float32))
+        for block in (0, 3):
+            put_grad(layer, block, jnp.zeros((rows_dev, width), jnp.float32))
+
+        def edge_tile(t, carry):
+            at = pl.ds(pl.multiple_of(t * tile, tile), tile)
+            grad = edge_grad[at] + chosen(gather[at], agg_high, agg_low)
+            edge_grad[at] = grad
+            norm, scale = normed(message_buf[at])
+            add_param(3, column(grad))
+            add_param(2, column(grad * norm))
+            grad = normed_back(grad * (1.0 + param_ref[layer, pl.ds(2, 1)]), norm, scale)
+            add_param(1, column(grad))
+            grad_high, grad_low = pieces(grad)
+            add_grad(layer, 3, product(silu(before_buf[at, own_rows]), grad, TN))
+            grad = weights.times(grad_high, grad_low, 3, NT) * silu_back(before_buf[at])
+            add_param(0, column(grad))
+            add_grad(layer, 0, product(edge_buf[at, own_rows], grad, TN))
+            grad_high, grad_low = pieces(grad)
+            part_high[at] = grad_high
+            part_low[at] = grad_low
+            return carry
+
+        lax.fori_loop(0, edges // tile, edge_tile, 0)
+        if layer > 0:
+            for kind in range(6):
+                load(kind, layer - 1).start()
+        else:
+            embed_load.start()
+            fed_load.start()
+        put_table(part_high[...], part_low[...], edges)
+        to_sibling(e).start()
+        sender = chosen(pick_t[pl.ds(0, nodes)], part_high[...], part_low[...])
+        give(e)
+        received = chosen(pick_t[pl.ds(nodes + table_rows, nodes)], part_high[...], part_low[...])
+
+        def edge_back(t, carry):
+            at = pl.ds(pl.multiple_of(t * tile, tile), tile)
+            edge_grad[at] += weights.times(part_high[at], part_low[at], 0, NT)
+            return carry
+
+        lax.fori_loop(0, edges // tile, edge_back, 0)
+        put_grad(layer, 2, product(node_buf[:, own_rows], received, TN))
+        node_grad[...] += weights.apply(received, 2, NT)
+        sender = sender + returned(e)
+        put_grad(layer, 1, product(node_buf[:, own_rows], sender, TN))
+        node_grad[...] += weights.apply(sender, 1, NT)
+        if layer > 0:
+            load(6, layer - 1).start()
+            weights.load((layer - 1) * each, (6, 4, 5, 3, 0, 1, 2))
+
+    embed_load.wait()
+    fed_load.wait()
+    norm, scale = normed(fed_buf[...])
+    fed_grad = normed_back(node_grad[...], norm, scale)
+    feed = hot(iota((grids, nodes), 1) == mask_ref[:, 1:2])
+    grad = picked(feed, fed_grad) * silu_back(embed_buf[...])
+    small_ref[pl.ds(0, encs)] = product(grid_ref[...], grad, TN)
+    small_ref[pl.ds(encs, 8)] = jnp.zeros((8, width), jnp.float32)
+
+    def embed_tile(t, carry):
+        at = pl.ds(pl.multiple_of(t * tile, tile), tile)
+        grad = edge_grad[at] * silu_back(product(edge_ref[at], enc_edge_ref[...]))
+        small_ref[pl.ds(encs, 8)] += product(edge_ref[at], grad, TN)[:8]
+        return carry
+
+    lax.fori_loop(0, edges // tile, embed_tile, 0)
+
+
+def backward(bands, rows, layers, rows_dev, inputs, saved):
+    f32, bf16 = jnp.float32, jnp.bfloat16
+    dma = pltpu.SemaphoreType.DMA
+    grid, edge, border = inputs[0], inputs[3], inputs[8]
+    full = saved[0]
+    width = full.shape[2]
+    each = full.shape[0] // layers
+    edges, grids, rim = edge.shape[0], grid.shape[0], border.shape[1]
+    nodes = NODE_DEV
+    chips = bands // 2
+    decs = inputs[10].shape[1]
+    small = grid.shape[1] + 8 + layers * 8 + decs + 8
+    small = -(-small // (16 * OWNER_CHIPS)) * 16 * OWNER_CHIPS
+    tile = edges // 2
+    node = pltpu.VMEM((nodes, width), f32)
+    return pl.pallas_call(
+        functools.partial(backward_kernel, bands, rows, each, tile),
+        out_shape=(
+            jax.ShapeDtypeStruct((2, OWNER_CHIPS, SLOTS, rows_dev, width), f32),
+            jax.ShapeDtypeStruct((small, width), f32),
+        ),
+        in_specs=[VMEM] * 12 + [ANY] * 11 + [VMEM],
+        out_specs=[VMEM, VMEM],
+        scratch_shapes=[
+            pltpu.VMEM((edges, width), f32),
+            pltpu.VMEM((edges, width), f32),
+            pltpu.VMEM((edges, width), f32),
+            node,
+            node,
+            node,
+            node,
+            pltpu.VMEM((edges, width), f32),
+            node,
+            pltpu.VMEM((edges, width), bf16),
+            pltpu.VMEM((edges, width), bf16),
+            pltpu.VMEM((2 * nodes + bands * rim, edges), bf16),
+            pltpu.VMEM((edges, nodes), bf16),
+            pltpu.VMEM((each, width, width), bf16),
+            pltpu.VMEM((each, width, width), bf16),
+            pltpu.VMEM((2, width, width), f32),
+            pltpu.VMEM((2, chips, rim, width), f32),
+            pltpu.VMEM((2, chips, rim, width), f32),
+            pltpu.VMEM((2, chips - 1, rim, width), f32),
+            dma((2,)),
+            dma((10,)),
+            dma((layers + 1,)),
+            dma((layers + 1,)),
+            dma((layers + 1, chips - 1)),
+            dma((layers + 1, chips - 1)),
+        ],
+        compiler_params=pltpu.CompilerParams(
+            collective_id=2, has_side_effects=True, vmem_limit_bytes=VMEM_BYTES
+        ),
+        name="backward",
+    )(*inputs, *saved)
 
 
 def newton(mom_ref, out_ref, first, count, gram, poly, temp, later):
@@ -293,7 +1083,7 @@
     def target(kind, slot, at_chip, at_core):
         at_owner = at_chip * 2 + at_core
         if slot == 3:
-            return shared_ref.at[at_owner]
+            return shared_ref.at[at_core * OWNER_CHIPS + at_chip]
         return (total_ref, ortho_ref)[kind].at[slot_block(at_owner, slot)]
 
     def keep(kind, slot):
@@ -540,7 +1330,7 @@
             dma((2, SLOTS + 1)),
         ],
         compiler_params=pltpu.CompilerParams(
-            collective_id=0, has_side_effects=True, vmem_limit_bytes=56 * 2**20
+            collective_id=0, has_side_effects=True, vmem_limit_bytes=VMEM_BYTES
         ),
         name="tail",
     )(grads, small, momentum)
@@ -583,87 +1373,75 @@
     decoder_first,
     decoder_second,
 ):
-    full_weights = lax.all_gather(processor_weights, "row", axis=2, tiled=True)
-
-    def share_border(node_lat):
-        return lax.all_gather(node_lat[border_nodes], "band", axis=0, tiled=True)
-
-    def return_border(table_grad, node_grad):
-        owned = lax.psum_scatter(table_grad, "band", scatter_dimension=0, tiled=True)
-        return node_grad + jax.ops.segment_sum(owned, border_nodes, num_segments=NODE_DEV)
-
-    def encode_local(encoder_now):
-        return encode(grid_input, edge_input, grid_to_mesh, encoder_now, NODE_DEV)
-
-    def layer_local(node_lat, edge_lat, table, weights, params):
-        combined = jnp.concatenate([node_lat, table], axis=0)
-        return processor(node_lat, edge_lat, combined[senders], receivers, weights, params)
-
-    def decode_local(node_lat, table, decoder_now):
-        combined = jnp.concatenate([node_lat, table], axis=0)
-        return decode(combined[mesh_to_grid], grid_input, grid_target, loss_mask, decoder_now)
-
-    node_lat, edge_lat = encode_local(encoder_weights)
-    kept = []
-    for depth in range(LAYERS):
-        table = share_border(node_lat)
-        kept.append((node_lat, edge_lat, table))
-        node_lat, edge_lat = layer_local(
-            node_lat, edge_lat, table, full_weights[depth], norm_params[depth]
-        )
-    table = share_border(node_lat)
-    local_loss, decode_back = jax.vjp(decode_local, node_lat, table, decoder_weights)
-    loss_total, mask_count = lax.psum((local_loss, jnp.sum(loss_mask.astype(jnp.float32))), "band")
-    node_grad, table_grad, decoder_grad = decode_back(1.0 / mask_count)
-    node_grad = return_border(table_grad, node_grad)
-    edge_grad = jnp.zeros_like(edge_lat)
-    weight_list = [None] * LAYERS
-    param_list = [None] * LAYERS
-    for depth in reversed(range(LAYERS)):
-        saved_nodes, saved_edges, saved_table = kept[depth]
-        outputs, layer_back = jax.vjp(
-            layer_local,
-            saved_nodes,
-            saved_edges,
-            saved_table,
-            full_weights[depth],
-            norm_params[depth],
-        )
-        node_grad, edge_grad, table_grad, weight_list[depth], param_list[depth] = layer_back(
-            (node_grad, edge_grad)
-        )
-        node_grad = return_border(table_grad, node_grad)
-    outputs, encode_back = jax.vjp(encode_local, encoder_weights)
-    (encoder_grad,) = encode_back((node_grad, edge_grad))
+    bands, rows = lax.axis_size("band"), lax.axis_size("row")
     layers, blocks, rows_dev, width = processor_weights.shape
-    row_start = lax.axis_index("row") * rows_dev
-    row_grads = [
-        lax.dynamic_slice_in_dim(weight_list[depth][block], row_start, rows_dev, 0)
-        for depth in range(layers)
-        for block in range(blocks)
-    ]
-    small_shapes = (encoder_weights.shape, decoder_weights.shape, norm_params.shape)
-    small = jnp.concatenate(
-        [encoder_grad.reshape(-1), decoder_grad.reshape(-1), jnp.stack(param_list).reshape(-1)]
+    channels = grid_input.shape[1]
+    edge_channels = edge_input.shape[1]
+    wide = -(-channels // 128) * 128
+    grids, rim = grid_input.shape[0], border_nodes.shape[0]
+
+    def widen(value, size, axis):
+        pads = [(0, 0), (0, 0)]
+        pads[axis] = (0, size - value.shape[axis])
+        return jnp.pad(value, pads)
+
+    def table_place(index):
+        owner, spot = (index - NODE_DEV) // rim, (index - NODE_DEV) % rim
+        moved = NODE_DEV + (owner % 2 * (bands // 2) + owner // 2) * rim + spot
+        return jnp.where(index < NODE_DEV, index, moved)
+
+    sent = table_place(senders)
+    reads = table_place(mesh_to_grid).reshape(grids, -1).T
+    grid_wide = widen(grid_input, wide, 1)
+    edge_wide = widen(edge_input, 128, 1)
+    edge_embed = widen(encoder_weights[channels:], 128, 0)
+    flat_weights = processor_weights.reshape(layers * blocks, rows_dev, width)
+    saved = forward(
+        bands,
+        rows,
+        layers,
+        grid_wide,
+        edge_wide,
+        sent,
+        receivers,
+        border_nodes,
+        grid_to_mesh,
+        loss_mask,
+        flat_weights,
+        widen(encoder_weights[:channels], wide, 0),
+        edge_embed,
+        norm_params,
     )
-    chunk = -(-small.shape[0] // (2 * OWNER_CHIPS * width * 8)) * 8
-    padded = jnp.pad(small, (0, 2 * OWNER_CHIPS * chunk * width - small.shape[0]))
-    padded = padded.reshape(OWNER_CHIPS, 2, chunk, width).swapaxes(0, 1)
+    inputs = (
+        grid_wide,
+        widen(grid_target, wide, 1),
+        jnp.stack([loss_mask, grid_to_mesh], axis=1),
+        edge_wide,
+        reads,
+        sent[None, :],
+        receivers[None, :],
+        receivers[:, None],
+        border_nodes[None, :],
+        edge_embed,
+        widen(decoder_weights, wide, 1),
+        norm_params,
+    )
+    grads, small = backward(bands, rows, layers, rows_dev, inputs, saved)
+    mask_count = jnp.sum(saved[-1][:, :, 0, 0])
     total, ortho, small = tail(
-        lax.axis_size("band"),
-        lax.axis_size("row"),
-        spread_slots(row_grads, rows_dev, width),
-        padded,
+        bands,
+        rows,
+        grads,
+        small.reshape(2, OWNER_CHIPS, -1, width),
         processor_momentum.reshape(layers * blocks, rows_dev, width),
     )
-    small = small.reshape(-1)
-    parts = []
-    start = 0
-    for shape in small_shapes:
-        size = shape[0] * shape[1] * (shape[2] if len(shape) > 2 else 1)
-        parts.append(small[start : start + size].reshape(shape))
-        start += size
-    encoder_grad, decoder_grad, param_grad = parts
+    small = small.reshape(-1, width)
+    params_at = wide + 8
+    decoder_at = params_at + layers * 8
+    encoder_grad = jnp.concatenate([small[:channels], small[wide : wide + edge_channels]])
+    param_grad = small[params_at:decoder_at].reshape(norm_params.shape)
+    decoder_grad = small[decoder_at : decoder_at + channels].T
+    loss_total = small[decoder_at + wide, 0]
     next_momentum = momentum_decay * processor_momentum + total.reshape(processor_weights.shape)
     next_weights = muon_finish(processor_weights, ortho.reshape(processor_weights.shape))
     next_average = average_decay * processor_average + (1.0 - average_decay) * next_weights

time: 1340 us -> 462 us (0.34)
  waiting for transfers between devices: 452 us -> 0 us
  matrix products: 346 us -> 0 us
  Pallas kernels: 137 us -> 415 us
  other arithmetic: 201 us -> 22.4 us
  local copies, waits for them, and re-layouts: 157 us -> 17.7 us
  between operations: 17.7 us -> 1.07 us
  blocking collectives: 13.9 us -> 0 us
    all_gather x5 -> x0, waiting for transfers between devices: 424 us -> none  [the longest x1 370 us: body(): full_weights = lax.all_gather(processor_weights, 'row', axis=2, tiled=True)]
    dot_general x70 -> x0, matrix products: 346 us -> none  [matmul(): return jnp.dot(left, right, precision=highest)]
    pallas_call x0 -> x2, Pallas kernels: none -> 273 us  [the longest x1 159 us: forward(): pl.pallas_call(functools.partial(forward_kernel, bands, rows, tuple(chunk...]
    scatter-add x15 -> x0, other arithmetic: 136 us -> none  [the longest x3 35.7 us: layer_local(): combined[senders]]
    gather x15 -> x0, local copies, waits for them, and re-layouts: 59.4 us -> none  [the longest x3 13.7 us: layer_local(): combined[senders]]
    unnamed x358 -> x38, local copies, waits for them, and re-layouts: 50.5 us -> 3.13 us
    reduce_scatter x4 -> x0, waiting for transfers between devices: 27.3 us -> none  [return_border(): lax.psum_scatter(table_grad, 'band', scatter_dimension=0, tiled=True)]
    reduce_sum x28 -> x1, other arithmetic: 25.9 us -> 1.37 us  [body(): mask_count = jnp.sum(saved[-1][:, :, 0, 0])]
  transfers between devices with their start and end apart: 9 -> 0, of which waited for: 8 -> 0; matrix products, arithmetic and copies ran while one was open for 14% -> 0% of each run, Pallas kernels for 0% -> 0%
where the time goes in v2:
time: 462 us; the launch traced here: 457 us
  Pallas kernels  415 us (90%)
  other arithmetic  22.4 us (5%)
  local copies, waits for them, and re-layouts  17.7 us (4%)
    pallas_call x1, Pallas kernels, forward(): pl.pallas_call(functools.partial(forward_kernel, bands, rows, tuple(chunk...  159 us
    pallas_call x1, Pallas kernels, tail(): pl.pallas_call(functools.partial(tail_kernel, bands, rows), out_shape=(ja...  143 us
    pallas_call x1, Pallas kernels, backward(): pl.pallas_call(functools.partial(backward_kernel, bands, rows, each, tile...  114 us
    add x1, other arithmetic, body(): average_decay * processor_average + (1.0 - average_decay) * next_weights  15.8 us

profile of v2, /device:TPU:0, one launch (start us, length us, event | category | flops | bytes accessed | tf_op | source)
XLA Modules:
  0.0 456.6 jit_solution(6070412339541339904)
XLA Ops:
  0.6 0.0 copy-start.14
  0.7 0.0 copy-start.10
  0.7 0.0 copy-start
  0.7 0.0 copy-start.15
  0.7 1.6 copy.52
  2.3 1.0 pad.23.grid_ref
  3.3 1.0 copy.54
  4.2 0.9 pad.25.edge_ref
  5.1 0.0 copy-done.14
  5.2 1.1 broadcast_in_dim.36.send_ref
  6.2 0.0 copy-done.10
  6.2 1.1 broadcast_in_dim.35.recv_ref
  7.3 0.0 copy-done
  7.3 0.7 pad.26.enc_edge_ref
  8.1 0.6 broadcast_in_dim.28.recv_row_ref
  8.7 0.8 pad.28.enc_ref
  9.5 0.7 copy.59.border_ref
  10.2 158.9 %forward.1 = (f32[21,512,512]{2,1,0:T(8,128)}, f32[3,1280,512]{2,1,0:T(8,128)}, f32[3,1280,512]{2,1,0:T(8,128)}, f32[3,1280,512]{2,1,0:T(8,128)}, f32[960,512]{1...) custom-call(f32[960,256]{1,0:T(8,128)} %pad.23.grid_ref, ...), custom_call_target="tpu_custom_call" | custom-call | tf_op jit(solution)/shard_map/forward/pallas_call | solution.py:515
  169.1 0.0 copy-start.11
  169.2 0.0 copy-start.12
  169.2 0.6 broadcast_in_dim.27.send_row_ref
  169.8 0.3 copy.53
  170.1 1.0 pad.24.target_ref
  171.1 0.0 copy-done.1
  171.1 0.2 copy.56
  171.3 0.9 pad.27.dec_ref
  172.2 0.4 reshape.54
  172.6 0.8 copy.55
  173.4 0.0 copy-done.11
  173.4 1.0 copy.60.mask_ref
  174.4 113.9 %backward.1 = (f32[2,4,3,128,512]{4,3,2,1,0:T(8,128)}, f32[576,512]{1,0:T(8,128)}) custom-call(f32[960,256]{1,0:T(8,128)} %pad.23.grid_ref, f32[960,256]{1,0:T(8,128)} %pad.24.target_ref, s32[960,2]{1,0:T(8,128)} %copy.60.mask_ref, f32[1280,128]{1,0:T(8,128)} %pad.25.edge_ref, s32[3,960]{1,0:T(4,128)} %bitcast.42, s32[1,1280]{1,0:T(1,128)} %broadcast_in_dim.27.send_row_ref, ...), custom_call_target="tpu_custom_call" | custom-call | tf_op jit(solution)/shard_map/backward/pallas_call | solution.py:887
  288.3 0.0 copy-start.3
  288.3 0.0 copy-start.4
  288.3 0.0 copy-start.16
  288.3 142.7 %tail.1 = (f32[21,128,512]{2,1,0:T(8,128)}, f32[21,128,512]{2,1,0:T(8,128)}, f32[8,72,512]{2,1,0:T(8,128)}) custom-call(f32[2,4,3,128,512]{4,3,2,1,0:T(8,128)} %get-tuple-element.43.grad_ref, f32[2,4,72,512]{3,2,1,0:T(8,128)} %bitcast.36, f32[21,128,512]{2,1,0:T(8,128)} %bitcast.31), custom_call_target="tpu_custom_call" | custom-call | tf_op jit(solution)/shard_map/tail/pallas_call | solution.py:1291
  431.0 1.1 slice.34
  432.1 0.7 slice.35
  432.8 1.3 multiply_subtract_fusion.2
  434.2 0.0 copy-done.16
  434.2 0.0 copy-start.8
  434.2 0.0 copy-start.9
  434.2 15.8 %multiply_add_fusion = (f32[3,7,128,512]{3,2,1,0:T(8,128)}, f32[3,7,128,512]{3,2,1,0:T(8,128)}, f32[3,7,128,512]{3,2,1,0:T(8,128)}) fusion(f32[3,7,128,512]{3,2,1,0:T(8,128)} %param.36, f32[3,7,128,512]{3,2,1,0:T(8,128)} %bitcast.34, f32[7]{0:T(128)S(1)} %copy-done.16, f32[3,7,128,512]{3,2,1,0:T(8,128)} %param.34, f32[3,7,128,512]{3,2,1,0:T(8,128)} %bitcast.33, ...), kind=kLoop, calls=%fused_computation | loop fusion | flops 11010048 | bytes 44040220 | tf_op jit(solution)/shard_map/add | solution.py:1447
  450.0 0.0 copy-done.6
  450.0 2.4 multiply_subtract_fusion.1
  452.4 0.0 copy-done.8
  452.4 1.5 multiply_subtract_fusion.3
  453.8 1.2 slice.32
  455.0 1.4 slice_reduce_fusion
  (19 shorter events, 0.1 us)
Async XLA Ops:
  0.6 4.5 copy-start.14
  0.7 5.6 %copy-start.10 = (s32[1280]{0:T(1024)S(1)}, s32[1280]{0:T(1024)}, u32[]{:S(2)}) copy-start(s32[1280]{0:T(1024)} %param.26) | copy-start | bytes 15364
  0.7 6.7 %copy-start = (f32[231,512]{1,0:T(8,128)S(1)}, f32[231,512]{1,0:T(8,128)}, u32[]{:S(2)}) copy-start(f32[231,512]{1,0:T(8,128)} %param.31) | copy-start | bytes 1419268
  0.7 8.8 %copy-start.15 = (s32[64]{0:T(128)S(1)}, s32[64]{0:T(128)}, u32[]{:S(2)}) copy-start(s32[64]{0:T(128)} %param.27) | copy-start | bytes 772
  7.3 162.4 %copy-start.2 = (f32[960,227]{0,1:T(8,128)S(1)}, f32[960,227]{0,1:T(8,128)}, u32[]{:S(2)}) copy-start(f32[960,227]{0,1:T(8,128)} %param.23) | copy-start | bytes 2615044
  10.2 160.9 %copy-start.1 = (f32[512,227]{0,1:T(8,128)S(1)}, f32[512,227]{0,1:T(8,128)}, u32[]{:S(2)}) copy-start(f32[512,227]{0,1:T(8,128)} %param.40) | copy-start | bytes 1394692
  10.2 162.0 %copy-start.13 = (s32[2880]{0:T(1024)S(1)}, s32[2880]{0:T(1024)}, u32[]{:S(2)}) copy-start(s32[2880]{0:T(1024)} %param.29) | copy-start | bytes 34564
  169.1 4.2 copy-start.11
  169.2 4.2 copy-start.12
  288.3 144.5 %copy-start.3 = (f32[231,512]{1,0:T(8,128)S(1)}, f32[231,512]{1,0:T(8,128)}, u32[]{:S(2)}) copy-start(f32[231,512]{1,0:T(8,128)} %param.33) | copy-start | bytes 1419268
  288.3 144.5 %copy-start.4 = (f32[231,512]{1,0:T(8,128)S(1)}, f32[231,512]{1,0:T(8,128)}, u32[]{:S(2)}) copy-start(f32[231,512]{1,0:T(8,128)} %param.32) | copy-start | bytes 1419268
  288.3 145.8 %copy-start.16 = (f32[7]{0:T(128)S(1)}, f32[7]{0:T(128)}, u32[]{:S(2)}) copy-start(f32[7]{0:T(128)} %constant.154) | copy-start | bytes 88
  434.2 15.8 %copy-start.5 = (f32[512,227]{0,1:T(8,128)S(1)}, f32[512,227]{0,1:T(8,128)}, u32[]{:S(2)}) copy-start(f32[512,227]{0,1:T(8,128)} %param.42) | copy-start | bytes 1394692
  434.2 15.8 %copy-start.6 = (f32[512,227]{0,1:T(8,128)S(1)}, f32[512,227]{0,1:T(8,128)}, u32[]{:S(2)}) copy-start(f32[512,227]{0,1:T(8,128)} %param.41) | copy-start | bytes 1394692
  434.2 18.2 %copy-start.7 = (f32[3,8,512]{2,1,0:T(8,128)S(1)}, f32[3,8,512]{2,1,0:T(8,128)}, u32[]{:S(2)}) copy-start(f32[3,8,512]{2,1,0:T(8,128)} %param_ref.3) | copy-start | bytes 147460
  434.2 18.2 %copy-start.8 = (f32[3,8,512]{2,1,0:T(8,128)S(1)}, f32[3,8,512]{2,1,0:T(8,128)}, u32[]{:S(2)}) copy-start(f32[3,8,512]{2,1,0:T(8,128)} %param.39) | copy-start | bytes 147460
  434.2 18.2 %copy-start.9 = (f32[3,8,512]{2,1,0:T(8,128)S(1)}, f32[3,8,512]{2,1,0:T(8,128)}, u32[]{:S(2)}) copy-start(f32[3,8,512]{2,1,0:T(8,128)} %param.38) | copy-start | bytes 147460

commit v3 on v2

--- a/solution.py
+++ b/solution.py
@@ -129,6 +129,9 @@
     return lax.broadcasted_iota(jnp.int32, shape, axis)
 
 
+SEND_ROW, RECV_ROW, BORDER_ROW, FEED_ROW, MASK_ROW, READ_ROW = range(6)
+
+
 class Weights:
     def __init__(self, full_ref, stage, high, low, sem):
         self.full, self.stage, self.high, self.low, self.sem = full_ref, stage, high, low, sem
@@ -178,10 +181,10 @@
     edge_ref,
     send_ref,
     recv_ref,
-    recv_row_ref,
     border_ref,
     feed_ref,
     mask_ref,
+    read_ref,
     w_ref,
     enc_ref,
     enc_edge_ref,
@@ -198,9 +201,11 @@
     update_ref,
     table_ref,
     count_ref,
+    index_ref,
     edge_buf,
     before_buf,
     message_buf,
+    index_t,
     pick,
     gather_t,
     src_high,
@@ -233,7 +238,8 @@
     rows_dev = w_ref.shape[1]
     nodes, width = fed_ref.shape
     edges = edge_buf.shape[1]
-    border = border_ref.shape[0]
+    border = border_buf.shape[1]
+    grids = grid_ref.shape[0]
     weights = Weights(full_ref, stage, high, low, stage_sem)
     quad, pos = chip // 4, chip % 4
     pos_x, pos_y = pos + 1 - 2 * (pos % 2), pos + 2 - 4 * (pos // 2)
@@ -306,7 +312,7 @@
             s_copy(g, j, 1 - core).wait_recv()
 
     def tick(t):
-        for g, stage_of in ((t - 4, ready), (t - 3, start_s), (t - 2, start_b), (t - 1, start_a), (t + 1, start_z)):
+        for g, stage_of in ((t - 5, ready), (t - 4, start_s), (t - 3, start_b), (t - 1, start_a), (t + 1, start_z)):
             if 0 <= g < len(chunks):
                 stage_of(g)
 
@@ -350,7 +356,7 @@
 
     def share(e, value):
         par = e % 2
-        choice = hot(iota((border, nodes), 1) == border_ref[...])
+        choice = hot(iota((border, nodes), 1) == index_t[pl.ds(0, border), BORDER_ROW : BORDER_ROW + 1])
         rows_out = picked(choice, value)
         border_buf[par] = rows_out
         table_of(e)[core, chip] = rows_out
@@ -384,50 +390,67 @@
         dst = (before_ref, message_ref, edges_ref, embed_ref)[kind]
         return pltpu.make_async_copy(src, dst if layer is None else dst.at[layer], save_sem.at[kind])
 
-    embed_buf = before_buf.at[pl.ds(0, grid_ref.shape[0])]
+    def table_place(index):
+        far = (index - nodes).astype(jnp.float32)
+        owner = jnp.floor((far + 0.5) * (1.0 / border))
+        at_chip = jnp.floor(owner * 0.5)
+        moved = ((owner - 2.0 * at_chip) * chips + at_chip) * border + far - owner * border
+        return jnp.where(index < nodes, index, moved.astype(jnp.int32) + nodes)
+
+    index_ref[...] = jnp.zeros_like(index_ref)
+    index_ref[SEND_ROW : SEND_ROW + 1] = table_place(send_ref[...])
+    index_ref[RECV_ROW : RECV_ROW + 1] = recv_ref[...]
+    index_ref[BORDER_ROW : BORDER_ROW + 1, pl.ds(0, border)] = border_ref[...]
+    index_ref[FEED_ROW : FEED_ROW + 1, pl.ds(0, grids)] = feed_ref[...]
+    index_ref[MASK_ROW : MASK_ROW + 1, pl.ds(0, grids)] = mask_ref[...]
+    index_ref[READ_ROW:, pl.ds(0, grids)] = table_place(read_ref[...])
+    index_t[...] = index_ref[...].T
+    embed_buf = before_buf.at[pl.ds(0, grids)]
     embed_buf[...] = product(grid_ref[...], enc_ref[...])
     save(3, None, embed_buf).start()
-    feed = hot(iota((nodes, grid_ref.shape[0]), 0) == feed_ref[...])
+    tick(1)
+    feed = hot(iota((nodes, grids), 0) == index_ref[FEED_ROW : FEED_ROW + 1, pl.ds(0, grids)])
     fed = picked(feed, silu(embed_buf[...]))
     fed_ref[...] = fed
     nodes_ref[0] = normed(fed)[0]
-    count = jnp.sum(mask_ref[...].astype(jnp.float32), axis=1, keepdims=True)
-    counts = jnp.broadcast_to(count, count_buf.shape)
+    mask = index_ref[MASK_ROW : MASK_ROW + 1, pl.ds(0, grids)].astype(jnp.float32)
+    counts = jnp.broadcast_to(jnp.sum(mask, axis=1, keepdims=True), count_buf.shape)
     count_buf[...] = counts
     count_ref[core, chip] = counts
+    tick(2)
     fill_rows(
         edge_buf.at[0], lambda at, size: silu(product(edge_ref[pl.ds(at, size)], enc_edge_ref[...])), 256
     )
-    tick(1)
-    table_rows = 2 * chips * border
     inputs = src_high.shape[0]
+    near_inputs = 2 * nodes
 
     def choose(at, size):
         columns = iota((size, inputs), 1)
-        sent = columns == send_ref[pl.ds(at, size)]
-        received = columns == recv_ref[pl.ds(at, size)] + (nodes + table_rows)
-        return hot(jnp.logical_or(sent, received))
+        sent = index_t[pl.ds(at, size), SEND_ROW : SEND_ROW + 1]
+        received = index_t[pl.ds(at, size), RECV_ROW : RECV_ROW + 1] + nodes
+        sent = jnp.where(sent < nodes, sent, sent + nodes)
+        return hot(jnp.logical_or(columns == sent, columns == received))
 
     fill_rows(pick, choose)
+    tick(3)
 
     def choose_receiver(at, size):
-        return hot(iota((size, edges), 0) + at == recv_row_ref[...])
+        return hot(iota((size, edges), 0) + at == index_ref[RECV_ROW : RECV_ROW + 1])
 
     fill_rows(gather_t, choose_receiver, 64)
-    tick(2)
-    tick(3)
     own.wait()
+    tick(4)
+    tick(5)
     for layer in range(layers):
         first = layer * blocks
         now, later = layer % 2, (layer + 1) % 2
-        tick(4 + 2 * layer)
-        weights.load(first, (1, 2, 0))
+        weights.load(first, (1, 2))
         node = nodes_ref[layer]
         node_high, node_low = pieces(node)
         sender = weights.times(node_high, node_low, 1)
         share(layer, sender)
         put_src(0, sender)
-        put_src(nodes + table_rows, weights.times(node_high, node_low, 2))
+        put_src(nodes, weights.times(node_high, node_low, 2))
         if layer > 0:
             save(0, layer - 1, before_buf).wait()
             save(1, layer - 1, message_buf).wait()
@@ -435,41 +458,60 @@
         else:
             save(3, None, embed_buf).wait()
         save(2, layer, edge_buf.at[now]).start()
-        tick(5 + 2 * layer)
+        tick(6 + 4 * layer)
+        weights.load(first, (0,))
+
+        def near_part(t):
+            at = pl.ds(t * tile, tile)
+            before_buf[at] = (
+                weights.apply(edge_buf[now, at], 0)
+                + chosen(
+                    pick[at, pl.ds(0, near_inputs)],
+                    src_high[pl.ds(0, near_inputs)],
+                    src_low[pl.ds(0, near_inputs)],
+                )
+                + param_ref[layer, pl.ds(0, 1)]
+            )
+
+        near_part(0)
+        tick(7 + 4 * layer)
         relay(layer)
-        weights.load(first, (3, 4, 5, 6))
+        near_part(1)
+        weights.load(first, (3, 4))
         inner = weights.times(node_high, node_low, 4) + param_ref[layer, pl.ds(4, 1)]
         gathered(layer)
         table_now = table_of(layer)
         for side in range(2):
-            for at in range(chips):
-                put_src(nodes + (side * chips + at) * border, table_now[side, at])
+            put_src(
+                near_inputs + side * chips * border,
+                table_now[side].reshape(chips * border, width),
+            )
         agg_ref[layer] = jnp.zeros((nodes, width), jnp.float32)
 
-        def edge_tile(t, carry):
-            at = pl.ds(pl.multiple_of(t * tile, tile), tile)
-            edge = edge_buf[now, at]
-            before = (
-                weights.apply(edge, 0)
-                + chosen(pick[at], src_high[...], src_low[...])
-                + param_ref[layer, pl.ds(0, 1)]
+        def edge_tile(t):
+            at = pl.ds(t * tile, tile)
+            far_inputs = pl.ds(near_inputs, inputs - near_inputs)
+            before = before_buf[at] + chosen(
+                pick[at, far_inputs], src_high[far_inputs], src_low[far_inputs]
             )
             before_buf[at] = before
             message = weights.apply(silu(before), 3) + param_ref[layer, pl.ds(1, 1)]
             message_buf[at] = message
             edge = (
-                edge
+                edge_buf[now, at]
                 + normed(message)[0] * (1.0 + param_ref[layer, pl.ds(2, 1)])
                 + param_ref[layer, pl.ds(3, 1)]
             )
             if layer < layers - 1:
                 edge_buf[later, at] = edge
             agg_ref[layer] += picked(gather_t[:, at], edge)
-            return carry
-
-        lax.fori_loop(0, edges // tile, edge_tile, 0)
+
+        edge_tile(0)
+        tick(8 + 4 * layer)
+        edge_tile(1)
         save(0, layer, before_buf).start()
         save(1, layer, message_buf).start()
+        weights.load(first, (5, 6))
         inner = inner + weights.apply(agg_ref[layer], 5)
         inner_ref[layer] = inner
         update = weights.apply(silu(inner), 6) + param_ref[layer, pl.ds(5, 1)]
@@ -479,6 +521,7 @@
             + normed(update)[0] * (1.0 + param_ref[layer, pl.ds(6, 1)])
             + param_ref[layer, pl.ds(7, 1)]
         )
+        tick(9 + 4 * layer)
     share(layers, nodes_ref[layers])
     relay(layers)
     gathered(layers)
@@ -494,18 +537,21 @@
             s_copy(g, j, core).wait_send()
 
 
-def forward(bands, rows, layers, grid, edge, send, recv, border, feed, mask, blocks, enc, enc_edge, params):
+def forward(bands, rows, grid, edge, indices, blocks, enc, enc_edge, params):
     f32, bf16 = jnp.float32, jnp.bfloat16
     dma = pltpu.SemaphoreType.DMA
     width = blocks.shape[2]
-    edges, grids, rim = edge.shape[0], grid.shape[0], border.shape[0]
+    edges, grids = edge.shape[0], grid.shape[0]
+    layers = params.shape[0]
+    rim = indices[2].shape[1]
+    index_rows = READ_ROW + indices[5].shape[0]
     nodes = NODE_DEV
     chips = bands // 2
     inputs = 2 * nodes + bands * rim
     each = blocks.shape[0] // layers
     chunks = []
     for layer in range(layers):
-        chunks += [(layer * each, 3), (layer * each + 3, each - 3)]
+        chunks += [(layer * each + first, size) for first, size in ((1, 2), (0, 1), (3, 2), (5, 2))]
     groups = len(chunks)
     tile = edges // 2
 
@@ -527,13 +573,15 @@
             array(layers, nodes, width),
             array(2, chips, rim, width),
             array(2, chips, 8, 128),
+            jax.ShapeDtypeStruct((index_rows, edges), jnp.int32),
         ),
         in_specs=[VMEM] * 12,
-        out_specs=[ANY] * 5 + [VMEM] * 7,
+        out_specs=[ANY] * 5 + [VMEM] * 8,
         scratch_shapes=[
             pltpu.VMEM((2, edges, width), f32),
             pltpu.VMEM((edges, width), f32),
             pltpu.VMEM((edges, width), f32),
+            pltpu.VMEM((edges, index_rows), jnp.int32),
             pltpu.VMEM((edges, inputs), bf16),
             pltpu.VMEM((nodes, edges), bf16),
             pltpu.VMEM((inputs, width), bf16),
@@ -567,12 +615,7 @@
     )(
         grid,
         edge,
-        send[:, None],
-        recv[:, None],
-        recv[None, :],
-        border[:, None],
-        feed[None, :],
-        mask[None, :],
+        *indices,
         blocks,
         enc,
         enc_edge,
@@ -580,11 +623,274 @@
     )
 
 
-def slot_of(block):
-    for owner in range(2 * OWNER_CHIPS):
-        for slot in range(SLOTS):
-            if slot_used(owner, slot) and slot_block(owner, slot) == block:
-                return owner % 2, owner // 2, slot
+def groups(layer):
+    return (
+        (layer, 0, 0, 3),
+        (3 + layer, 0, 4, 3),
+        (6 + layer // 2, layer % 2, 3, 1),
+    )
+
+
+class Reducer:
+    def __init__(self, bands, layer, at, grads, sib, land, total, sems):
+        band, row, self.chip, self.core = place(bands, 1)
+        self.row = row
+        self.chips = bands // 2
+        self.sibling = (self.chip * 2 + 1 - self.core, row)
+        self.layer, self.at = layer, at
+        self.grads, self.sib, self.land, self.total = grads, sib, land, total
+        (self.c_send, self.c_recv, self.r_send, self.r_recv) = sems[:4]
+        (self.o_send, self.o_recv, self.p_send, self.p_recv, self.k_sem) = sems[4:]
+
+    def each(self):
+        for q, (owner, slot, block, count) in enumerate(groups(self.layer)):
+            yield q, owner // 2, owner % 2, slot, pl.ds(block, count), count
+
+    def to_sibling(self, q, rows):
+        return remote(
+            self.grads.at[rows],
+            self.sib.at[rows],
+            self.c_send.at[self.at, q],
+            self.c_recv.at[self.at, q],
+            self.sibling,
+        )
+
+    def to_owner(self, q, at_chip, at_core, rows, count):
+        step = (at_chip - self.chip + self.chips) % self.chips
+        return remote(
+            self.grads.at[rows],
+            self.land.at[self.at, step - 1, pl.ds(0, count)],
+            self.r_send.at[self.at, q],
+            self.r_recv.at[self.at, step - 1],
+            (at_chip * 2 + at_core, self.row),
+        )
+
+    def to_chip(self, q, rows, j):
+        return remote(
+            self.grads.at[rows],
+            self.total.at[rows],
+            self.o_send.at[self.at, j - 1],
+            self.o_recv.at[self.at, q],
+            ((self.chip + j) % self.chips * 2 + self.core, self.row),
+        )
+
+    def across(self, q, rows, src):
+        return remote(
+            src.at[rows],
+            self.total.at[rows],
+            self.p_send.at[self.at, q],
+            self.p_recv.at[self.at, q],
+            self.sibling,
+        )
+
+    def keep(self, rows):
+        return pltpu.make_async_copy(self.grads.at[rows], self.total.at[rows], self.k_sem.at[self.at])
+
+    def start(self):
+        for q, at_chip, at_core, slot, rows, count in self.each():
+            @pl.when(self.core != at_core)
+            def _():
+                self.to_sibling(q, rows).start()
+
+    def pair(self):
+        for q, at_chip, at_core, slot, rows, count in self.each():
+            @pl.when(self.core == at_core)
+            def _():
+                self.to_sibling(q, rows).wait_recv()
+                self.grads[rows] += self.sib[rows]
+
+                @pl.when(self.chip != at_chip)
+                def _():
+                    self.to_owner(q, at_chip, at_core, rows, count).start()
+
+    def reduce(self, take, load):
+        for q, at_chip, at_core, slot, rows, count in self.each():
+            @pl.when(jnp.logical_and(self.core == at_core, self.chip == at_chip))
+            def _():
+                value = self.grads[rows]
+                for j in range(1, self.chips):
+                    landed = self.land.at[self.at, j - 1, pl.ds(0, count)]
+                    remote(
+                        landed,
+                        landed,
+                        self.r_send.at[self.at, q],
+                        self.r_recv.at[self.at, j - 1],
+                        self.sibling,
+                    ).wait_recv()
+                    value = value + load(landed, count)
+                self.grads[rows] = value
+                take(slot, count, value)
+                for j in range(1, self.chips):
+                    self.to_chip(q, rows, j).start()
+                self.across(q, rows, self.grads).start()
+                self.keep(rows).start()
+
+    def relay(self):
+        for q, at_chip, at_core, slot, rows, count in self.each():
+            @pl.when(jnp.logical_and(self.core == at_core, self.chip != at_chip))
+            def _():
+                self.to_chip(q, rows, 1).wait_recv()
+                self.across(q, rows, self.total).start()
+
+    def finish(self):
+        for q, at_chip, at_core, slot, rows, count in self.each():
+            @pl.when(self.core != at_core)
+            def _():
+                self.to_sibling(q, rows).wait_send()
+                self.across(q, rows, self.total).wait_recv()
+
+            @pl.when(self.core == at_core)
+            def _():
+                self.across(q, rows, self.total).wait_send()
+
+                @pl.when(self.chip != at_chip)
+                def _():
+                    self.to_owner(q, at_chip, at_core, rows, count).wait_send()
+
+                @pl.when(self.chip == at_chip)
+                def _():
+                    for j in range(1, self.chips):
+                        self.to_chip(q, rows, j).wait_send()
+                    self.keep(rows).wait()
+
+
+def reducer_sems(count, chips):
+    dma = pltpu.SemaphoreType.DMA
+    return [
+        dma((count, 3)),
+        dma((count, 3)),
+        dma((count, 3)),
+        dma((count, chips - 1)),
+        dma((count, chips - 1)),
+        dma((count, 3)),
+        dma((count, 3)),
+        dma((count, 3)),
+        dma((count,)),
+    ]
+
+
+class Spreader:
+    def __init__(self, bands, at, grads, sib, land, landed, total, sems):
+        band, self.row, self.chip, self.core = place(bands, 1)
+        self.chips = bands // 2
+        self.sibling = (self.chip * 2 + 1 - self.core, self.row)
+        self.at = at
+        self.grads, self.sib, self.land, self.landed, self.total = grads, sib, land, landed, total
+        self.half = grads.shape[1] // 2
+        self.piece = self.half // OWNER_CHIPS
+        (self.c_sem, self.r_send, self.r_recv, self.o_send, self.o_recv, self.p_sem, self.k_sem) = sems
+
+    def rows(self, core):
+        return pl.ds(pl.multiple_of(core * self.half, 8), self.half)
+
+    def part(self, core, chip):
+        return pl.ds(pl.multiple_of(core * self.half + chip * self.piece, 8), self.piece)
+
+    def to_sibling(self):
+        return remote(
+            self.grads.at[:, self.rows(1 - self.core)],
+            self.sib,
+            self.c_sem.at[self.at, 0],
+            self.c_sem.at[self.at, 1],
+            self.sibling,
+        )
+
+    def to_owner(self, chip):
+        step = (chip - self.chip + self.chips) % self.chips
+        return remote(
+            self.grads.at[:, self.part(self.core, chip)],
+            self.land.at[step - 1],
+            self.r_send.at[self.at, chip],
+            self.r_recv.at[self.at, step - 1],
+            (chip * 2 + self.core, self.row),
+        )
+
+    def to_chip(self, j, chip):
+        part = self.part(self.core, chip)
+        return remote(
+            self.grads.at[:, part],
+            self.total.at[:, part],
+            self.o_send.at[self.at, j - 1],
+            self.o_recv.at[self.at, chip],
+            ((self.chip + j) % self.chips * 2 + self.core, self.row),
+        )
+
+    def keep(self):
+        part = self.part(self.core, self.chip)
+        return pltpu.make_async_copy(
+            self.grads.at[:, part], self.total.at[:, part], self.k_sem.at[self.at, 0]
+        )
+
+    def across(self, core):
+        region = self.total.at[:, self.rows(core)]
+        return remote(region, region, self.p_sem.at[self.at, 0], self.p_sem.at[self.at, 1], self.sibling)
+
+    def owned(self, body):
+        if self.chips == OWNER_CHIPS:
+            body()
+        else:
+            pl.when(self.chip < OWNER_CHIPS)(body)
+
+    def start(self):
+        self.to_sibling().start()
+
+    def pair(self):
+        self.to_sibling().wait()
+        self.grads[:, self.rows(self.core)] += self.sib[...]
+        for chip in range(OWNER_CHIPS):
+            pl.when(self.chip != chip)(self.to_owner(chip).start)
+
+    def reduce(self):
+        def body():
+            part = self.part(self.core, self.chip)
+            for j in range(1, self.chips):
+                remote(
+                    self.landed,
+                    self.land.at[j - 1],
+                    self.r_send.at[self.at, 0],
+                    self.r_recv.at[self.at, j - 1],
+                    self.sibling,
+                ).wait_recv()
+                copy = pltpu.make_async_copy(self.land.at[j - 1], self.landed, self.k_sem.at[self.at, 1])
+                copy.start()
+                copy.wait()
+                self.grads[:, part] += self.landed[...]
+            for j in range(1, self.chips):
+                self.to_chip(j, self.chip).start()
+            self.keep().start()
+
+        self.owned(body)
+
+    def relay(self):
+        for chip in range(OWNER_CHIPS):
+            pl.when(self.chip != chip)(self.to_chip(1, chip).wait_recv)
+        self.owned(lambda: self.keep().wait())
+        self.across(self.core).start()
+
+    def finish(self):
+        self.across(self.core).wait_send()
+        self.across(1 - self.core).wait_recv()
+        for chip in range(OWNER_CHIPS):
+            pl.when(self.chip != chip)(self.to_owner(chip).wait_send)
+
+        def body():
+            for j in range(1, self.chips):
+                self.to_chip(j, self.chip).wait_send()
+
+        self.owned(body)
+
+
+def spreader_sems(count, chips):
+    dma = pltpu.SemaphoreType.DMA
+    return [
+        dma((count, 2)),
+        dma((count, OWNER_CHIPS)),
+        dma((count, chips - 1)),
+        dma((count, chips - 1)),
+        dma((count, OWNER_CHIPS)),
+        dma((count, 2)),
+        dma((count, 2)),
+    ]
 
 
 def backward_kernel(
@@ -594,13 +900,8 @@
     tile,
     grid_ref,
     target_ref,
-    mask_ref,
     edge_ref,
-    read_ref,
-    send_row_ref,
-    recv_row_ref,
-    recv_ref,
-    border_row_ref,
+    index_ref,
     enc_edge_ref,
     dec_ref,
     param_ref,
@@ -618,6 +919,8 @@
     count_ref,
     grads_ref,
     small_ref,
+    total_ref,
+    land_grads,
     edge_buf,
     before_buf,
     message_buf,
@@ -625,6 +928,7 @@
     agg_buf,
     inner_buf,
     update_buf,
+    index_t,
     edge_grad,
     node_grad,
     part_high,
@@ -637,12 +941,16 @@
     table,
     sib,
     land,
+    grads_buf,
+    sib_grads,
+    landed_buf,
     stage_sem,
     load_sem,
     d_send,
     d_recv,
     r_send,
     r_recv,
+    *sems,
 ):
     band, row, chip, core = place(bands, rows)
     chips = bands // 2
@@ -650,9 +958,9 @@
     nodes, width = node_buf.shape
     edges = edge_buf.shape[0]
     grids = grid_ref.shape[0]
-    border = border_row_ref.shape[1]
+    border = table.shape[2]
     table_rows = bands * border
-    rows_dev = grads_ref.shape[3]
+    rows_dev = grads_ref.shape[1]
     weights = Weights(full_ref, stage, high, low, stage_sem)
     sibling = (chip * 2 + 1 - core, row)
     partners = [((chip + j) % chips * 2 + core, row) for j in range(1, chips)] + [sibling]
@@ -696,7 +1004,7 @@
             total = total + land[e % 2, j - 1]
         for j in range(1, chips):
             to_band(e, j).wait_send()
-        return picked(hot(iota((nodes, border), 0) == border_row_ref[...]), total)
+        return picked(hot(iota((nodes, border), 0) == index_ref[BORDER_ROW : BORDER_ROW + 1, pl.ds(0, border)]), total)
 
     def put_table(value_high, value_low, count):
         side_rows = chips * border
@@ -704,17 +1012,36 @@
             choice = pick_t[pl.ds(nodes + side * side_rows, side_rows), pl.ds(0, count)]
             table[side] = chosen(choice, value_high, value_low).reshape(chips, border, width)
 
+    def grads_of(layer):
+        return grads_buf.at[layer - 1] if layer > 0 else grads_ref
+
+    reducers = [None] + [
+        Spreader(
+            bands,
+            layer - 1,
+            grads_of(layer),
+            sib_grads,
+            land_grads.at[layer - 1],
+            landed_buf,
+            total_ref.at[pl.ds(layer * each, each)],
+            sems,
+        )
+        for layer in range(1, layers)
+    ]
+
     def put_grad(layer, block, value):
-        grads_ref[slot_of(layer * each + block)] = value
+        grads_of(layer)[block] = value
 
     def add_grad(layer, block, value):
-        grads_ref[slot_of(layer * each + block)] += value
+        grads_of(layer)[block] += value
+
+    index_t[...] = index_ref[...].T
 
     def choose_reads(at, size):
         line = iota((size, grids), 0) + at
         counts = jnp.zeros((size, grids), jnp.float32)
-        for way in range(read_ref.shape[0]):
-            counts = counts + jnp.where(line == read_ref[pl.ds(way, 1)], 1.0, 0.0)
+        for way in range(READ_ROW, index_ref.shape[0]):
+            counts = counts + jnp.where(line == index_ref[way : way + 1, pl.ds(0, grids)], 1.0, 0.0)
         return counts.astype(jnp.bfloat16)
 
     def fill_reads(t, carry):
@@ -725,7 +1052,7 @@
     lax.fori_loop(0, (nodes + table_rows) // 64, fill_reads, 0)
 
     def choose_gather(at, size):
-        return hot(iota((size, nodes), 1) == recv_ref[pl.ds(at, size)])
+        return hot(iota((size, nodes), 1) == index_t[pl.ds(at, size), RECV_ROW : RECV_ROW + 1])
 
     fill_rows(gather, choose_gather)
     load(6, layers).wait()
@@ -741,7 +1068,7 @@
     load(6, layers - 1).start()
     weights.load((layers - 1) * each, (6, 4, 5, 3, 0, 1, 2))
     active = silu(reads[...])
-    mask = mask_ref[:, 0:1].astype(jnp.float32)
+    mask = index_t[pl.ds(0, grids), MASK_ROW : MASK_ROW + 1].astype(jnp.float32)
     missed = grid_ref[...] + product(active, dec_ref[...]) - target_ref[...]
     total = jnp.sum(jnp.sum(count_ref[:, :, 0:1, 0:1], axis=0), axis=0)
     masked = mask * missed
@@ -760,8 +1087,8 @@
 
     def choose(at, size):
         line = iota((size, edges), 0) + at
-        sent = line == send_row_ref[...]
-        received = line == recv_row_ref[...] + (nodes + table_rows)
+        sent = line == index_ref[SEND_ROW : SEND_ROW + 1]
+        received = line == index_ref[RECV_ROW : RECV_ROW + 1] + (nodes + table_rows)
         return hot(jnp.logical_or(sent, received))
 
     fill_rows(pick_t, choose, 64)
@@ -782,6 +1109,10 @@
 
         for kind in (3, 4, 5, 6):
             load(kind, layer).wait()
+        if layer + 1 < layers:
+            reducers[layer + 1].pair()
+        if layer + 2 < layers:
+            reducers[layer + 2].reduce()
         grad = node_grad[...]
         norm, scale = normed(update_buf[...])
         put_param(7, column(grad))
@@ -844,18 +1175,22 @@
         lax.fori_loop(0, edges // tile, edge_back, 0)
         put_grad(layer, 2, product(node_buf[:, own_rows], received, TN))
         node_grad[...] += weights.apply(received, 2, NT)
+        if layer > 0:
+            weights.load((layer - 1) * each, (6, 4, 5, 3, 0))
         sender = sender + returned(e)
         put_grad(layer, 1, product(node_buf[:, own_rows], sender, TN))
         node_grad[...] += weights.apply(sender, 1, NT)
         if layer > 0:
             load(6, layer - 1).start()
-            weights.load((layer - 1) * each, (6, 4, 5, 3, 0, 1, 2))
-
+            weights.load((layer - 1) * each, (1, 2))
+            reducers[layer].start()
+
+    reducers[1].reduce()
     embed_load.wait()
     fed_load.wait()
     norm, scale = normed(fed_buf[...])
     fed_grad = normed_back(node_grad[...], norm, scale)
-    feed = hot(iota((grids, nodes), 1) == mask_ref[:, 1:2])
+    feed = hot(iota((grids, nodes), 1) == index_t[pl.ds(0, grids), FEED_ROW : FEED_ROW + 1])
     grad = picked(feed, fed_grad) * silu_back(embed_buf[...])
     small_ref[pl.ds(0, encs)] = product(grid_ref[...], grad, TN)
     small_ref[pl.ds(encs, 8)] = jnp.zeros((8, width), jnp.float32)
@@ -867,19 +1202,24 @@
         return carry
 
     lax.fori_loop(0, edges // tile, embed_tile, 0)
-
-
-def backward(bands, rows, layers, rows_dev, inputs, saved):
+    for layer in range(layers - 1, 0, -1):
+        reducers[layer].relay()
+    for layer in range(1, layers):
+        reducers[layer].finish()
+
+
+def backward(bands, rows, rim, rows_dev, inputs, saved):
     f32, bf16 = jnp.float32, jnp.bfloat16
     dma = pltpu.SemaphoreType.DMA
-    grid, edge, border = inputs[0], inputs[3], inputs[8]
+    grid, edge, index, decoder, params = inputs[0], inputs[2], inputs[3], inputs[5], inputs[6]
+    layers = params.shape[0]
     full = saved[0]
     width = full.shape[2]
     each = full.shape[0] // layers
-    edges, grids, rim = edge.shape[0], grid.shape[0], border.shape[1]
+    edges, grids = edge.shape[0], grid.shape[0]
     nodes = NODE_DEV
     chips = bands // 2
-    decs = inputs[10].shape[1]
+    decs = decoder.shape[1]
     small = grid.shape[1] + 8 + layers * 8 + decs + 8
     small = -(-small // (16 * OWNER_CHIPS)) * 16 * OWNER_CHIPS
     tile = edges // 2
@@ -887,11 +1227,13 @@
     return pl.pallas_call(
         functools.partial(backward_kernel, bands, rows, each, tile),
         out_shape=(
-            jax.ShapeDtypeStruct((2, OWNER_CHIPS, SLOTS, rows_dev, width), f32),
+            jax.ShapeDtypeStruct((each, rows_dev, width), f32),
             jax.ShapeDtypeStruct((small, width), f32),
+            jax.ShapeDtypeStruct((full.shape[0], rows_dev, width), f32),
+            jax.ShapeDtypeStruct((layers - 1, chips - 1, each, rows_dev // 8, width), f32),
         ),
-        in_specs=[VMEM] * 12 + [ANY] * 11 + [VMEM],
-        out_specs=[VMEM, VMEM],
+        in_specs=[VMEM] * 7 + [ANY] * 11 + [VMEM],
+        out_specs=[VMEM, VMEM, ANY, ANY],
         scratch_shapes=[
             pltpu.VMEM((edges, width), f32),
             pltpu.VMEM((edges, width), f32),
@@ -900,6 +1242,7 @@
             node,
             node,
             node,
+            pltpu.VMEM((edges, index.shape[0]), jnp.int32),
             pltpu.VMEM((edges, width), f32),
             node,
             pltpu.VMEM((edges, width), bf16),
@@ -912,13 +1255,17 @@
             pltpu.VMEM((2, chips, rim, width), f32),
             pltpu.VMEM((2, chips, rim, width), f32),
             pltpu.VMEM((2, chips - 1, rim, width), f32),
+            pltpu.VMEM((layers - 1, each, rows_dev, width), f32),
+            pltpu.VMEM((each, rows_dev // 2, width), f32),
+            pltpu.VMEM((each, rows_dev // 8, width), f32),
             dma((2,)),
             dma((10,)),
             dma((layers + 1,)),
             dma((layers + 1,)),
             dma((layers + 1, chips - 1)),
             dma((layers + 1, chips - 1)),
-        ],
+            ]
+        + spreader_sems(layers - 1, chips),
         compiler_params=pltpu.CompilerParams(
             collective_id=2, has_side_effects=True, vmem_limit_bytes=VMEM_BYTES
         ),
@@ -956,23 +1303,27 @@
     lax.fori_loop(0, count, finish, 0)
 
 
+def late_slot(owner, slot):
+    return owner in (0, 3) or (owner == 6 and slot == 0)
+
+
 def tail_kernel(
     bands,
     rows,
-    grad_ref,
+    grads_ref,
     small_ref,
     mom_ref,
+    given_ref,
     total_ref,
     ortho_ref,
     shared_ref,
-    sib_grad,
+    land,
+    grads,
+    sib,
+    landed_buf,
     sib_small,
-    part,
     part_small,
-    land,
     land_small,
-    mine,
-    mine_small,
     held,
     matrix,
     result,
@@ -982,194 +1333,80 @@
     temp,
     later,
     load_sem,
-    sib_send,
-    sib_recv,
-    red_send,
-    red_recv,
-    all_send,
-    all_recv,
-    pass_send,
-    pass_recv,
+    landed_sem,
+    m_pair,
+    m_red_send,
+    m_red_recv,
+    m_out_send,
+    m_out_recv,
+    m_pass,
+    m_keep,
     up_send,
     up_recv,
     down_send,
     down_recv,
+    o_send,
+    o_recv,
+    p_send,
+    p_recv,
     keep_sem,
+    *sems,
 ):
+    band, row, chip, core = place(bands, rows)
     chips = bands // 2
-    band = lax.axis_index("band")
-    row = lax.axis_index("row")
-    chip, core = band // 2, band % 2
+    rows_dev = held.shape[1]
     sibling = (chip * 2 + 1 - core, row)
-    rows_dev = held.shape[1]
-    everyone = chips == OWNER_CHIPS
-
-    def guard(cond, body):
-        if cond is True:
-            body()
-        else:
-            pl.when(cond)(body)
-
-    def owns(at_chip):
-        return True if everyone else at_chip < OWNER_CHIPS
-
-    def both(one, two):
-        if one is True:
-            return two
-        if two is True:
-            return one
-        return jnp.logical_and(one, two)
-
-    def used(at_chip, slot):
-        owner = at_chip * 2 + core
-        return both(owns(at_chip), True if slot in (0, 3) else slot_used(owner, slot))
-
-    barrier = pltpu.get_barrier_semaphore()
     partners = [((chip + j) % chips * 2 + core, row) for j in range(1, chips)] + [sibling]
     partners += [(band, (row + j) % rows) for j in range(1, rows)]
-    for partner in partners:
-        pl.semaphore_signal(barrier, inc=1, device_id=partner, device_id_type=MESH)
-    pl.semaphore_wait(barrier, len(partners))
-
-    first = remote(grad_ref.at[1 - core], sib_grad, sib_send.at[0], sib_recv.at[0], sibling)
-    second = remote(small_ref.at[1 - core], sib_small, sib_send.at[1], sib_recv.at[1], sibling)
-    first.start()
-    second.start()
-    owner = band
+    reducer = Reducer(bands, 0, 0, grads, sib.at[0], land, total_ref.at[pl.ds(0, grads.shape[0])], sems)
+    grads[...] = grads_ref[...]
 
     def load(slot):
         return pltpu.make_async_copy(
-            mom_ref.at[slot_block(owner, slot)], held.at[slot], load_sem.at[slot]
-        )
-
+            mom_ref.at[slot_block(band, slot)], held.at[slot], load_sem.at[slot]
+        )
+
+    owned = [band < (8, 7, 6)[slot] for slot in range(SLOTS)]
+    third = band // 3
+    last = [jnp.logical_and(band < 7, band % 3 == 0)]
+    last += [jnp.logical_and(band < 6, band % 3 == 0)] * 2
     for slot in range(SLOTS):
-        guard(used(chip, slot), lambda slot=slot: load(slot).start())
-    first.wait()
-    second.wait()
-    for at in range(OWNER_CHIPS):
-        part[at] = grad_ref[core, at] + sib_grad[at]
-    part_small[...] = small_ref[core] + sib_small[...]
-
-    def to_owner(j):
-        to = (chip + j) % chips
-        return (
-            remote(part.at[to], land.at[j - 1], red_send.at[j - 1, 0], red_recv.at[j - 1, 0], (to * 2 + core, row)),
-            remote(part_small.at[to], land_small.at[j - 1], red_send.at[j - 1, 1], red_recv.at[j - 1, 1], (to * 2 + core, row)),
-        )
-
-    for j in range(1, chips):
-        def send(j=j):
-            for copy in to_owner(j):
-                copy.start()
-
-        guard(owns((chip + j) % chips), send)
-
-    def reduce():
-        mine[...] = part[chip]
-        mine_small[...] = part_small[chip]
-        for j in range(1, chips):
-            for copy in to_owner(j):
-                copy.wait_recv()
-            mine[...] += land[j - 1]
-            mine_small[...] += land_small[j - 1]
-
-    guard(owns(chip), reduce)
-
-    def source(kind, slot):
-        if slot == 3:
-            return mine_small
-        return (mine, back)[kind].at[slot]
-
-    def target(kind, slot, at_chip, at_core):
-        at_owner = at_chip * 2 + at_core
-        if slot == 3:
-            return shared_ref.at[at_core * OWNER_CHIPS + at_chip]
-        return (total_ref, ortho_ref)[kind].at[slot_block(at_owner, slot)]
-
-    def keep(kind, slot):
+        pl.when(owned[slot])(load(slot).start)
+    meet(partners)
+
+    small_pair = remote(small_ref.at[1 - core], sib_small, m_pair.at[0], m_pair.at[1], sibling)
+
+    def small_to(at):
+        step = (at - chip + chips) % chips
+        return remote(
+            part_small.at[at],
+            land_small.at[step - 1],
+            m_red_send.at[at],
+            m_red_recv.at[step - 1],
+            (at * 2 + core, row),
+        )
+
+    def small_out(at, j):
+        home = shared_ref.at[core * OWNER_CHIPS + at]
+        return remote(
+            part_small.at[at],
+            home,
+            m_out_send.at[j - 1],
+            m_out_recv.at[at],
+            ((chip + j) % chips * 2 + core, row),
+        )
+
+    def small_across(at, of_core, local):
+        home = shared_ref.at[of_core * OWNER_CHIPS + at]
+        return remote(
+            part_small.at[at] if local else home, home, m_pass.at[0, at], m_pass.at[1, at], sibling
+        )
+
+    def small_keep(at):
         return pltpu.make_async_copy(
-            source(kind, slot), target(kind, slot, chip, core), keep_sem.at[kind, slot]
-        )
-
-    def out(kind, slot, j):
-        return remote(
-            source(kind, slot),
-            target(kind, slot, chip, core),
-            all_send.at[kind, j - 1, slot],
-            all_recv.at[kind, j - 1, slot],
-            ((chip + j) % chips * 2 + core, row),
-        )
-
-    def across(kind, slot, at_chip, j):
-        src = source(kind, slot) if j == 0 else target(kind, slot, at_chip, core)
-        return remote(
-            src,
-            target(kind, slot, at_chip, core),
-            pass_send.at[kind, j, slot],
-            pass_recv.at[kind, j, slot],
-            sibling,
-        )
-
-    def crossed(kind, slot, at_chip, j):
-        return remote(
-            source(kind, slot),
-            target(kind, slot, at_chip, 1 - core),
-            pass_send.at[kind, j, slot],
-            pass_recv.at[kind, j, slot],
-            sibling,
-        )
-
-    def used_other(at_chip, slot):
-        at_owner = at_chip * 2 + 1 - core
-        return both(owns(at_chip), True if slot in (0, 3) else slot_used(at_owner, slot))
-
-    def publish(kind, slots):
-        for slot in slots:
-            def start(slot=slot):
-                for j in range(1, chips):
-                    out(kind, slot, j).start()
-                keep(kind, slot).start()
-                across(kind, slot, chip, 0).start()
-
-            guard(used(chip, slot), start)
-
-    def relay(kind, slots):
-        for j in range(1, chips):
-            origin = (chip - j + chips) % chips
-            for slot in slots:
-                def start(slot=slot, j=j, origin=origin):
-                    remote(
-                        source(kind, slot),
-                        target(kind, slot, origin, core),
-                        all_send.at[kind, j - 1, slot],
-                        all_recv.at[kind, j - 1, slot],
-                        (origin * 2 + core, row),
-                    ).wait_recv()
-                    across(kind, slot, origin, j).start()
-
-                guard(used(origin, slot), start)
-
-    def settle(kind, slots):
-        for j in range(chips):
-            origin = (chip - j + chips) % chips
-            for slot in slots:
-                def finish(slot=slot, j=j, origin=origin):
-                    across(kind, slot, origin, j).wait_send()
-
-                def arrive(slot=slot, j=j, origin=origin):
-                    crossed(kind, slot, origin, j).wait_recv()
-
-                guard(used(origin, slot), finish)
-                guard(used_other(origin, slot), arrive)
-        for slot in slots:
-            def sent(slot=slot):
-                for j in range(1, chips):
-                    out(kind, slot, j).wait_send()
-                keep(kind, slot).wait()
-
-            guard(used(chip, slot), sent)
-
-    third = owner // 3
+            part_small.at[at], shared_ref.at[core * OWNER_CHIPS + at], m_keep
+        )
+
     row_a = rows // 2 - 1 + core
     row_b = rows // 2 - core
     split_at = 3 - third
@@ -1177,98 +1414,215 @@
     def home(slot):
         if slot == 0:
             return row_a
-        late = (slot + third) // 3
-        return row_a + late * (row_b - row_a)
+        return row_a + (slot + third) // 3 * (row_b - row_a)
+
+    def rows_of(at_row):
+        return pl.ds(pl.multiple_of(at_row * rows_dev, rows_dev), rows_dev)
 
     def up(slot, from_row):
-        at = pl.ds(pl.multiple_of(from_row * rows_dev, rows_dev), rows_dev)
         step = (from_row - home(slot) + rows) % rows
         return remote(
             held.at[slot],
-            matrix.at[slot, at],
+            matrix.at[slot, rows_of(from_row)],
             up_send.at[slot],
             up_recv.at[slot, step],
             (band, home(slot)),
         )
 
-    for slot in range(SLOTS):
-        def momentum(slot=slot):
-            load(slot).wait()
-            held[slot] = momentum_decay * held[slot] + mine[slot]
-
-            @pl.when(row == home(slot))
-            def _():
-                at = pl.ds(pl.multiple_of(row * rows_dev, rows_dev), rows_dev)
-                matrix[slot, at] = held[slot]
-
-            @pl.when(row != home(slot))
-            def _():
-                up(slot, row).start()
-
-        guard(used(chip, slot), momentum)
-    publish(0, (0, 1, 2, 3))
-
     def down(slot, to_row):
-        at = pl.ds(pl.multiple_of(to_row * rows_dev, rows_dev), rows_dev)
         step = (to_row - home(slot) + rows) % rows
         return remote(
-            result.at[slot, at],
+            result.at[slot, rows_of(to_row)],
             back.at[slot],
             down_send.at[slot, step],
             down_recv.at[slot],
             (band, to_row),
         )
 
+    def momentum(slot, value):
+        load(slot).wait()
+        held[slot] = momentum_decay * held[slot] + value
+
+        @pl.when(row == home(slot))
+        def _():
+            matrix[slot, rows_of(row)] = held[slot]
+
+        @pl.when(row != home(slot))
+        def _():
+            up(slot, row).start()
+
+    def solve(when):
+        own_b = jnp.logical_and(row == row_b, jnp.logical_and(band > 2, band < 7))
+        own_b = jnp.logical_and(own_b, jnp.logical_not(band == 3) if when == 0 else band == 3)
+        own_a = jnp.logical_and(row == row_a, band < 8)
+        own_a = jnp.logical_and(own_a, jnp.logical_not(last[0]) if when == 0 else last[0])
+
+        @pl.when(jnp.logical_or(own_a, own_b))
+        def _():
+            second = (row - row_a) * (row_b - row_a)
+            first = second * split_at
+            count = (1 - second) * split_at + second
+            for slot in range(SLOTS):
+                @pl.when(jnp.logical_and(slot >= first, slot < first + count))
+                def _():
+                    for step in range(1, rows):
+                        up(slot, (row + step) % rows).wait_recv()
+
+            newton(matrix, result, first, count, gram, poly, temp, later)
+            for slot in range(SLOTS):
+                @pl.when(jnp.logical_and(slot >= first, slot < first + count))
+                def _():
+                    for step in range(1, rows):
+                        down(slot, (row + step) % rows).start()
+                    back[slot] = result[slot, rows_of(row)]
+
+    units = [
+        (owner, slot)
+        for owner in range(2 * OWNER_CHIPS)
+        for slot in range(SLOTS)
+        if slot_used(owner, slot)
+    ]
+
+    def target(owner, slot):
+        return ortho_ref.at[slot_block(owner, slot)]
+
+    def out(owner, slot, j):
+        return remote(
+            back.at[slot],
+            target(owner, slot),
+            o_send.at[slot, j - 1],
+            o_recv.at[owner // 2, slot],
+            ((chip + j) % chips * 2 + core, row),
+        )
+
+    def across(owner, slot, local):
+        return remote(
+            back.at[slot] if local else target(owner, slot),
+            target(owner, slot),
+            p_send.at[owner // 2, slot],
+            p_recv.at[owner // 2, slot],
+            sibling,
+        )
+
+    def keep(owner, slot):
+        return pltpu.make_async_copy(back.at[slot], target(owner, slot), keep_sem.at[slot])
+
+    def publish(when):
+        for owner, slot in units:
+            if late_slot(owner, slot) != (when == 1):
+                continue
+
+            @pl.when(band == owner)
+            def _():
+                @pl.when(row != home(slot))
+                def _():
+                    down(slot, row).wait_recv()
+
+                for j in range(1, chips):
+                    out(owner, slot, j).start()
+                across(owner, slot, True).start()
+                keep(owner, slot).start()
+
+    def relay(when):
+        for owner, slot in units:
+            if late_slot(owner, slot) != (when == 1):
+                continue
+
+            @pl.when(jnp.logical_and(core == owner % 2, chip != owner // 2))
+            def _():
+                out(owner, slot, 1).wait_recv()
+                across(owner, slot, False).start()
+
+    reducer.start()
+    small_pair.start()
     for slot in range(SLOTS):
-        def arrived(slot=slot):
-            @pl.when(row == home(slot))
-            def _():
-                for step in range(1, rows):
-                    up(slot, (row + step) % rows).wait_recv()
-
-        guard(used(chip, slot), arrived)
-
-    def at_a():
-        newton(matrix, result, 0, split_at, gram, poly, temp, later)
-
-    def at_b():
-        newton(matrix, result, split_at, 1, gram, poly, temp, later)
-
-    guard(both(owns(chip), row == row_a), at_a)
-    guard(
-        both(owns(chip), jnp.logical_and(row == row_b, jnp.logical_and(owner > 2, owner < 7))), at_b
-    )
-
-    for slot in range(SLOTS):
-        def give(slot=slot):
-            @pl.when(row == home(slot))
-            def _():
-                for step in range(1, rows):
-                    down(slot, (row + step) % rows).start()
-                at = pl.ds(pl.multiple_of(row * rows_dev, rows_dev), rows_dev)
-                back[slot] = result[slot, at]
-
-        guard(used(chip, slot), give)
-    relay(0, (0, 1, 2, 3))
-    for slot in range(SLOTS):
-        def take(slot=slot):
-            @pl.when(row != home(slot))
-            def _():
-                down(slot, row).wait_recv()
-
-        guard(used(chip, slot), take)
-    publish(1, (0, 1, 2))
-    relay(1, (0, 1, 2))
-    settle(0, (0, 1, 2, 3))
-    settle(1, (0, 1, 2))
-    for j in range(1, chips):
-        def reduced(j=j):
-            for copy in to_owner(j):
-                copy.wait_send()
-
-        guard(owns((chip + j) % chips), reduced)
-    for slot in range(SLOTS):
-        def closed(slot=slot):
+        @pl.when(jnp.logical_and(owned[slot], jnp.logical_not(last[slot])))
+        def _():
+            ready = pltpu.make_async_copy(
+                total_ref.at[slot_block(band, slot)], back.at[slot], load_sem.at[SLOTS + slot]
+            )
+            ready.start()
+            ready.wait()
+            momentum(slot, back[slot])
+
+    reducer.pair()
+    small_pair.wait()
+    part_small[...] = small_ref[core] + sib_small[...]
+    for at in range(OWNER_CHIPS):
+        pl.when(chip != at)(small_to(at).start)
+    solve(0)
+
+    def take(slot, count, value):
+        for n in range(count):
+            momentum(slot + n, value[n])
+
+    def load_landed(src, count):
+        dst = landed_buf.at[pl.ds(0, count)]
+        copy = pltpu.make_async_copy(src, dst, landed_sem)
+        copy.start()
+        copy.wait()
+        return dst[...]
+
+    reducer.reduce(take, load_landed)
+    for at in range(OWNER_CHIPS):
+        @pl.when(chip == at)
+        def _():
+            for j in range(1, chips):
+                remote(
+                    land_small.at[j - 1],
+                    land_small.at[j - 1],
+                    m_red_send.at[at],
+                    m_red_recv.at[j - 1],
+                    sibling,
+                ).wait_recv()
+                part_small[at] += land_small[j - 1]
+            for j in range(1, chips):
+                small_out(at, j).start()
+            small_across(at, core, True).start()
+            small_keep(at).start()
+
+    publish(0)
+    solve(1)
+    reducer.relay()
+    for at in range(OWNER_CHIPS):
+        @pl.when(chip != at)
+        def _():
+            small_out(at, 1).wait_recv()
+            small_across(at, core, False).start()
+
+    publish(1)
+    relay(0)
+    relay(1)
+    reducer.finish()
+    for at in range(OWNER_CHIPS):
+        small_across(at, core, False).wait_send()
+        small_across(at, 1 - core, False).wait_recv()
+
+        @pl.when(chip != at)
+        def _():
+            small_to(at).wait_send()
+
+        @pl.when(chip == at)
+        def _():
+            for j in range(1, chips):
+                small_out(at, j).wait_send()
+            small_keep(at).wait()
+
+    for owner, slot in units:
+        @pl.when(core == owner % 2)
+        def _():
+            across(owner, slot, False).wait_send()
+
+        @pl.when(core != owner % 2)
+        def _():
+            across(owner, slot, False).wait_recv()
+
+        @pl.when(band == owner)
+        def _():
+            for j in range(1, chips):
+                out(owner, slot, j).wait_send()
+            keep(owner, slot).wait()
+
             @pl.when(row != home(slot))
             def _():
                 up(slot, row).wait_send()
@@ -1278,67 +1632,173 @@
                 for step in range(1, rows):
                     down(slot, (row + step) % rows).wait_send()
 
-        guard(used(chip, slot), closed)
-
-
-def tail(bands, rows, grads, small, momentum):
+
+def tail(bands, rows, grads, small, momentum, given):
     blocks, rows_dev, width = momentum.shape
+    each = grads.shape[0]
     chips = bands // 2
     chunk = small.shape[2]
     f32 = jnp.float32
     dma = pltpu.SemaphoreType.DMA
     square = pltpu.VMEM((width, width), f32)
+    slots = pltpu.VMEM((SLOTS, rows_dev, width), f32)
     return pl.pallas_call(
         functools.partial(tail_kernel, bands, rows),
         out_shape=(
-            jax.ShapeDtypeStruct((blocks, rows_dev, width), f32),
+            jax.ShapeDtypeStruct(given.shape, f32),
             jax.ShapeDtypeStruct((blocks, rows_dev, width), f32),
             jax.ShapeDtypeStruct((2 * OWNER_CHIPS, chunk, width), f32),
+            jax.ShapeDtypeStruct((1, chips - 1, SLOTS, rows_dev, width), f32),
         ),
-        in_specs=[VMEM, VMEM, ANY],
-        out_specs=[ANY, ANY, ANY],
+        in_specs=[VMEM, VMEM, ANY, ANY],
+        out_specs=[ANY, ANY, ANY, ANY],
+        input_output_aliases={3: 0},
         scratch_shapes=[
-            pltpu.VMEM((OWNER_CHIPS, SLOTS, rows_dev, width), f32),
+            pltpu.VMEM((each, rows_dev, width), f32),
+            pltpu.VMEM((1, each, rows_dev, width), f32),
+            slots,
             pltpu.VMEM((OWNER_CHIPS, chunk, width), f32),
-            pltpu.VMEM((OWNER_CHIPS, SLOTS, rows_dev, width), f32),
             pltpu.VMEM((OWNER_CHIPS, chunk, width), f32),
-            pltpu.VMEM((chips - 1, SLOTS, rows_dev, width), f32),
             pltpu.VMEM((chips - 1, chunk, width), f32),
-            pltpu.VMEM((SLOTS, rows_dev, width), f32),
-            pltpu.VMEM((chunk, width), f32),
-            pltpu.VMEM((SLOTS, rows_dev, width), f32),
+            slots,
             pltpu.VMEM((SLOTS, width, width), f32),
             pltpu.VMEM((SLOTS, width, width), f32),
-            pltpu.VMEM((SLOTS, rows_dev, width), f32),
+            slots,
             square,
             square,
             square,
             square,
-            dma((SLOTS,)),
+            dma((2 * SLOTS,)),
+            dma,
             dma((2,)),
-            dma((2,)),
-            dma((chips - 1, 2)),
-            dma((chips - 1, 2)),
-            dma((2, chips - 1, SLOTS + 1)),
-            dma((2, chips - 1, SLOTS + 1)),
-            dma((2, chips, SLOTS + 1)),
-            dma((2, chips, SLOTS + 1)),
+            dma((OWNER_CHIPS,)),
+            dma((chips - 1,)),
+            dma((chips - 1,)),
+            dma((OWNER_CHIPS,)),
+            dma((2, OWNER_CHIPS)),
+            dma,
             dma((SLOTS,)),
             dma((SLOTS, rows)),
             dma((SLOTS, rows)),
             dma((SLOTS,)),
-            dma((2, SLOTS + 1)),
-        ],
+            dma((SLOTS, chips - 1)),
+            dma((OWNER_CHIPS, SLOTS)),
+            dma((OWNER_CHIPS, SLOTS)),
+            dma((OWNER_CHIPS, SLOTS)),
+            dma((SLOTS,)),
+        ]
+        + reducer_sems(1, chips),
         compiler_params=pltpu.CompilerParams(
             collective_id=0, has_side_effects=True, vmem_limit_bytes=VMEM_BYTES
         ),
         name="tail",
-    )(grads, small, momentum)
-
-
-def muon_finish(weights, ortho):
-    scales = jnp.array(block_scale, dtype=weights.dtype)[None, :, None, None]
-    return weights * (1.0 - muon_rate * weight_decay) - muon_rate * scales * ortho
+    )(grads, small, momentum, given)
+
+
+def finish_kernel(
+    shapes,
+    channels,
+    edge_channels,
+    w_ref,
+    average_ref,
+    mom_ref,
+    total_ref,
+    ortho_ref,
+    small_ref,
+    count_ref,
+    enc_ref,
+    enc_first_ref,
+    enc_second_ref,
+    dec_ref,
+    dec_first_ref,
+    dec_second_ref,
+    param_ref,
+    param_first_ref,
+    param_second_ref,
+    loss_ref,
+    total_count_ref,
+    new_w_ref,
+    new_mom_ref,
+    new_average_ref,
+    enc_outs,
+    dec_outs,
+    param_outs,
+):
+    wide, params_at, decoder_at, loss_at = shapes
+    step = pl.program_id(0)
+    for n in range(w_ref.shape[0]):
+        block = lax.rem(step * w_ref.shape[0] + n, len(block_scale))
+        scale = jnp.where(block < 3, block_scale[0], jnp.where(block == 4, block_scale[4], 1.0))
+        scale = jnp.where(block == 5, block_scale[5], scale)
+        fresh = w_ref[n] * (1.0 - muon_rate * weight_decay) - (muon_rate * scale) * ortho_ref[n]
+        new_w_ref[n] = fresh
+        new_average_ref[n] = average_decay * average_ref[n] + (1.0 - average_decay) * fresh
+        new_mom_ref[n] = momentum_decay * mom_ref[n] + total_ref[n]
+
+    def put(outs, at, values):
+        for ref, value in zip(outs, values):
+            ref[at] = value
+
+    @pl.when(step == 0)
+    def _():
+        for at, grad in (
+            (pl.ds(0, channels), small_ref[pl.ds(0, channels)]),
+            (pl.ds(channels, edge_channels), small_ref[pl.ds(wide, edge_channels)]),
+        ):
+            put(enc_outs, at, adam_update(enc_ref[at], enc_first_ref[at], enc_second_ref[at], grad, adam_rate))
+        grad = small_ref[pl.ds(decoder_at, channels)]
+        put(dec_outs, ..., adam_update(dec_ref[...], dec_first_ref[...], dec_second_ref[...], grad, adam_rate))
+        for layer in range(param_ref.shape[0]):
+            grad = small_ref[pl.ds(params_at + layer * 8, 8)]
+            put(
+                param_outs,
+                layer,
+                adam_update(param_ref[layer], param_first_ref[layer], param_second_ref[layer], grad, param_rate),
+            )
+        loss_ref[...] = small_ref[pl.ds(loss_at, 1), 0:1]
+        total_count_ref[...] = jnp.sum(jnp.sum(count_ref[:, :, 0:1, 0:1], axis=0), axis=0)
+
+
+def finish(shapes, edge_channels, blocks, small, counts, encoder, decoder, params):
+    f32 = jnp.float32
+    channels = decoder[0].shape[0]
+    big = blocks[0]
+    tiled = pl.BlockSpec((SLOTS,) + big.shape[1:], lambda i: (i, 0, 0))
+
+    def whole(value):
+        return pl.BlockSpec(value.shape, lambda i: (0,) * value.ndim)
+
+    def like(value):
+        return jax.ShapeDtypeStruct(value.shape, f32)
+
+    scalar = jax.ShapeDtypeStruct((1, 1), f32)
+    return pl.pallas_call(
+        functools.partial(finish_kernel, shapes, channels, edge_channels),
+        grid=(big.shape[0] // SLOTS,),
+        out_shape=(
+            scalar,
+            scalar,
+            like(big),
+            like(big),
+            like(big),
+            (like(encoder[0]),) * 3,
+            (like(decoder[0]),) * 3,
+            (like(params[0]),) * 3,
+        ),
+        in_specs=[tiled] * 5 + [whole(value) for value in (small, counts, *encoder, *decoder, *params)],
+        out_specs=(
+            whole(scalar),
+            whole(scalar),
+            tiled,
+            tiled,
+            tiled,
+            (whole(encoder[0]),) * 3,
+            (whole(decoder[0]),) * 3,
+            (whole(params[0]),) * 3,
+        ),
+        compiler_params=pltpu.CompilerParams(vmem_limit_bytes=VMEM_BYTES),
+        name="finish",
+    )(*blocks, small, counts, *encoder, *decoder, *params)
 
 
 def adam_update(values, first, second, gradient, rate):
@@ -1385,28 +1845,20 @@
         pads[axis] = (0, size - value.shape[axis])
         return jnp.pad(value, pads)
 
-    def table_place(index):
-        owner, spot = (index - NODE_DEV) // rim, (index - NODE_DEV) % rim
-        moved = NODE_DEV + (owner % 2 * (bands // 2) + owner // 2) * rim + spot
-        return jnp.where(index < NODE_DEV, index, moved)
-
-    sent = table_place(senders)
-    reads = table_place(mesh_to_grid).reshape(grids, -1).T
+    reads = mesh_to_grid.reshape(grids, -1).T
+    indices = tuple(
+        value[None, :] for value in (senders, receivers, border_nodes, grid_to_mesh, loss_mask)
+    ) + (reads,)
     grid_wide = widen(grid_input, wide, 1)
     edge_wide = widen(edge_input, 128, 1)
     edge_embed = widen(encoder_weights[channels:], 128, 0)
     flat_weights = processor_weights.reshape(layers * blocks, rows_dev, width)
-    saved = forward(
+    *saved, index = forward(
         bands,
         rows,
-        layers,
         grid_wide,
         edge_wide,
-        sent,
-        receivers,
-        border_nodes,
-        grid_to_mesh,
-        loss_mask,
+        indices,
         flat_weights,
         widen(encoder_weights[:channels], wide, 0),
         edge_embed,
@@ -1415,44 +1867,40 @@
     inputs = (
         grid_wide,
         widen(grid_target, wide, 1),
-        jnp.stack([loss_mask, grid_to_mesh], axis=1),
         edge_wide,
-        reads,
-        sent[None, :],
-        receivers[None, :],
-        receivers[:, None],
-        border_nodes[None, :],
+        index,
         edge_embed,
         widen(decoder_weights, wide, 1),
         norm_params,
     )
-    grads, small = backward(bands, rows, layers, rows_dev, inputs, saved)
-    mask_count = jnp.sum(saved[-1][:, :, 0, 0])
-    total, ortho, small = tail(
+    grads, small, total, _ = backward(bands, rows, rim, rows_dev, inputs, saved)
+    flat_momentum = processor_momentum.reshape(layers * blocks, rows_dev, width)
+    total, ortho, small, _ = tail(
         bands,
         rows,
         grads,
         small.reshape(2, OWNER_CHIPS, -1, width),
-        processor_momentum.reshape(layers * blocks, rows_dev, width),
+        flat_momentum,
+        total,
     )
-    small = small.reshape(-1, width)
     params_at = wide + 8
     decoder_at = params_at + layers * 8
-    encoder_grad = jnp.concatenate([small[:channels], small[wide : wide + edge_channels]])
-    param_grad = small[params_at:decoder_at].reshape(norm_params.shape)
-    decoder_grad = small[decoder_at : decoder_at + channels].T
-    loss_total = small[decoder_at + wide, 0]
-    next_momentum = momentum_decay * processor_momentum + total.reshape(processor_weights.shape)
-    next_weights = muon_finish(processor_weights, ortho.reshape(processor_weights.shape))
-    next_average = average_decay * processor_average + (1.0 - average_decay) * next_weights
-    param_moment, param_square, param_values = adam_update(
-        norm_params, norm_first, norm_second, param_grad, param_rate
+    loss_total, mask_count, next_weights, next_momentum, next_average, encoder, decoder, params = finish(
+        (wide, params_at, decoder_at, decoder_at + wide),
+        edge_channels,
+        (flat_weights, processor_average.reshape(flat_momentum.shape), flat_momentum, total, ortho),
+        small.reshape(-1, width),
+        saved[-1],
+        (encoder_weights, encoder_first, encoder_second),
+        (decoder_weights.T, decoder_first.T, decoder_second.T),
+        (norm_params, norm_first, norm_second),
     )
-    encoder_moment, encoder_square, encoder_values = adam_update(
-        encoder_weights, encoder_first, encoder_second, encoder_grad, adam_rate
-    )
-    decoder_moment, decoder_square, decoder_values = adam_update(
-        decoder_weights, decoder_first, decoder_second, decoder_grad, adam_rate
+    encoder_moment, encoder_square, encoder_values = encoder
+    decoder_moment, decoder_square, decoder_values = (value.T for value in decoder)
+    param_moment, param_square, param_values = params
+    loss_total, mask_count = loss_total[0, 0], mask_count[0, 0]
+    next_weights, next_momentum, next_average = (
+        value.reshape(processor_weights.shape) for value in (next_weights, next_momentum, next_average)
     )
     return (
         loss_total,

time: 462 us -> 412 us (0.89)
  Pallas kernels: 415 us -> 388 us
  other arithmetic: 22.4 us -> 0 us
    pallas_call x1, Pallas kernels: 143 us -> 108 us  [tail(): pl.pallas_call(functools.partial(tail_kernel, bands, rows), out_shape=(ja...]
    pallas_call x1, Pallas kernels: 159 us -> 130 us  [forward(): pl.pallas_call(functools.partial(forward_kernel, bands, rows, tuple(chunk...]
    pallas_call x0 -> x1, Pallas kernels: none -> 20.1 us  [finish(): pl.pallas_call(functools.partial(finish_kernel, shapes, channels, edge_ch...]
    add x1 -> x0, other arithmetic: 15.8 us -> none  [body(): average_decay * processor_average + (1.0 - average_decay) * next_weights]
    pallas_call x1, Pallas kernels: 114 us -> 129 us  [backward(): pl.pallas_call(functools.partial(backward_kernel, bands, rows, each, tile...]
    sub x3 -> x0, other arithmetic: 5.16 us -> none  [adam_update(): values * (1.0 - rate * weight_decay) - rate * corrected]
where the time goes in v3:
time: 412 us; the launch traced here: 403 us
  Pallas kernels  388 us (94%)
  local copies, waits for them, and re-layouts  14.5 us (4%)
    pallas_call x1, Pallas kernels, forward(): pl.pallas_call(functools.partial(forward_kernel, bands, rows, tuple(chunk...  130 us
    pallas_call x1, Pallas kernels, backward(): pl.pallas_call(functools.partial(backward_kernel, bands, rows, each, tile...  129 us
    pallas_call x1, Pallas kernels, tail(): pl.pallas_call(functools.partial(tail_kernel, bands, rows), out_shape=(ja...  108 us
    pallas_call x1, Pallas kernels, finish(): pl.pallas_call(functools.partial(finish_kernel, shapes, channels, edge_ch...  20.1 us

profile of v3, /device:TPU:0, one launch (start us, length us, event | category | flops | bytes accessed | tf_op | source)
XLA Modules:
  0.0 403.4 jit_solution(1422443726520116041)
XLA Ops:
  0.6 0.0 copy-start.1
  0.7 0.0 copy-start
  0.7 1.4 broadcast_in_dim.15.send_ref
  2.1 1.3 broadcast_in_dim.16.recv_ref
  3.4 0.7 slice.7
  4.1 0.7 pad.27.enc_edge_ref
  4.8 1.1 reshape.58
  5.9 0.8 copy.43
  6.7 1.9 pad.26.enc_ref
  8.6 1.2 copy.44
  9.8 0.8 pad.28.dec_ref
  10.6 1.0 copy.42
  11.6 0.9 pad.25.edge_ref
  12.5 0.0 copy-done
  12.5 0.3 copy.40
  12.8 1.0 pad.23.grid_ref
  13.8 0.0 copy-done.1
  13.8 0.3 copy.41
  14.2 1.0 pad.24.target_ref
  15.2 130.0 %forward.1 = (f32[21,512,512]{2,1,0:T(8,128)}, f32[3,1280,512]{2,1,0:T(8,128)}, f32[3,1280,512]{2,1,0:T(8,128)}, f32[3,1280,512]{2,1,0:T(8,128)}, f32[960,512]{1...) custom-call(f32[960,256]{1,0:T(8,128)} %pad.23.grid_ref, ...), custom_call_target="tpu_custom_call" | custom-call | tf_op jit(solution)/shard_map/forward/pallas_call | solution.py:561
  145.2 129.4 %backward.1 = (f32[7,128,512]{2,1,0:T(8,128)}, f32[576,512]{1,0:T(8,128)}, f32[21,128,512]{2,1,0:T(8,128)}, f32[2,3,7,16,512]{4,3,2,1,0:T(8,128)}) custom-call(f32[960,256]{1,0:T(8,128)} %pad.23.grid_ref, f32[960,256]{1,0:T(8,128)} %pad.24.target_ref, f32[1280,128]{1,0:T(8,128)} %pad.25.edge_ref, s32[8,1280]{1,0:T(8,128)} %get-tuple-element.47.index_ref, ...), custom_call_target="tpu_custom_call" | custom-call | tf_op jit(solution)/shard_map/backward/pallas_call | solution.py:1227
  274.6 108.5 %tail.1 = (f32[21,128,512]{2,1,0:T(8,128)}, f32[21,128,512]{2,1,0:T(8,128)}, f32[8,72,512]{2,1,0:T(8,128)}, f32[1,3,3,128,512]{4,3,2,1,0:T(8,128)}) custom-call(f32[7,128,512]{2,1,0:T(8,128)} %get-tuple-element.60.grads_ref, f32[2,4,72,512]{3,2,1,0:T(8,128)} %bitcast.29, f32[21,128,512]{2,1,0:T(8,128)} %bitcast.23, ...), custom_call_target="tpu_custom_call", output_to_operand_aliasing={{0}: (3, {})} | custom-call | tf_op jit(solution)/shard_map/tail/pallas_call | solution.py:1645
  383.1 20.1 %finish.1 = (f32[1,1]{1,0:T(1,128)}, f32[1,1]{1,0:T(1,128)}, f32[21,128,512]{2,1,0:T(8,128)}, f32[21,128,512]{2,1,0:T(8,128)}, f32[21,128,512]{2,1,0:T(8,128)}, ...) custom-call(f32[21,128,512]{2,1,0:T(8,128)} %bitcast.22, ...), custom_call_target="tpu_custom_call" | custom-call | tf_op jit(solution)/shard_map/finish/pallas_call | solution.py:1775
Async XLA Ops:
  0.6 13.2 %copy-start.1 = (f32[960,227]{0,1:T(8,128)S(1)}, f32[960,227]{0,1:T(8,128)}, u32[]{:S(2)}) copy-start(f32[960,227]{0,1:T(8,128)} %param.22) | copy-start | bytes 2615044
  0.7 11.8 %copy-start = (f32[960,227]{0,1:T(8,128)S(1)}, f32[960,227]{0,1:T(8,128)}, u32[]{:S(2)}) copy-start(f32[960,227]{0,1:T(8,128)} %param.21) | copy-start | bytes 2615044

commit v4 on v3

--- a/solution.py
+++ b/solution.py
@@ -132,6 +132,18 @@
 SEND_ROW, RECV_ROW, BORDER_ROW, FEED_ROW, MASK_ROW, READ_ROW = range(6)
 
 
+def edge_rows(edge_ref, size):
+    empty = jnp.zeros((size - edge_ref.shape[0], edge_ref.shape[1]), jnp.float32)
+    return jnp.concatenate([edge_ref[...], empty], axis=0)
+
+
+def embedded_edges(edge_t, enc_ref, first, count, at, size):
+    total = edge_t[pl.ds(at, size), 0:1] * enc_ref[pl.ds(first, 1)]
+    for n in range(1, count):
+        total = total + edge_t[pl.ds(at, size), n : n + 1] * enc_ref[pl.ds(first + n, 1)]
+    return total
+
+
 class Weights:
     def __init__(self, full_ref, stage, high, low, sem):
         self.full, self.stage, self.high, self.low, self.sem = full_ref, stage, high, low, sem
@@ -179,15 +191,13 @@
     tile,
     grid_ref,
     edge_ref,
-    send_ref,
-    recv_ref,
+    ends_ref,
     border_ref,
     feed_ref,
     mask_ref,
     read_ref,
     w_ref,
     enc_ref,
-    enc_edge_ref,
     param_ref,
     full_ref,
     before_ref,
@@ -206,6 +216,7 @@
     before_buf,
     message_buf,
     index_t,
+    edge_t,
     pick,
     gather_t,
     src_high,
@@ -239,7 +250,7 @@
     nodes, width = fed_ref.shape
     edges = edge_buf.shape[1]
     border = border_buf.shape[1]
-    grids = grid_ref.shape[0]
+    grids = grid_ref.shape[1]
     weights = Weights(full_ref, stage, high, low, stage_sem)
     quad, pos = chip // 4, chip % 4
     pos_x, pos_y = pos + 1 - 2 * (pos % 2), pos + 2 - 4 * (pos // 2)
@@ -398,15 +409,16 @@
         return jnp.where(index < nodes, index, moved.astype(jnp.int32) + nodes)
 
     index_ref[...] = jnp.zeros_like(index_ref)
-    index_ref[SEND_ROW : SEND_ROW + 1] = table_place(send_ref[...])
-    index_ref[RECV_ROW : RECV_ROW + 1] = recv_ref[...]
+    index_ref[SEND_ROW : SEND_ROW + 1] = table_place(ends_ref[0:1])
+    index_ref[RECV_ROW : RECV_ROW + 1] = ends_ref[1:2]
     index_ref[BORDER_ROW : BORDER_ROW + 1, pl.ds(0, border)] = border_ref[...]
     index_ref[FEED_ROW : FEED_ROW + 1, pl.ds(0, grids)] = feed_ref[...]
     index_ref[MASK_ROW : MASK_ROW + 1, pl.ds(0, grids)] = mask_ref[...]
     index_ref[READ_ROW:, pl.ds(0, grids)] = table_place(read_ref[...])
     index_t[...] = index_ref[...].T
     embed_buf = before_buf.at[pl.ds(0, grids)]
-    embed_buf[...] = product(grid_ref[...], enc_ref[...])
+    channels = grid_ref.shape[0]
+    embed_buf[...] = product(grid_ref[...], enc_ref[pl.ds(0, channels)], TN)
     save(3, None, embed_buf).start()
     tick(1)
     feed = hot(iota((nodes, grids), 0) == index_ref[FEED_ROW : FEED_ROW + 1, pl.ds(0, grids)])
@@ -418,9 +430,12 @@
     count_buf[...] = counts
     count_ref[core, chip] = counts
     tick(2)
-    fill_rows(
-        edge_buf.at[0], lambda at, size: silu(product(edge_ref[pl.ds(at, size)], enc_edge_ref[...])), 256
-    )
+    edge_t[...] = edge_rows(edge_ref, edge_t.shape[1]).T
+
+    def embed_edges(at, size):
+        return silu(embedded_edges(edge_t, enc_ref, channels, edge_ref.shape[0], at, size))
+
+    fill_rows(edge_buf.at[0], embed_edges)
     inputs = src_high.shape[0]
     near_inputs = 2 * nodes
 
@@ -537,14 +552,14 @@
             s_copy(g, j, core).wait_send()
 
 
-def forward(bands, rows, grid, edge, indices, blocks, enc, enc_edge, params):
+def forward(bands, rows, grid, edge, indices, blocks, enc, params):
     f32, bf16 = jnp.float32, jnp.bfloat16
     dma = pltpu.SemaphoreType.DMA
     width = blocks.shape[2]
-    edges, grids = edge.shape[0], grid.shape[0]
+    edges, grids = edge.shape[1], grid.shape[1]
     layers = params.shape[0]
-    rim = indices[2].shape[1]
-    index_rows = READ_ROW + indices[5].shape[0]
+    rim = indices[1].shape[1]
+    index_rows = READ_ROW + indices[4].shape[0]
     nodes = NODE_DEV
     chips = bands // 2
     inputs = 2 * nodes + bands * rim
@@ -575,13 +590,14 @@
             array(2, chips, 8, 128),
             jax.ShapeDtypeStruct((index_rows, edges), jnp.int32),
         ),
-        in_specs=[VMEM] * 12,
+        in_specs=[VMEM] * 10,
         out_specs=[ANY] * 5 + [VMEM] * 8,
         scratch_shapes=[
             pltpu.VMEM((2, edges, width), f32),
             pltpu.VMEM((edges, width), f32),
             pltpu.VMEM((edges, width), f32),
             pltpu.VMEM((edges, index_rows), jnp.int32),
+            pltpu.VMEM((edges, 8), f32),
             pltpu.VMEM((edges, inputs), bf16),
             pltpu.VMEM((nodes, edges), bf16),
             pltpu.VMEM((inputs, width), bf16),
@@ -618,7 +634,6 @@
         *indices,
         blocks,
         enc,
-        enc_edge,
         params,
     )
 
@@ -902,7 +917,7 @@
     target_ref,
     edge_ref,
     index_ref,
-    enc_edge_ref,
+    enc_ref,
     dec_ref,
     param_ref,
     full_ref,
@@ -929,6 +944,8 @@
     inner_buf,
     update_buf,
     index_t,
+    edge_t,
+    features,
     edge_grad,
     node_grad,
     part_high,
@@ -957,7 +974,7 @@
     layers = param_ref.shape[0]
     nodes, width = node_buf.shape
     edges = edge_buf.shape[0]
-    grids = grid_ref.shape[0]
+    grids = grid_ref.shape[1]
     border = table.shape[2]
     table_rows = bands * border
     rows_dev = grads_ref.shape[1]
@@ -1068,19 +1085,20 @@
     load(6, layers - 1).start()
     weights.load((layers - 1) * each, (6, 4, 5, 3, 0, 1, 2))
     active = silu(reads[...])
-    mask = index_t[pl.ds(0, grids), MASK_ROW : MASK_ROW + 1].astype(jnp.float32)
-    missed = grid_ref[...] + product(active, dec_ref[...]) - target_ref[...]
+    mask = index_ref[MASK_ROW : MASK_ROW + 1, pl.ds(0, grids)].astype(jnp.float32)
+    missed = grid_ref[...] + product(dec_ref[...], active, NT) - target_ref[...]
     total = jnp.sum(jnp.sum(count_ref[:, :, 0:1, 0:1], axis=0), axis=0)
     masked = mask * missed
     loss = jnp.sum(column(masked * missed), axis=1, keepdims=True)
     grad = (2.0 / total) * masked
-    encs = grid_ref.shape[1]
-    decs = dec_ref.shape[1]
+    channels = grid_ref.shape[0]
+    encs = -(-channels // 8) * 8
+    decs = encs
     decoder_at = encs + 8 + layers * 8
-    small_ref[pl.ds(decoder_at, decs)] = product(grad, active, TN)
+    small_ref[pl.ds(decoder_at, channels)] = product(grad, active)
     tail_rows = small_ref.shape[0] - decoder_at - decs
     small_ref[pl.ds(decoder_at + decs, tail_rows)] = jnp.broadcast_to(loss, (tail_rows, width))
-    read_high, read_low = pieces(product(grad, dec_ref[...], NT) * silu_back(reads[...]))
+    read_high, read_low = pieces(product(grad, dec_ref[...], TN) * silu_back(reads[...]))
     put_table(read_high, read_low, grids)
     to_sibling(0).start()
     node_grad[...] = chosen(pick_t[pl.ds(0, nodes), pl.ds(0, grids)], read_high, read_low)
@@ -1192,16 +1210,20 @@
     fed_grad = normed_back(node_grad[...], norm, scale)
     feed = hot(iota((grids, nodes), 1) == index_t[pl.ds(0, grids), FEED_ROW : FEED_ROW + 1])
     grad = picked(feed, fed_grad) * silu_back(embed_buf[...])
-    small_ref[pl.ds(0, encs)] = product(grid_ref[...], grad, TN)
+    small_ref[pl.ds(0, channels)] = product(grid_ref[...], grad)
     small_ref[pl.ds(encs, 8)] = jnp.zeros((8, width), jnp.float32)
-
-    def embed_tile(t, carry):
-        at = pl.ds(pl.multiple_of(t * tile, tile), tile)
-        grad = edge_grad[at] * silu_back(product(edge_ref[at], enc_edge_ref[...]))
-        small_ref[pl.ds(encs, 8)] += product(edge_ref[at], grad, TN)[:8]
+    features[...] = edge_rows(edge_ref, 8)
+    edge_t[...] = features[...].T
+
+    def embed_back(t, carry):
+        first = pl.multiple_of(t * 128, 128)
+        at = pl.ds(first, 128)
+        embed = embedded_edges(edge_t, enc_ref, channels, edge_ref.shape[0], first, 128)
+        grad = edge_grad[at] * silu_back(embed)
+        small_ref[pl.ds(encs, 8)] += product(features[:, at], grad)
         return carry
 
-    lax.fori_loop(0, edges // tile, embed_tile, 0)
+    lax.fori_loop(0, edges // 128, embed_back, 0)
     for layer in range(layers - 1, 0, -1):
         reducers[layer].relay()
     for layer in range(1, layers):
@@ -1216,11 +1238,11 @@
     full = saved[0]
     width = full.shape[2]
     each = full.shape[0] // layers
-    edges, grids = edge.shape[0], grid.shape[0]
+    edges, grids = edge.shape[1], grid.shape[1]
     nodes = NODE_DEV
     chips = bands // 2
-    decs = decoder.shape[1]
-    small = grid.shape[1] + 8 + layers * 8 + decs + 8
+    padded = -(-grid.shape[0] // 8) * 8
+    small = padded + 8 + layers * 8 + padded + 8
     small = -(-small // (16 * OWNER_CHIPS)) * 16 * OWNER_CHIPS
     tile = edges // 2
     node = pltpu.VMEM((nodes, width), f32)
@@ -1243,6 +1265,8 @@
             node,
             node,
             pltpu.VMEM((edges, index.shape[0]), jnp.int32),
+            pltpu.VMEM((edges, 8), f32),
+            pltpu.VMEM((8, edges), f32),
             pltpu.VMEM((edges, width), f32),
             node,
             pltpu.VMEM((edges, width), bf16),
@@ -1273,34 +1297,33 @@
     )(*inputs, *saved)
 
 
-def newton(mom_ref, out_ref, first, count, gram, poly, temp, later):
-    def add_square(i, total):
-        block = mom_ref[first + i]
-        return total + jnp.sum(jnp.sum(block * block, axis=0, keepdims=True), axis=1, keepdims=True)
-
-    total = lax.fori_loop(0, count, add_square, jnp.zeros((1, 1), jnp.float32))
-    scale = 1.0 / (jnp.sqrt(total) + 1e-07)
+def newton(matrix, result, first, count, arrive, leave, gram, poly, temp, later):
     gram[...] = jnp.zeros_like(gram)
 
     def add_gram(i, carry):
-        block = mom_ref[first + i] * scale
-        mom_ref[first + i] = block
+        arrive(first + i)
+        block = matrix[first + i]
         gram[...] += product(block, block, TN)
         return carry
 
     lax.fori_loop(0, count, add_gram, 0)
+    diagonal = iota(gram.shape, 0) == iota(gram.shape, 1)
+    squares = column(jnp.where(diagonal, gram[...], 0.0))
+    scale = 1.0 / (jnp.sqrt(jnp.sum(squares, axis=1, keepdims=True)) + 1e-07)
+    gram[...] = gram[...] * (scale * scale)
     poly[...] = coef_b * gram[...] + coef_c * product(gram[...], gram[...])
     temp[...] = coef_a * gram[...] + product(gram[...], poly[...])
     gram[...] = coef_a * temp[...] + product(temp[...], poly[...])
     later[...] = coef_b * gram[...] + coef_c * product(gram[...], gram[...])
     temp[...] = coef_a * (poly[...] + later[...]) + product(poly[...], later[...])
 
-    def finish(i, carry):
-        block = mom_ref[first + i]
-        out_ref[first + i] = (coef_a * coef_a) * block + product(block, temp[...])
+    def last(i, carry):
+        block = matrix[first + i] * scale
+        result[first + i] = (coef_a * coef_a) * block + product(block, temp[...])
+        leave(first + i)
         return carry
 
-    lax.fori_loop(0, count, finish, 0)
+    lax.fori_loop(0, count, last, 0)
 
 
 def late_slot(owner, slot):
@@ -1412,8 +1435,6 @@
     split_at = 3 - third
 
     def home(slot):
-        if slot == 0:
-            return row_a
         return row_a + (slot + third) // 3 * (row_b - row_a)
 
     def rows_of(at_row):
@@ -1462,19 +1483,17 @@
             second = (row - row_a) * (row_b - row_a)
             first = second * split_at
             count = (1 - second) * split_at + second
-            for slot in range(SLOTS):
-                @pl.when(jnp.logical_and(slot >= first, slot < first + count))
-                def _():
-                    for step in range(1, rows):
-                        up(slot, (row + step) % rows).wait_recv()
-
-            newton(matrix, result, first, count, gram, poly, temp, later)
-            for slot in range(SLOTS):
-                @pl.when(jnp.logical_and(slot >= first, slot < first + count))
-                def _():
-                    for step in range(1, rows):
-                        down(slot, (row + step) % rows).start()
-                    back[slot] = result[slot, rows_of(row)]
+
+            def arrive(slot):
+                for step in range(1, rows):
+                    up(slot, (row + step) % rows).wait_recv()
+
+            def leave(slot):
+                for step in range(1, rows):
+                    down(slot, (row + step) % rows).start()
+                back[slot] = result[slot, rows_of(row)]
+
+            newton(matrix, result, first, count, arrive, leave, gram, poly, temp, later)
 
     units = [
         (owner, slot)
@@ -1837,40 +1856,30 @@
     layers, blocks, rows_dev, width = processor_weights.shape
     channels = grid_input.shape[1]
     edge_channels = edge_input.shape[1]
-    wide = -(-channels // 128) * 128
+    wide = -(-channels // 8) * 8
     grids, rim = grid_input.shape[0], border_nodes.shape[0]
-
-    def widen(value, size, axis):
-        pads = [(0, 0), (0, 0)]
-        pads[axis] = (0, size - value.shape[axis])
-        return jnp.pad(value, pads)
-
     reads = mesh_to_grid.reshape(grids, -1).T
-    indices = tuple(
-        value[None, :] for value in (senders, receivers, border_nodes, grid_to_mesh, loss_mask)
+    indices = (jnp.stack([senders, receivers]),) + tuple(
+        value[None, :] for value in (border_nodes, grid_to_mesh, loss_mask)
     ) + (reads,)
-    grid_wide = widen(grid_input, wide, 1)
-    edge_wide = widen(edge_input, 128, 1)
-    edge_embed = widen(encoder_weights[channels:], 128, 0)
     flat_weights = processor_weights.reshape(layers * blocks, rows_dev, width)
     *saved, index = forward(
         bands,
         rows,
-        grid_wide,
-        edge_wide,
+        grid_input.T,
+        edge_input.T,
         indices,
         flat_weights,
-        widen(encoder_weights[:channels], wide, 0),
-        edge_embed,
+        encoder_weights,
         norm_params,
     )
     inputs = (
-        grid_wide,
-        widen(grid_target, wide, 1),
-        edge_wide,
+        grid_input.T,
+        grid_target.T,
+        edge_input.T,
         index,
-        edge_embed,
-        widen(decoder_weights, wide, 1),
+        encoder_weights,
+        decoder_weights.T,
         norm_params,
     )
     grads, small, total, _ = backward(bands, rows, rim, rows_dev, inputs, saved)

time: 412 us -> 392 us (0.951)
  local copies, waits for them, and re-layouts: 14.5 us -> 3.25 us
  Pallas kernels: 388 us -> 380 us
    pallas_call x1, Pallas kernels: 108 us -> 102 us  [tail(): pl.pallas_call(functools.partial(tail_kernel, bands, rows), out_shape=(ja...]
    pad x6 -> x0, local copies, waits for them, and re-layouts: 6.34 us -> none  [widen(): return jnp.pad(value, pads)]
where the time goes in v4:
time: 392 us; the launch traced here: 385 us
  Pallas kernels  380 us (97%)
    pallas_call x1, Pallas kernels, forward(): pl.pallas_call(functools.partial(forward_kernel, bands, rows, tuple(chunk...  130 us
    pallas_call x1, Pallas kernels, backward(): pl.pallas_call(functools.partial(backward_kernel, bands, rows, each, tile...  129 us
    pallas_call x1, Pallas kernels, tail(): pl.pallas_call(functools.partial(tail_kernel, bands, rows), out_shape=(ja...  102 us
    pallas_call x1, Pallas kernels, finish(): pl.pallas_call(functools.partial(finish_kernel, shapes, channels, edge_ch...  20.1 us

profile of v4, /device:TPU:0, one launch (start us, length us, event | category | flops | bytes accessed | tf_op | source)
XLA Modules:
  0.0 384.9 jit_solution(6758260092720814859)
XLA Ops:
  0.6 0.7 stack.9
  1.3 0.7 stack.10
  2.0 0.6 pad_add_fusion.ends_ref
  2.7 1.1 reshape.58
  3.7 0.8 copy.36
  4.5 129.7 %forward.1 = (f32[21,512,512]{2,1,0:T(8,128)}, f32[3,1280,512]{2,1,0:T(8,128)}, f32[3,1280,512]{2,1,0:T(8,128)}, f32[3,1280,512]{2,1,0:T(8,128)}, f32[960,512]{1...) custom-call(f32[227,960]{1,0:T(8,128)} %bitcast.28, ...), custom_call_target="tpu_custom_call" | custom-call | tf_op jit(solution)/shard_map/forward/pallas_call | solution.py:576
  134.3 128.5 %backward.1 = (f32[7,128,512]{2,1,0:T(8,128)}, f32[512,512]{1,0:T(8,128)}, f32[21,128,512]{2,1,0:T(8,128)}, f32[2,3,7,16,512]{4,3,2,1,0:T(8,128)}) custom-call(f32[227,960]{1,0:T(8,128)} %bitcast.29, f32[227,960]{1,0:T(8,128)} %bitcast.34, f32[4,1280]{1,0:T(4,128)} %bitcast.38, s32[8,1280]{1,0:T(8,128)} %get-tuple-element.47.index_ref, f32[231,512]{1,0:T(8,128)} %enc_ref.5, ...), custom_call_target="tpu_custom_call" | custom-call | tf_op jit(solution)/shard_map/backward/pallas_call | solution.py:1249
  262.8 101.5 %tail.1 = (f32[21,128,512]{2,1,0:T(8,128)}, f32[21,128,512]{2,1,0:T(8,128)}, f32[8,64,512]{2,1,0:T(8,128)}, f32[1,3,3,128,512]{4,3,2,1,0:T(8,128)}) custom-call(f32[7,128,512]{2,1,0:T(8,128)} %get-tuple-element.60.grads_ref, f32[2,4,64,512]{3,2,1,0:T(8,128)} %bitcast.33, f32[21,128,512]{2,1,0:T(8,128)} %bitcast.25, ...), custom_call_target="tpu_custom_call", output_to_operand_aliasing={{0}: (3, {})} | custom-call | tf_op jit(solution)/shard_map/tail/pallas_call | solution.py:1664
  364.4 20.1 %finish.1 = (f32[1,1]{1,0:T(1,128)}, f32[1,1]{1,0:T(1,128)}, f32[21,128,512]{2,1,0:T(8,128)}, f32[21,128,512]{2,1,0:T(8,128)}, f32[21,128,512]{2,1,0:T(8,128)}, ...) custom-call(f32[21,128,512]{2,1,0:T(8,128)} %bitcast.24, ...), custom_call_target="tpu_custom_call" | custom-call | tf_op jit(solution)/shard_map/finish/pallas_call | solution.py:1794

commit v5 on v4

--- a/solution.py
+++ b/solution.py
@@ -1244,7 +1244,7 @@
     padded = -(-grid.shape[0] // 8) * 8
     small = padded + 8 + layers * 8 + padded + 8
     small = -(-small // (16 * OWNER_CHIPS)) * 16 * OWNER_CHIPS
-    tile = edges // 2
+    tile = edges
     node = pltpu.VMEM((nodes, width), f32)
     return pl.pallas_call(
         functools.partial(backward_kernel, bands, rows, each, tile),
@@ -1782,7 +1782,7 @@
     f32 = jnp.float32
     channels = decoder[0].shape[0]
     big = blocks[0]
-    tiled = pl.BlockSpec((SLOTS,) + big.shape[1:], lambda i: (i, 0, 0))
+    tiled = pl.BlockSpec((len(block_scale),) + big.shape[1:], lambda i: (i, 0, 0))
 
     def whole(value):
         return pl.BlockSpec(value.shape, lambda i: (0,) * value.ndim)
@@ -1793,7 +1793,7 @@
     scalar = jax.ShapeDtypeStruct((1, 1), f32)
     return pl.pallas_call(
         functools.partial(finish_kernel, shapes, channels, edge_channels),
-        grid=(big.shape[0] // SLOTS,),
+        grid=(big.shape[0] // len(block_scale),),
         out_shape=(
             scalar,
             scalar,

time: 392 us -> 389 us (level)
  no operation moved by 1% of the time
where the time goes in v5:
time: 389 us; the launch traced here: 382 us
  Pallas kernels  377 us (97%)
    pallas_call x1, Pallas kernels, forward(): pl.pallas_call(functools.partial(forward_kernel, bands, rows, tuple(chunk...  130 us
    pallas_call x1, Pallas kernels, backward(): pl.pallas_call(functools.partial(backward_kernel, bands, rows, each, tile...  127 us
    pallas_call x1, Pallas kernels, tail(): pl.pallas_call(functools.partial(tail_kernel, bands, rows), out_shape=(ja...  102 us
    pallas_call x1, Pallas kernels, finish(): pl.pallas_call(functools.partial(finish_kernel, shapes, channels, edge_ch...  19.3 us

profile of v5, /device:TPU:0, one launch (start us, length us, event | category | flops | bytes accessed | tf_op | source)
XLA Modules:
  0.0 381.9 jit_solution(10691197922456236635)
XLA Ops:
  0.6 0.7 stack.9
  1.3 0.7 stack.10
  2.0 0.6 pad_add_fusion.ends_ref
  2.7 1.1 reshape.58
  3.7 0.8 copy.36
  4.5 129.8 %forward.1 = (f32[21,512,512]{2,1,0:T(8,128)}, f32[3,1280,512]{2,1,0:T(8,128)}, f32[3,1280,512]{2,1,0:T(8,128)}, f32[3,1280,512]{2,1,0:T(8,128)}, f32[960,512]{1...) custom-call(f32[227,960]{1,0:T(8,128)} %bitcast.28, ...), custom_call_target="tpu_custom_call" | custom-call | tf_op jit(solution)/shard_map/forward/pallas_call | solution.py:576
  134.3 126.5 %backward.1 = (f32[7,128,512]{2,1,0:T(8,128)}, f32[512,512]{1,0:T(8,128)}, f32[21,128,512]{2,1,0:T(8,128)}, f32[2,3,7,16,512]{4,3,2,1,0:T(8,128)}) custom-call(f32[227,960]{1,0:T(8,128)} %bitcast.29, f32[227,960]{1,0:T(8,128)} %bitcast.34, f32[4,1280]{1,0:T(4,128)} %bitcast.38, s32[8,1280]{1,0:T(8,128)} %get-tuple-element.47.index_ref, f32[231,512]{1,0:T(8,128)} %enc_ref.5, ...), custom_call_target="tpu_custom_call" | custom-call | tf_op jit(solution)/shard_map/backward/pallas_call | solution.py:1249
  260.8 101.5 %tail.1 = (f32[21,128,512]{2,1,0:T(8,128)}, f32[21,128,512]{2,1,0:T(8,128)}, f32[8,64,512]{2,1,0:T(8,128)}, f32[1,3,3,128,512]{4,3,2,1,0:T(8,128)}) custom-call(f32[7,128,512]{2,1,0:T(8,128)} %get-tuple-element.60.grads_ref, f32[2,4,64,512]{3,2,1,0:T(8,128)} %bitcast.33, f32[21,128,512]{2,1,0:T(8,128)} %bitcast.25, ...), custom_call_target="tpu_custom_call", output_to_operand_aliasing={{0}: (3, {})} | custom-call | tf_op jit(solution)/shard_map/tail/pallas_call | solution.py:1664
  362.4 19.3 %finish.1 = (f32[1,1]{1,0:T(1,128)}, f32[1,1]{1,0:T(1,128)}, f32[21,128,512]{2,1,0:T(8,128)}, f32[21,128,512]{2,1,0:T(8,128)}, f32[21,128,512]{2,1,0:T(8,128)}, ...) custom-call(f32[21,128,512]{2,1,0:T(8,128)} %bitcast.24, ...), custom_call_target="tpu_custom_call" | custom-call | tf_op jit(solution)/shard_map/finish/pallas_call | solution.py:1794

commit v6 on v5

--- a/solution.py
+++ b/solution.py
@@ -1600,15 +1600,18 @@
             small_across(at, core, True).start()
             small_keep(at).start()
 
+    def pass_on():
+        reducer.relay()
+        for at in range(OWNER_CHIPS):
+            @pl.when(chip != at)
+            def _():
+                small_out(at, 1).wait_recv()
+                small_across(at, core, False).start()
+
+    pl.when(jnp.logical_not(last[0]))(pass_on)
     publish(0)
     solve(1)
-    reducer.relay()
-    for at in range(OWNER_CHIPS):
-        @pl.when(chip != at)
-        def _():
-            small_out(at, 1).wait_recv()
-            small_across(at, core, False).start()
-
+    pl.when(last[0])(pass_on)
     publish(1)
     relay(0)
     relay(1)

time: 389 us -> 391 us (level)
  Pallas kernels: 377 us -> 383 us
    pallas_call x1, Pallas kernels: 102 us -> 107 us  [tail(): pl.pallas_call(functools.partial(tail_kernel, bands, rows), out_shape=(ja...]
where the time goes in v6:
time: 391 us; the launch traced here: 387 us
  Pallas kernels  383 us (98%)
    pallas_call x1, Pallas kernels, forward(): pl.pallas_call(functools.partial(forward_kernel, bands, rows, tuple(chunk...  130 us
    pallas_call x1, Pallas kernels, backward(): pl.pallas_call(functools.partial(backward_kernel, bands, rows, each, tile...  127 us
    pallas_call x1, Pallas kernels, tail(): pl.pallas_call(functools.partial(tail_kernel, bands, rows), out_shape=(ja...  107 us
    pallas_call x1, Pallas kernels, finish(): pl.pallas_call(functools.partial(finish_kernel, shapes, channels, edge_ch...  19.3 us

profile of v6, /device:TPU:0, one launch (start us, length us, event | category | flops | bytes accessed | tf_op | source)
XLA Modules:
  0.0 387.4 jit_solution(17816177799038801009)
XLA Ops:
  0.6 0.7 stack.9
  1.3 0.7 stack.10
  2.0 0.6 pad_add_fusion.ends_ref
  2.7 1.1 reshape.58
  3.7 0.8 copy.36
  4.5 129.8 %forward.1 = (f32[21,512,512]{2,1,0:T(8,128)}, f32[3,1280,512]{2,1,0:T(8,128)}, f32[3,1280,512]{2,1,0:T(8,128)}, f32[3,1280,512]{2,1,0:T(8,128)}, f32[960,512]{1...) custom-call(f32[227,960]{1,0:T(8,128)} %bitcast.28, ...), custom_call_target="tpu_custom_call" | custom-call | tf_op jit(solution)/shard_map/forward/pallas_call | solution.py:576
  134.3 126.5 %backward.1 = (f32[7,128,512]{2,1,0:T(8,128)}, f32[512,512]{1,0:T(8,128)}, f32[21,128,512]{2,1,0:T(8,128)}, f32[2,3,7,16,512]{4,3,2,1,0:T(8,128)}) custom-call(f32[227,960]{1,0:T(8,128)} %bitcast.29, f32[227,960]{1,0:T(8,128)} %bitcast.34, f32[4,1280]{1,0:T(4,128)} %bitcast.38, s32[8,1280]{1,0:T(8,128)} %get-tuple-element.47.index_ref, f32[231,512]{1,0:T(8,128)} %enc_ref.5, ...), custom_call_target="tpu_custom_call" | custom-call | tf_op jit(solution)/shard_map/backward/pallas_call | solution.py:1249
  260.8 107.1 %tail.1 = (f32[21,128,512]{2,1,0:T(8,128)}, f32[21,128,512]{2,1,0:T(8,128)}, f32[8,64,512]{2,1,0:T(8,128)}, f32[1,3,3,128,512]{4,3,2,1,0:T(8,128)}) custom-call(f32[7,128,512]{2,1,0:T(8,128)} %get-tuple-element.60.grads_ref, f32[2,4,64,512]{3,2,1,0:T(8,128)} %bitcast.33, f32[21,128,512]{2,1,0:T(8,128)} %bitcast.25, ...), custom_call_target="tpu_custom_call", output_to_operand_aliasing={{0}: (3, {})} | custom-call | tf_op jit(solution)/shard_map/tail/pallas_call | solution.py:1667
  367.9 19.3 %finish.1 = (f32[1,1]{1,0:T(1,128)}, f32[1,1]{1,0:T(1,128)}, f32[21,128,512]{2,1,0:T(8,128)}, f32[21,128,512]{2,1,0:T(8,128)}, f32[21,128,512]{2,1,0:T(8,128)}, ...) custom-call(f32[21,128,512]{2,1,0:T(8,128)} %bitcast.24, ...), custom_call_target="tpu_custom_call" | custom-call | tf_op jit(solution)/shard_map/finish/pallas_call | solution.py:1797
